TPU v7x, 32 devices: a whole 2x2x4 slice. The times are simulated.
32 devices in a mesh: grp: 4 (over z), dev: 8 (over y, x, core).
Axes of the slice: x: 2, y: 2, z: 4, core: 2. Of those that a mesh axis runs over, the one named last changes fastest.
Arguments:
- head_emb: bfloat16 [32768, 400], P(('grp', 'dev')), may hold values from -2 to 2
- tail_emb: bfloat16 [32768, 400], P(('grp', 'dev')), may hold values from -2 to 2
- relation: int32 [32768], P(('grp', 'dev')), may hold values from 0 to 14823
- owners: int32 [32768, 2], P(('grp', 'dev')), may hold values from 0 to 31, all different within a row; in each aligned block of 1024 rows (0 to 1023, 1024 to 2047, ...) at most 128 rows name the same one
- owner_rows: int32 [32768, 2], P(('grp', 'dev')), may hold values from 0 to 4095
- entities: bfloat16 [131072, 400], P(('grp', 'dev')), may hold values from -2 to 2
- neg_rows: int32 [1, 4096], P(None, ('grp', 'dev')), may hold values from 0 to 4095
- coef: float32 [14824, 100], replicated, may hold values from -4 to 4
- bases: float32 [100, 400], replicated, may hold values from -0.625 to 0.625
Outputs:
- ent_grad: float32 [131072, 400], P(('grp', 'dev'))
- coef_grad: float32 [14824, 100], replicated
- bases_grad: float32 [100, 400], replicated
Inputs may be any that keep to these rules, and one draw needn't show every extreme that they name: The two owners of a row differ; within the triples of one device no owner is named by more than 128 entries of both columns together.
All inputs are finite; a program needn't handle non-finite values.
Results may differ from a plain program's by a relative error of at most 0.0029.
Values may be sent and summed in bfloat16 or wider, within the bound.
No kernel may reach another device: no remote copies, remote signals or barrier semaphores. Data moves between devices by JAX's collectives and lax.ppermute only.
A program may use at most 128 MiB of HBM per device.

v0:
```python
import jax
import jax.numpy as jnp
from jax import lax
from jax.sharding import PartitionSpec as P


def per_device(head_emb, tail_emb, relation, owners, owner_rows, entities, neg_rows, coef, bases):
    highest = lax.Precision.HIGHEST
    triple_count, columns = head_emb.shape
    block_count, neg_local = neg_rows.shape
    group_size = lax.axis_size("dev")
    all_devices = lax.axis_size("grp") * group_size
    neg_count = neg_local * group_size
    ent_local = entities.shape[0]
    picked = coef[relation]
    rel_vec = jnp.dot(picked, bases, precision=highest)
    local_negs = entities[neg_rows]
    group_negs = lax.all_gather(local_negs, "dev", axis=1, tiled=True)
    head_f = head_emb.astype(jnp.float32)
    tail_f = tail_emb.astype(jnp.float32)
    head_rel = (head_f * rel_vec).astype(jnp.bfloat16)
    number = 0
    negatives = group_negs[number]
    scores = lax.dot_general(
        head_rel, negatives, (((1,), (1,)), ((), ())), preferred_element_type=jnp.float32
    )
    neg_prob = jax.nn.sigmoid(scores).astype(jnp.bfloat16)
    probs_list = [neg_prob]
    mix_list = jnp.dot(neg_prob, negatives, preferred_element_type=jnp.float32)
    number = 0
    probs_part = probs_list[number]
    pieces = [
        lax.dot_general(
            probs_part, head_rel, (((0,), (0,)), ((), ())), preferred_element_type=jnp.float32
        )
        / neg_count
    ]
    own_neg = lax.psum_scatter(
        jnp.stack(pieces, axis=1).astype(jnp.bfloat16), "dev", scatter_dimension=0, tiled=True
    ).astype(jnp.float32)
    pos_gate = jax.nn.sigmoid(-jnp.sum(head_f * rel_vec * tail_f, axis=1))[:, None]
    head_grad = (-pos_gate * rel_vec * tail_f + rel_vec * mix_list / neg_count).astype(jnp.bfloat16)
    tail_grad = (-pos_gate * head_f * rel_vec).astype(jnp.bfloat16)
    rel_grad = -pos_gate * head_f * tail_f + head_f * mix_list / neg_count
    ent_grad = jnp.zeros((ent_local, columns), jnp.float32)
    ent_grad = ent_grad.at[neg_rows.T.reshape(-1)].add(own_neg.reshape(-1, columns))
    capacity = 4 * triple_count // all_devices
    grad_rows = jnp.stack([head_grad, tail_grad], axis=1).reshape(2 * triple_count, columns)
    target_dev = owners.reshape(-1)
    entry_rows = owner_rows.reshape(-1)
    onehot = (target_dev[:, None] == jnp.arange(all_devices, dtype=jnp.int32)[None, :]).astype(
        jnp.int32
    )
    slot_index = jnp.sum(jnp.cumsum(onehot, axis=0) * onehot, axis=1) - 1
    position = target_dev * capacity + slot_index
    send_rows = (
        jnp.zeros((all_devices * capacity, columns), jnp.bfloat16).at[position].set(grad_rows)
    )
    send_index = jnp.zeros((all_devices * capacity,), jnp.int32).at[position].set(entry_rows)
    recv_rows, recv_index = (
        lax.all_to_all(send_rows, ("grp", "dev"), split_axis=0, concat_axis=0, tiled=True),
        lax.all_to_all(send_index, ("grp", "dev"), split_axis=0, concat_axis=0, tiled=True),
    )
    ent_grad = ent_grad.at[recv_index].add(recv_rows.astype(jnp.float32))
    coef_rows = jnp.dot(rel_grad, bases.T, precision=highest)
    coef_local = jax.ops.segment_sum(coef_rows, relation, num_segments=coef.shape[0])
    bases_local = jnp.dot(picked.T, rel_grad, precision=highest)
    coef_grad, bases_grad = lax.psum((coef_local, bases_local), ("grp", "dev"))
    return (ent_grad, coef_grad, bases_grad)


def solution(mesh):
    return jax.shard_map(
        per_device,
        mesh=mesh,
        in_specs=(
            P(("grp", "dev"), None),
            P(("grp", "dev"), None),
            P(("grp", "dev")),
            P(("grp", "dev"), None),
            P(("grp", "dev"), None),
            P(("grp", "dev"), None),
            P(None, ("grp", "dev")),
            P(),
            P(),
        ),
        out_specs=(P(("grp", "dev"), None), P(), P()),
        check_vma=False,
    )
```

profile of v0, /device:TPU:0, one launch (start us, length us, event | category | flops | bytes accessed | tf_op | source)
XLA Modules:
  0.0 418.2 jit_solution(15996322358806685574)
XLA Ops:
  8.0 1.0 copy.46
  9.5 0.7 broadcast_multiply_fusion
  10.3 9.1 %reduce-window.6 = s32[32,16,128]{2,1,0:T(8,128)S(1)} reduce-window(s32[32,16,128]{2,1,0:T(8,128)S(1)} %fusion.22, s32[]{:T(128)} %constant.10.clone.1), window={size=1x1x128 pad=0_0x0_0x127_0}, to_apply=%region_2.0 | reduce-window | flops 8323072 | bytes 524292 | tf_op jit(solution)/shard_map/reduce-window
  21.3 8.6 %scatter_custom_fusion.1 = s32[4096]{0:T(1024)} fusion(s32[2048]{0:T(1024)S(1)} %bitcast.59, s32[2048]{0:T(1024)S(1)} %reshape.175, s32[]{:T(128)} %constant.10.clone.1), kind=kCustom, calls=%fused_computation.44 | custom fusion | bytes 16388 | tf_op jit(solution)/shard_map/scatter | solution.py:59
  29.9 7.3 %all-to-all-start = ((s32[32,128,1]{1,2,0:T(1,128)}), s32[32,128,1]{1,2,0:T(1,128)S(1)}, u32[]{:S(2)}, u32[]{:S(2)}) async-start(s32[32,128,1]{1,2,0:T(1,128)} %bitcast.11), calls=%async_computation | async-start | bytes 32768 | tf_op jit(solution)/shard_map/all_to_all | solution.py:62
  37.2 8.3 %copy.42 = f32[14824,100]{1,0:T(8,128)} copy(f32[14824,100]{0,1:T(8,128)} %param.16) | data formatting | bytes 11859200 | tf_op args[7]
  45.6 4.8 %copy.43 = bf16[4096,400]{1,0:T(8,128)(2,1)} copy(bf16[4096,400]{0,1:T(8,128)(2,1)S(1)} %copy-done.6) | data formatting | bytes 6553600 | tf_op args[5]
  50.4 3.6 gather_fusion.1
  54.0 11.4 %all-gather = bf16[1024,400]{1,0:T(8,128)(2,1)S(1)} all-gather(bf16[128,400]{1,0:T(8,128)(2,1)S(1)} %gather_fusion.1), channel_id=2, replica_groups=mesh['grp'=4,'dev'=8] {'dev'}, dimensions={0}, use_global_device_ids=true | all-gather | bytes 921600 | tf_op jit(solution)/shard_map/all_gather | solution.py:18
  65.4 6.4 %gather_fusion = f32[1024,100]{1,0:T(8,128)S(1)} fusion(f32[14824,100]{1,0:T(8,128)} %copy.42, s32[1024]{0:T(1024)S(1)} %fusion.25), kind=kCustom, calls=%fused_computation | custom fusion | bytes 823296 | tf_op jit(solution)/shard_map/gather | solution.py:15
  71.9 1.7 fusion.10
  73.6 2.0 divide_convert_fusion
  75.7 3.1 fusion.32
  79.5 1.3 pad_maximum_fusion
  80.8 6.1 %copy.52 = bf16[1024,2,400]{2,1,0:T(2,128)(2,1)} copy(bf16[1024,2,400]{0,2,1:T(8,128)(2,1)} %pad_maximum_fusion) | data formatting | bytes 3276800 | tf_op jit(solution)/shard_map/stack | solution.py:48
  86.9 4.5 %reshape.183 = bf16[2048,400]{1,0:T(8,128)(2,1)} reshape(bf16[1024,2,400]{2,1,0:T(2,128)(2,1)} %copy.52) | data formatting | bytes 3276800 | tf_op jit(solution)/shard_map/reshape | solution.py:48
  91.4 12.6 %scatter_custom_fusion.2 = bf16[4096,400]{1,0:T(8,128)(2,1)} fusion(s32[2048]{0:T(1024)S(1)} %bitcast.60, bf16[2048,400]{1,0:T(8,128)(2,1)} %reshape.183, bf16[]{:T(256)} %constant.17.clone.1), kind=kCustom, calls=%fused_computation.18 | custom fusion | bytes 3277312 | tf_op jit(solution)/shard_map/scatter | solution.py:57
  104.0 6.0 %copy.53 = bf16[32,128,400]{1,2,0:T(8,128)(2,1)} copy(bf16[32,128,400]{2,1,0:T(8,128)(2,1)} %bitcast.53) | data formatting | bytes 6553600 | tf_op jit(solution)/shard_map/all_to_all | solution.py:61
  110.1 4.8 %all-to-all-start.1 = ((bf16[32,128,400]{1,2,0:T(8,128)(2,1)}), bf16[32,128,400]{1,2,0:T(8,128)(2,1)}, u32[]{:S(2)}, u32[]{:S(2)}) async-start(bf16[32,128,400]{1,2,0:T(8,128)(2,1)} %copy.53), calls=%async_computation.1 | async-start | bytes 6553600 | tf_op jit(solution)/shard_map/all_to_all | solution.py:61
  115.1 4.0 multiply_convert_fusion
  119.2 2.2 copy.64
  121.5 4.4 %fusion.18 = f32[1024,100]{1,0:T(8,128)} fusion(f32[100,400]{0,1:T(8,128)S(1)} %copy-done, f32[1024,400]{0,1:T(8,128)S(1)} %fusion.32, bf16[1024,400]{0,1:T(8,128)(2,1)S(1)} %copy-done.3, bf16[1024,400]{0,1:T(8,128)(2,1)S(1)} %copy-done.2, f32[1024]{0:T(1024)S(1)} %divide_negate_fusion), kind=kOutput, calls=%fused_computation.33 | convolution fusion | flops 494387200 | bytes 3850496 | tf_op jit(solution)/shard_map/dot_general | solution.py:65
  125.9 9.9 %scatter_custom_fusion.4 = f32[14824,100]{1,0:T(8,128)} fusion(s32[1024]{0:T(1024)S(1)} %copy-done.10, f32[1024,100]{1,0:T(8,128)} %fusion.18, f32[]{:T(128)} %constant.9.clone.1), kind=kCustom, calls=%fused_computation.10 | custom fusion | flops 102400 | bytes 5930112 | tf_op jit(solution)/shard_map/scatter-add | solution.py:66
  135.8 3.3 fusion.16
  139.2 30.4 %reduce-scatter.4.cloned.1.call-done = bf16[128,400]{1,0:T(8,128)(2,1)} async-done(((bf16[1024,400]{1,0:T(8,128)(2,1)}), bf16[128,400]{1,0:T(8,128)(2,1)}) %reduce-scatter.4.cloned.1.call-update) | async-done | bytes 102416
  169.6 1.0 copy.65
  170.7 5.2 %scatter_custom_fusion = f32[4096,400]{1,0:T(8,128)} fusion(s32[128]{0:T(128)S(1)} %fusion.26, f32[128,400]{1,0:T(8,128)S(1)} %copy.44, f32[]{:T(128)} %constant.9.clone.1), kind=kCustom, calls=%fused_computation.8 | custom fusion | flops 51200 | bytes 6553604 | tf_op jit(solution)/shard_map/scatter-add | solution.py:46
  175.9 176.4 %all-reduce.3.cloned.1.call-done = (f32[14824,100]{1,0:T(8,128)}, f32[100,400]{0,1:T(8,128)}) async-done(((f32[14824,100]{1,0:T(8,128)}, f32[100,400]{0,1:T(8,128)}), (f32[14824,100]{1,0:T(8,128)}, f32[100,400]{0,1:T(8,128)})) %all-reduce.3.cloned.1.call-update) | async-done | bytes 6089616 | tf_op jit(solution)/shard_map/psum | solution.py:68
  352.2 8.5 %copy.58 = f32[14824,100]{0,1:T(8,128)} copy(f32[14824,100]{1,0:T(8,128)} %get-tuple-element.12) | data formatting | bytes 11859200
  360.7 6.5 %copy.61 = f32[32,128,400]{2,1,0:T(8,128)} copy(bf16[32,128,400]{1,2,0:T(8,128)(2,1)} %all-to-all-done.1) | data formatting | bytes 9830400 | tf_op jit(solution)/shard_map/convert_element_type | solution.py:64
  367.2 34.2 %scatter_fusion = f32[4096,400]{1,0:T(8,128)} fusion(f32[4096,400]{1,0:T(8,128)} %scatter_custom_fusion, s32[4096]{0:T(1024)S(1)} %bitcast.55, f32[4096,400]{1,0:T(8,128)} %bitcast.52), kind=kCustom, calls=%fused_computation.5 | custom fusion | flops 1638400 | bytes 19677184 | tf_op jit(solution)/shard_map/scatter-add | solution.py:64
  401.5 8.6 %copy.57 = f32[4096,400]{0,1:T(8,128)} copy(f32[4096,400]{1,0:T(8,128)} %scatter_fusion) | data formatting | bytes 13107200
  (55 shorter events, 4.4 us)
Async XLA Ops:
  8.0 63.8 %copy-start = (f32[100,400]{0,1:T(8,128)S(1)}, f32[100,400]{0,1:T(8,128)}, u32[]{:S(2)}) copy-start(f32[100,400]{0,1:T(8,128)} %param.17) | copy-start | bytes 480004
  10.2 10.5 %copy-start.9 = (s32[1024,2]{0,1:T(2,128)S(1)}, s32[1024,2]{0,1:T(2,128)}, u32[]{:S(2)}) copy-start(s32[1024,2]{0,1:T(2,128)} %param.13) | copy-start | bytes 24580
  29.9 80.2 %all-to-all-start = ((s32[32,128,1]{1,2,0:T(1,128)}), s32[32,128,1]{1,2,0:T(1,128)S(1)}, u32[]{:S(2)}, u32[]{:S(2)}) async-start(s32[32,128,1]{1,2,0:T(1,128)} %bitcast.11), calls=%async_computation | async-start | bytes 32768 | tf_op jit(solution)/shard_map/all_to_all | solution.py:62
  37.2 8.4 %copy-start.10 = (s32[1024]{0:T(1024)S(1)}, s32[1024]{0:T(1024)}, u32[]{:S(2)}) copy-start(s32[1024]{0:T(1024)} %param.11) | copy-start | bytes 12292
  37.2 8.4 %copy-start.6 = (bf16[4096,400]{0,1:T(8,128)(2,1)S(1)}, bf16[4096,400]{0,1:T(8,128)(2,1)}, u32[]{:S(2)}) copy-start(bf16[4096,400]{0,1:T(8,128)(2,1)} %param.14) | copy-start | bytes 9830404
  45.6 4.8 %copy-start.11 = (s32[1,128]{1,0:T(1,128)S(1)}, s32[1,128]{1,0:T(1,128)}, u32[]{:S(2)}) copy-start(s32[1,128]{1,0:T(1,128)} %param.15) | copy-start | bytes 1540
  65.4 8.2 %copy-start.7 = (bf16[1024,400]{1,0:T(8,128)(2,1)}, bf16[1024,400]{1,0:T(8,128)(2,1)S(1)}, u32[]{:S(2)}) copy-start(bf16[1024,400]{1,0:T(8,128)(2,1)S(1)} %all-gather) | copy-start | bytes 2457604
  65.4 6.4 %copy-start.2 = (bf16[1024,400]{0,1:T(8,128)(2,1)S(1)}, bf16[1024,400]{0,1:T(8,128)(2,1)}, u32[]{:S(2)}) copy-start(bf16[1024,400]{0,1:T(8,128)(2,1)} %param.10) | copy-start | bytes 2457604
  65.4 6.4 %copy-start.3 = (bf16[1024,400]{0,1:T(8,128)(2,1)S(1)}, bf16[1024,400]{0,1:T(8,128)(2,1)}, u32[]{:S(2)}) copy-start(bf16[1024,400]{0,1:T(8,128)(2,1)} %param.9) | copy-start | bytes 2457604
  71.9 1.7 copy-start.5
  73.6 5.2 %copy-start.4 = (f32[1024,400]{0,1:T(8,128)}, f32[1024,400]{0,1:T(8,128)S(1)}, u32[]{:S(2)}) copy-start(f32[1024,400]{0,1:T(8,128)S(1)} %get-tuple-element.17) | copy-start | bytes 4915204
  75.7 3.1 copy-start.12
  110.1 250.6 %all-to-all-start.1 = ((bf16[32,128,400]{1,2,0:T(8,128)(2,1)}), bf16[32,128,400]{1,2,0:T(8,128)(2,1)}, u32[]{:S(2)}, u32[]{:S(2)}) async-start(bf16[32,128,400]{1,2,0:T(8,128)(2,1)} %copy.53), calls=%async_computation.1 | async-start | bytes 6553600 | tf_op jit(solution)/shard_map/all_to_all | solution.py:61
  114.9 54.7 %reduce-scatter.4.cloned.1.call-start = ((), (), s32[]{:S(2)}) async-start(), calls=%async_computation.3 | async-start | bytes 1179648
  121.4 230.8 %all-reduce.3.cloned.1.call-start = ((), (), s32[]{:S(2)}) async-start(), calls=%async_computation.4 | async-start | bytes 15589376 | tf_op jit(solution)/shard_map/psum | solution.py:68
  401.5 8.6 %copy-start.8 = (f32[100,400]{0,1:T(8,128)S(1)}, f32[100,400]{0,1:T(8,128)}, u32[]{:S(2)}) copy-start(f32[100,400]{0,1:T(8,128)} %get-tuple-element.20) | copy-start | bytes 480004
  401.5 9.3 %copy-start.1 = (f32[100,400]{0,1:T(8,128)S(1)}, f32[100,400]{0,1:T(8,128)}, u32[]{:S(2)}) copy-start(f32[100,400]{0,1:T(8,128)} %param.17) | copy-start | bytes 480004
Sparse Core Ops, SparseCore 0:
  121.5 47.9 reduce-scatter.3
Sparse Core Ops, SparseCore 1:
  139.2 213.0 all-reduce.2
where the time goes:
time: 420 us; the launch traced here: 418 us
  waiting for transfers between devices  207 us (49%)
  local copies, waits for them, and re-layouts  91.7 us (22%)
  other arithmetic  61.6 us (15%)
  matrix products  18.6 us (4%)
  between operations  15.8 us (4%)
  starting transfers between devices  12.4 us (3%)
  blocking collectives  11.4 us (3%)
    psum x1, waiting for transfers between devices, per_device(): coef_grad, bases_grad = lax.psum((coef_local, bases_local), ('grp', 'dev'))  176 us
    unnamed x35, local copies, waits for them, and re-layouts  35.4 us
    scatter-add x1, other arithmetic, per_device(): ent_grad = ent_grad.at[recv_index].add(recv_rows.astype(jnp.float32))  34.2 us
    unnamed x3, waiting for transfers between devices  30.4 us
    scatter x1, local copies, waits for them, and re-layouts, per_device(): jnp.zeros((all_devices * capacity, columns), jnp.bfloat16).at[position]  12.6 us
    all_gather x1, blocking collectives, per_device(): group_negs = lax.all_gather(local_negs, 'dev', axis=1, tiled=True)  11.4 us
    scatter-add x1, other arithmetic, per_device(): jax.ops.segment_sum(coef_rows, relation, num_segments=coef.shape[0])  9.9 us
    another operation x3, other arithmetic  9.41 us
  transfers between devices with their start and end apart: 4, of which 2 were waited for; matrix products, arithmetic and copies ran while one was open for 24% of the time, Pallas kernels for 0%

commit v1 on v0

v1 whole, which is shorter than its diff:
```python
import functools

import jax
import jax.numpy as jnp
from jax import lax
from jax.experimental import pallas as pl
from jax.experimental.pallas import tpu as pltpu
from jax.sharding import PartitionSpec as P

F32, BF16, I32 = jnp.float32, jnp.bfloat16, jnp.int32
HIGHEST = lax.Precision.HIGHEST
LANES = 128
PAD = 112
VMEM_BYTES = 56 * 1024 * 1024


def nt(a, b, **kw):
    return lax.dot_general(a, b, (((1,), (1,)), ((), ())), preferred_element_type=F32, **kw)


def tn(a, b, **kw):
    return lax.dot_general(a, b, (((0,), (0,)), ((), ())), preferred_element_type=F32, **kw)


def nn(a, b, **kw):
    return lax.dot_general(a, b, (((1,), (0,)), ((), ())), preferred_element_type=F32, **kw)


def params():
    return pltpu.CompilerParams(vmem_limit_bytes=VMEM_BYTES)


def cost(flops, nbytes):
    return pl.CostEstimate(flops=flops, bytes_accessed=nbytes, transcendentals=0)


def hits(ids, rows, first):
    row = lax.broadcasted_iota(I32, (rows, ids.shape[1]), 0)
    return jnp.where(row == ids - first, 1.0, 0.0).astype(BF16)


def pick_negs_kernel(ids_ref, ent_ref, out_ref, acc_ref):
    step = pl.program_id(0)
    width = ent_ref.shape[1]
    part = nn(ent_ref[...], hits(ids_ref[...], width, step * width))

    @pl.when(step == 0)
    def _():
        acc_ref[...] = part

    @pl.when(step > 0)
    def _():
        acc_ref[...] += part

    @pl.when(step == pl.num_programs(0) - 1)
    def _():
        rows = acc_ref[...].astype(BF16)
        for k in range(out_ref.shape[0]):
            out_ref[k] = rows


def pick_negs(ids, ent_t, group):
    cols, ent = ent_t.shape
    width = 1024
    return pl.pallas_call(
        pick_negs_kernel,
        grid=(ent // width,),
        in_specs=[
            pl.BlockSpec((1, ids.shape[1]), lambda i: (0, 0)),
            pl.BlockSpec((cols, width), lambda i: (0, i)),
        ],
        out_specs=pl.BlockSpec((group, cols, ids.shape[1]), lambda i: (0, 0, 0)),
        out_shape=jax.ShapeDtypeStruct((group, cols, ids.shape[1]), BF16),
        scratch_shapes=[pltpu.VMEM((cols, ids.shape[1]), F32)],
        compiler_params=params(),
        cost_estimate=cost(2 * cols * ent * 128, cols * ent * 2),
        name="pick_negs",
    )(ids, ent_t)


def relation_kernel(nrel, devices, cap, rel_ref, coef_ref, bases_ref, head_ref, tail_ref,
                    owner_ref, picked_ref, vec_ref, gate_ref, tgrad_ref, pos_ref, halves, acc):
    step = pl.program_id(0)
    width = coef_ref.shape[1]
    nb = coef_ref.shape[0]
    lane = lax.broadcasted_iota(I32, (nb, width), 1) + step * width
    block = jnp.where(lane < nrel, coef_ref[...], 0.0)
    high = block.astype(BF16)

    @pl.when(step == 0)
    def _():
        acc[...] = jnp.zeros_like(acc)

    low = block - high.astype(F32)
    spare = jnp.zeros((PAD - nb, width), F32)
    halves[0:PAD] = jnp.concatenate([block, spare], axis=0).astype(BF16)
    halves[PAD:] = jnp.concatenate([low, spare], axis=0).astype(BF16)
    acc[...] += nn(halves[...], hits(rel_ref[...], width, step * width))

    @pl.when(step == pl.num_programs(0) - 1)
    def _():
        picked = acc[0:nb] + acc[PAD:PAD + nb]
        picked_ref[...] = picked
        vec = nn(bases_ref[...], picked, precision=HIGHEST)
        vec_ref[...] = vec
        head = head_ref[...].astype(F32)
        head_vec = head * vec
        score = jnp.sum(head_vec * tail_ref[...].astype(F32), axis=0, keepdims=True)
        gate = jax.nn.sigmoid(-score)
        gate_ref[...] = gate
        tgrad_ref[...] = (-gate * head * vec).astype(BF16)
        owner = owner_ref[...]
        triples = owner.shape[1]
        rows = lax.broadcasted_iota(I32, (LANES, LANES), 0)
        cols = lax.broadcasted_iota(I32, (LANES, LANES), 1)
        upto = jnp.where(rows <= cols, 1.0, 0.0).astype(BF16)
        number = lax.broadcasted_iota(I32, (devices, LANES), 0)
        owners, marks = [], []
        for side in range(2):
            for b in range(triples // LANES):
                o = owner[side:side + 1, b * LANES:(b + 1) * LANES]
                owners.append(o)
                marks.append(jnp.where(number == o, 1.0, 0.0))
        sums = nn(jnp.concatenate(marks, axis=0).astype(BF16), upto)
        carry = jnp.zeros((devices, 1), F32)
        for b, (o, mark) in enumerate(zip(owners, marks)):
            part = sums[b * devices:(b + 1) * devices]
            slot = jnp.sum(mark * (part + carry), axis=0, keepdims=True) - 1.0
            pos_ref[:, b * LANES:(b + 1) * LANES] = o * cap + slot.astype(I32)
            carry = carry + part[:, LANES - 1:LANES]


def relation_step(rel, coef_t, bases_t, head_t, tail_t, owner_t, devices, cap):
    nb, nrel = coef_t.shape
    cols, triples = head_t.shape
    width = 1920
    steps = pl.cdiv(nrel, width)
    whole = lambda shape: pl.BlockSpec(shape, lambda i: (0,) * len(shape))
    outs = [((nb, triples), F32), ((cols, triples), F32), ((1, triples), F32),
            ((cols, triples), BF16), ((1, 2 * triples), I32)]
    return pl.pallas_call(
        functools.partial(relation_kernel, nrel, devices, cap),
        grid=(steps,),
        in_specs=[
            whole((1, triples)),
            pl.BlockSpec((nb, width), lambda i: (0, i)),
            whole((cols, nb)), whole((cols, triples)), whole((cols, triples)),
            whole((2, triples)),
        ],
        out_specs=[whole(s) for s, _ in outs],
        out_shape=[jax.ShapeDtypeStruct(s, d) for s, d in outs],
        scratch_shapes=[pltpu.VMEM((2 * PAD, width), BF16), pltpu.VMEM((2 * PAD, triples), F32)],
        compiler_params=params(),
        cost_estimate=cost(2 * 2 * PAD * nrel * triples, nb * nrel * 4),
        name="relation_step",
    )(rel, coef_t, bases_t, head_t, tail_t, owner_t)


def score_kernel(neg_count, negs_ref, vec_ref, head_ref, tail_ref, gate_ref, tgrad_ref, pos_ref,
                 row_ref, send_ref, probs_ref, hrel_ref, mix_ref, grads):
    group, cols, per = negs_ref.shape
    triples = head_ref.shape[1]
    vec = vec_ref[...]
    head_rel = (head_ref[...].astype(F32) * vec).astype(BF16)
    hrel_ref[...] = head_rel
    mix = jnp.zeros((cols, triples), F32)
    for first in range(0, group, 8):
        negs = jnp.concatenate([negs_ref[first + k] for k in range(8)], axis=1)
        probs = jax.nn.sigmoid(tn(negs, head_rel)).astype(BF16)
        probs_ref[first * per:(first + 8) * per] = probs
        mix = mix + nn(negs, probs)
    mix_ref[...] = mix
    tail = tail_ref[...].astype(F32)
    grads[0:cols, 0:triples] = (-gate_ref[...] * vec * tail + vec * mix / neg_count).astype(BF16)
    grads[0:cols, triples:] = tgrad_ref[...]
    for side in range(2):
        ids = row_ref[side:side + 1]
        lanes = slice(side * triples, (side + 1) * triples)
        high = ids // 64
        pair = jnp.concatenate([high, ids - high * 64], axis=0).astype(F32)
        spare = jnp.zeros((grads.shape[0] - cols - 2, triples), F32)
        grads[cols:, lanes] = jnp.concatenate([pair, spare], axis=0).astype(BF16)
    slots = 2 * LANES
    rows = send_ref.shape[1]

    @pl.loop(0, send_ref.shape[0] // 2)
    def _(b):
        part = nt(grads[...], hits(pos_ref[...], slots, b * slots)).astype(BF16)
        send_ref[2 * b] = part[0:rows, 0:LANES]
        send_ref[2 * b + 1] = part[0:rows, LANES:]


def score_step(negs, vec, head_t, tail_t, gate, tgrad, pos, rows, blocks, neg_count):
    group, cols, per = negs.shape
    triples = head_t.shape[1]
    outs = [((blocks, cols + 2, LANES), BF16), ((group * per, triples), BF16),
            ((cols, triples), BF16), ((cols, triples), F32)]
    return pl.pallas_call(
        functools.partial(score_kernel, neg_count),
        out_shape=[jax.ShapeDtypeStruct(s, d) for s, d in outs],
        scratch_shapes=[pltpu.VMEM((cols + 16, 2 * triples), BF16)],
        compiler_params=params(),
        cost_estimate=cost(2 * cols * triples * (2 * group * per + 2 * blocks * LANES), 16 << 20),
        name="score_step",
    )(negs, vec, head_t, tail_t, gate, tgrad, pos, rows)


def partial_kernel(neg_count, share, probs_ref, hrel_ref, mix_ref, head_ref, tail_ref, gate_ref,
                   picked_ref, bases_ref, rel_ref, rows_ref, parts_ref):
    group = parts_ref.shape[0]
    cols, triples = head_ref.shape
    nb = picked_ref.shape[0]
    head = head_ref[...].astype(F32)
    rel_grad = -gate_ref[...] * head * tail_ref[...].astype(F32) + head * mix_ref[...] / neg_count
    coef_rows = nn(bases_ref[...].T, rel_grad, precision=HIGHEST)
    ids = rel_ref[...]
    high = ids // 128
    pair = jnp.concatenate([high, ids - high * 128], axis=0).astype(F32)
    rows_ref[...] = jnp.concatenate([coef_rows, pair], axis=0).astype(BF16)
    base_grad = nt(picked_ref[...], rel_grad, precision=HIGHEST)
    low = base_grad - base_grad.astype(BF16).astype(F32)
    per = LANES
    for first in range(0, group, 8):
        part = nt(hrel_ref[...], probs_ref[first * per:(first + 8) * per]) / neg_count
        for k in range(8):
            parts_ref[first + k, 0:cols] = part[:, k * per:(k + 1) * per].astype(BF16)
    for k in range(group):
        first = min(k * share, cols)
        last = min(first + share, cols)
        gap = jnp.zeros((nb, 64 - max(last - first, 0)), F32)
        pieces = [base_grad[:, first:last], gap, low[:, first:last], gap]
        pieces = [p for p in pieces if p.shape[1] > 0]
        parts_ref[k, cols:] = jnp.concatenate(pieces, axis=1).astype(BF16)


def partial_step(probs, hrel, mix, head_t, tail_t, gate, picked, bases_t, rel, group, share,
                 neg_count):
    cols, triples = head_t.shape
    nb = picked.shape[0]
    outs = [((nb + 2, triples), BF16), ((group, cols + nb, LANES), BF16)]
    return pl.pallas_call(
        functools.partial(partial_kernel, neg_count, share),
        out_shape=[jax.ShapeDtypeStruct(s, d) for s, d in outs],
        compiler_params=params(),
        cost_estimate=cost(1, 1),
        name="partial_step",
    )(probs, hrel, mix, head_t, tail_t, gate, picked, bases_t, rel)


def gather_coef_kernel(span, share, me_ref, *refs):
    row_refs, parts_ref, out_ref = refs[:-2], refs[-2], refs[-1]
    step = pl.program_id(0)
    nb, width = out_ref.shape[1], out_ref.shape[2]
    first = step * width
    total = jnp.zeros((nb, width), F32)
    for ref in row_refs:
        for s in range(ref.shape[0]):
            ids = (ref[s, nb:nb + 1].astype(F32) * 128.0 + ref[s, nb + 1:nb + 2].astype(F32))
            ids = ids.astype(I32) - me_ref[0] * span
            ids = jnp.where((ids >= 0) & (ids < span), ids, -1)
            total = total + nt(ref[s, 0:nb], hits(ids, width, first))
    out_ref[0] = total

    @pl.when(step == span // width)
    def _():
        both = jnp.sum(parts_ref[:, parts_ref.shape[1] - nb:].astype(F32), axis=0)
        at = span % width
        out_ref[0, :, at:at + share] = both[:, 0:share] + both[:, 64:64 + share]


def gather_coef(me, row_sets, parts, span, share, width, quarters):
    nb = row_sets[0].shape[1] - 2
    whole = lambda shape: pl.BlockSpec(shape, lambda i, me: (0,) * len(shape))
    return pl.pallas_call(
        functools.partial(gather_coef_kernel, span, share),
        grid_spec=pltpu.PrefetchScalarGridSpec(
            num_scalar_prefetch=1,
            grid=(quarters,),
            in_specs=[whole(r.shape) for r in row_sets] + [whole(parts.shape)],
            out_specs=pl.BlockSpec((1, nb, width), lambda i, me: (i, 0, 0)),
        ),
        out_shape=jax.ShapeDtypeStruct((quarters, nb, width), F32),
        compiler_params=params(),
        cost_estimate=cost(1, 1),
        name="gather_coef",
    )(me, *row_sets, parts)


def spread_kernel(span, share, where_ref, which_ref, a_ref, b_ref, coef_ref, base_ref, pieces):
    step = pl.program_id(0)
    steps = pl.num_programs(0)
    quarters, width = a_ref.shape[1], a_ref.shape[3]
    cols = base_ref.shape[1]

    def put(ref):
        for q in range(quarters):
            first = q * width
            if first < span:
                last = min(first + width, span)
                coef_ref[:, first:last] = ref[0, q, :, 0:last - first].astype(F32)
        at = span % width
        piece = ref[0, span // width, :, at:at + LANES].astype(F32)
        spare = jnp.zeros((pieces.shape[1] - piece.shape[0], LANES), F32)
        pieces[step] = jnp.concatenate([piece, spare], axis=0)

    @pl.when(which_ref[step] == 0)
    def _():
        put(a_ref)

    @pl.when(which_ref[step] != 0)
    def _():
        put(b_ref)

    @pl.when(step == steps - 1)
    def _():
        count = pieces.shape[0]
        row = jnp.concatenate([pieces[k][:, 0:share] for k in range(count)], axis=1)
        base_ref[...] = row[0:base_ref.shape[0], 0:cols]


def spread(where, which, a, b, span, share, nrel, cols):
    group = where.shape[0]
    _, quarters, nb, width = a.shape
    pick = lambda i, where, which: (where[i], 0, 0, 0)
    return pl.pallas_call(
        functools.partial(spread_kernel, span, share),
        grid_spec=pltpu.PrefetchScalarGridSpec(
            num_scalar_prefetch=2,
            grid=(group,),
            in_specs=[pl.BlockSpec((1, quarters, nb, width), pick)] * 2,
            out_specs=[
                pl.BlockSpec((nb, span), lambda i, where, which: (0, i)),
                pl.BlockSpec((nb, cols), lambda i, where, which: (0, 0)),
            ],
            scratch_shapes=[pltpu.VMEM((group, PAD, LANES), F32)],
        ),
        out_shape=[jax.ShapeDtypeStruct((nb, nrel), F32), jax.ShapeDtypeStruct((nb, cols), F32)],
        compiler_params=params(),
        cost_estimate=cost(1, 1),
        name="spread",
    )(where, which, a, b)


def add_rows_kernel(recv_ref, parts_ref, neg_ref, out_ref, grads, ids, negs):
    step = pl.program_id(0)
    cols, width = out_ref.shape
    sources = recv_ref.shape[0]

    @pl.when(step == 0)
    def _():
        for s in range(sources):
            lanes = slice(s * LANES, (s + 1) * LANES)
            grads[:, lanes] = recv_ref[s, 0:cols]
            pair = recv_ref[s, cols:cols + 2].astype(F32)
            ids[:, lanes] = (pair[0:1] * 64.0 + pair[1:2]).astype(I32)
        total = parts_ref[0, 0:cols].astype(F32)
        for k in range(1, parts_ref.shape[0]):
            total = total + parts_ref[k, 0:cols].astype(F32)
        top = total.astype(BF16)
        negs[:, 0:LANES] = top
        negs[:, LANES:] = (total - top.astype(F32)).astype(BF16)

    first = step * width
    mine = hits(neg_ref[...], width, first)
    out_ref[...] = nt(grads[...], hits(ids[...], width, first)) + nt(
        negs[...], jnp.concatenate([mine, mine], axis=1))


def add_rows(recv, parts, neg_ids, cols, ent):
    sources = recv.shape[0]
    width = 512
    whole = lambda shape: pl.BlockSpec(shape, lambda i: (0,) * len(shape))
    return pl.pallas_call(
        add_rows_kernel,
        grid=(ent // width,),
        in_specs=[whole(recv.shape), whole(parts.shape), whole(neg_ids.shape)],
        out_specs=pl.BlockSpec((cols, width), lambda i: (0, i)),
        out_shape=jax.ShapeDtypeStruct((cols, ent), F32),
        scratch_shapes=[pltpu.VMEM((cols, sources * LANES), BF16),
                        pltpu.VMEM((1, sources * LANES), I32),
                        pltpu.VMEM((cols, 2 * LANES), BF16)],
        compiler_params=params(),
        cost_estimate=cost(1, 1),
        name="add_rows",
    )(recv, parts, neg_ids)


def from_group(block, group):
    numbers = jnp.arange(group, dtype=I32)
    if group != 8:
        everything = lax.all_gather(block, "dev", axis=0)
        return everything, everything, numbers, jnp.zeros_like(numbers)
    own = [block] + [
        lax.ppermute(block, "dev", [(i, i ^ far) for i in range(group)]) for far in (2, 4, 6)
    ]
    own = jnp.stack(own)
    sibling = lax.ppermute(own, "dev", [(i, i ^ 1) for i in range(group)])
    offset = numbers ^ lax.axis_index("dev").astype(I32)
    return own, sibling, offset // 2, offset % 2


def per_device(head_emb, tail_emb, relation, owners, owner_rows, entities, neg_rows, coef, bases):
    triples, cols = head_emb.shape
    group = lax.axis_size("dev")
    layers = lax.axis_size("grp")
    devices = layers * group
    neg_count = neg_rows.shape[1] * group
    ent_local = entities.shape[0]
    nrel, nb = coef.shape
    cap = 4 * triples // devices
    blocks = devices * cap // LANES
    share = pl.cdiv(cols, group)
    span = pl.cdiv(pl.cdiv(nrel, group), LANES) * LANES
    quarter = pl.cdiv(span + LANES, layers * LANES) * LANES

    head_t, tail_t, owner_t, row_t = head_emb.T, tail_emb.T, owners.T, owner_rows.T
    coef_t, bases_t = coef.T, bases.T
    rel = relation.reshape(1, triples)

    sent_negs = pick_negs(neg_rows, entities.T, group)
    negs = lax.all_to_all(sent_negs, "dev", 0, 0, tiled=True)
    picked, vec, gate, tgrad, pos = relation_step(
        rel, coef_t, bases_t, head_t, tail_t, owner_t, devices, cap)
    send, probs, hrel, mix = score_step(
        negs, vec, head_t, tail_t, gate, tgrad, pos, row_t, blocks, neg_count)
    per_block = LANES // cap
    if per_block > 1:
        send = send.reshape(blocks, cols + 2, per_block, cap).transpose(0, 2, 1, 3)
        send = send.reshape(devices, cols + 2, cap)
    recv = lax.all_to_all(send, ("grp", "dev"), 0, 0, tiled=True)
    if per_block > 1:
        recv = recv.reshape(blocks, per_block, cols + 2, cap).transpose(0, 2, 1, 3)
        recv = recv.reshape(blocks, cols + 2, LANES)

    rows, parts = partial_step(
        probs, hrel, mix, head_t, tail_t, gate, picked, bases_t, rel, group, share, neg_count)
    own_rows, sibling_rows, _, _ = from_group(rows, group)
    parts = lax.all_to_all(parts, "dev", 0, 0, tiled=True)
    me = lax.axis_index("dev").astype(I32).reshape(1)
    row_sets = [own_rows, sibling_rows] if group == 8 else [own_rows]
    columns = gather_coef(me, row_sets, parts, span, share, quarter, layers)
    columns = lax.all_to_all(columns, "grp", 0, 0, tiled=True)
    columns = jnp.sum(columns, axis=0).astype(BF16)
    columns = lax.all_gather(columns, "grp", axis=0)
    a, b, where, which = from_group(columns, group)
    coef_grad, bases_grad = spread(where, which, a, b, span, share, nrel, cols)

    ent_grad = add_rows(recv, parts, neg_rows, cols, ent_local)
    return ent_grad.T, coef_grad.T, bases_grad


def solution(mesh):
    return jax.shard_map(
        per_device,
        mesh=mesh,
        in_specs=(
            P(("grp", "dev"), None),
            P(("grp", "dev"), None),
            P(("grp", "dev")),
            P(("grp", "dev"), None),
            P(("grp", "dev"), None),
            P(("grp", "dev"), None),
            P(None, ("grp", "dev")),
            P(),
            P(),
        ),
        out_specs=(P(("grp", "dev"), None), P(), P()),
        check_vma=False,
    )
```

time: 420 us -> 267 us (0.64)
  waiting for transfers between devices: 207 us -> 34.5 us
  blocking collectives: 11.4 us -> 109 us
  Pallas kernels: 0 us -> 88.6 us
  local copies, waits for them, and re-layouts: 91.7 us -> 10.4 us
  other arithmetic: 61.6 us -> 2.18 us
  matrix products: 18.6 us -> 0 us
  between operations: 15.8 us -> 0.71 us
  starting transfers between devices: 12.4 us -> 20.6 us
    psum x1 -> x0, waiting for transfers between devices: 176 us -> none  [per_device(): coef_grad, bases_grad = lax.psum((coef_local, bases_local), ('grp', 'dev'))]
    pallas_call x0 -> x7, Pallas kernels: none -> 88.6 us  [the longest x1 20.3 us: add_rows(): pl.pallas_call(add_rows_kernel, grid=(ent // width,), in_specs=[whole(rec...]
    all_gather x1, blocking collectives: 11.4 us -> 84 us  [per_device(): columns = lax.all_gather(columns, 'grp', axis=0)]
    scatter-add x3 -> x0, other arithmetic: 49.3 us -> none  [the longest x1 34.2 us: per_device(): ent_grad = ent_grad.at[recv_index].add(recv_rows.astype(jnp.float32))]
    unnamed x3 -> x0, waiting for transfers between devices: 30.4 us -> none
    unnamed x35 -> x13, local copies, waits for them, and re-layouts: 35.4 us -> 5.37 us
    ppermute x0 -> x8, waiting for transfers between devices: none -> 29.8 us  [the longest x6 24.4 us: from_group(): lax.ppermute(block, 'dev', [(i, i ^ far) for i in range(group)])]
    all_to_all x0 -> x1, blocking collectives: none -> 25.3 us  [per_device(): columns = lax.all_to_all(columns, 'grp', 0, 0, tiled=True)]
  transfers between devices with their start and end apart: 4 -> 11, of which waited for: 2 -> 9; matrix products, arithmetic and copies ran while one was open for 24% -> 3% of each run, Pallas kernels for 0% -> 9%
where the time goes in v1:
time: 267 us; the launch traced here: 266 us
  blocking collectives  109 us (41%)
  Pallas kernels  88.6 us (33%)
  waiting for transfers between devices  34.5 us (13%)
  starting transfers between devices  20.6 us (8%)
  local copies, waits for them, and re-layouts  10.4 us (4%)
    all_gather x1, blocking collectives, per_device(): columns = lax.all_gather(columns, 'grp', axis=0)  84 us
    all_to_all x1, blocking collectives, per_device(): columns = lax.all_to_all(columns, 'grp', 0, 0, tiled=True)  25.3 us
    ppermute x6, waiting for transfers between devices, from_group(): lax.ppermute(block, 'dev', [(i, i ^ far) for i in range(group)])  24.4 us
    pallas_call x1, Pallas kernels, add_rows(): pl.pallas_call(add_rows_kernel, grid=(ent // width,), in_specs=[whole(rec...  20.3 us
    pallas_call x1, Pallas kernels, score_step(): pl.pallas_call(functools.partial(score_kernel, neg_count), out_shape=[jax...  17.5 us
    pallas_call x1, Pallas kernels, relation_step(): pl.pallas_call(functools.partial(relation_kernel, nrel, devices, cap), gr...  16.8 us
    pallas_call x1, Pallas kernels, gather_coef(): pl.pallas_call(functools.partial(gather_coef_kernel, span, share), grid_s...  13.5 us
    pallas_call x1, Pallas kernels, spread(): pl.pallas_call(functools.partial(spread_kernel, span, share), grid_spec=p...  8.47 us
  transfers between devices with their start and end apart: 11, of which 9 were waited for; matrix products, arithmetic and copies ran while one was open for 3% of the time, Pallas kernels for 9%

profile of v1, /device:TPU:0, one launch (start us, length us, event | category | flops | bytes accessed | tf_op | source)
XLA Modules:
  0.0 266.4 jit_solution(10144748079299900748)
XLA Ops:
  0.6 4.5 %pick_negs.1 = bf16[8,400,128]{2,1,0:T(8,128)(2,1)} custom-call(s32[1,128]{1,0:T(1,128)} %neg_ref.1, bf16[400,4096]{1,0:T(8,128)(2,1)} %bitcast.23), custom_call_target="tpu_custom_call" | custom-call | flops 419430400 | bytes 3276800 | tf_op jit(solution)/shard_map/pick_negs/pallas_call | solution.py:65
  5.2 5.2 %all-to-all-start = ((bf16[8,400,128]{2,1,0:T(8,128)(2,1)}), bf16[8,400,128]{2,1,0:T(8,128)(2,1)S(1)}, u32[]{:S(2)}, u32[]{:S(2)}) async-start(bf16[8,400,128]{2,1,0:T(8,128)(2,1)} %pick_negs.1), calls=%async_computation | async-start | bytes 1638400 | tf_op jit(solution)/shard_map/all_to_all | solution.py:421
  10.3 16.8 %relation_step.1 = (f32[100,1024]{1,0:T(8,128)}, f32[400,1024]{1,0:T(8,128)}, f32[1,1024]{1,0:T(1,128)}, bf16[400,1024]{1,0:T(8,128)(2,1)}, s32[1,2048]{1,0:T(1,128)}) custom-call(s32[1,1024]{1,0:T(1,128)} %bitcast.41, f32[100,14824]{1,0:T(8,128)} %bitcast.43, f32[400,100]{1,0:T(8,128)} %bitcast.39, bf16[400,1024]{1,0:T(8,128)(2,1)} %bitcast.25, ...), custom_call_target="tpu_custom_call" | custom-call | flops 6800539648 | bytes 5929600 | tf_op jit(solution)/shard_map/relation_step/pallas_call | solution.py:141
  28.1 17.5 %score_step.1 = (bf16[32,402,128]{2,1,0:T(8,128)(2,1)}, bf16[1024,1024]{1,0:T(8,128)(2,1)}, bf16[400,1024]{1,0:T(8,128)(2,1)}, f32[400,1024]{1,0:T(8,128)}) custom-call(bf16[8,400,128]{2,1,0:T(8,128)(2,1)} %copy-done.4, f32[400,1024]{1,0:T(8,128)} %get-tuple-element.16.vec_ref, bf16[400,1024]{1,0:T(8,128)(2,1)} %bitcast.26, bf16[400,1024]{1,0:T(8,128)(2,1)} %bitcast.29, ...), custom_call_target="tpu_custom_call" | custom-call | flops 8388608000 | bytes 16777216 | tf_op jit(solution)/shard_map/score_step/pallas_call | solution.py:198
  45.6 7.5 %partial_step.1 = (bf16[102,1024]{1,0:T(8,128)(2,1)}, bf16[8,500,128]{2,1,0:T(8,128)(2,1)}) custom-call(bf16[1024,1024]{1,0:T(8,128)(2,1)} %get-tuple-element.21.probs_ref, bf16[400,1024]{1,0:T(8,128)(2,1)} %get-tuple-element.22.hrel_ref, f32[400,1024]{1,0:T(8,128)} %get-tuple-element.23.mix_ref, bf16[400,1024]{1,0:T(8,128)(2,1)} %bitcast.27, ...), custom_call_target="tpu_custom_call" | custom-call | flops 1 | bytes 1 | tf_op jit(solution)/shard_map/partial_step/pallas_call | solution.py:241
  53.1 2.9 %collective-permute-start.2 = (bf16[102,1024]{1,0:T(8,128)(2,1)}, bf16[102,1024]{1,0:T(8,128)(2,1)S(1)}, u32[]{:S(2)}, u32[]{:S(2)}) collective-permute-start(bf16[102,1024]{1,0:T(8,128)(2,1)} %get-tuple-element.26), channel_id=1, source_target_pairs={{0,6},{1,7},{2,4},{3,5},{4,2},{5,3},{6,0},{7,1},{8,14},{9,15},{10,... | collective-permute-start | bytes 626696 | tf_op jit(solution)/shard_map/ppermute | solution.py:394
  56.7 4.1 %all-to-all-start.2 = ((bf16[8,500,128]{2,1,0:T(8,128)(2,1)}), bf16[8,500,128]{2,1,0:T(8,128)(2,1)S(1)}, u32[]{:S(2)}, u32[]{:S(2)}) async-start(bf16[8,500,128]{2,1,0:T(8,128)(2,1)} %get-tuple-element.25), calls=%async_computation.2 | async-start | bytes 2064384 | tf_op jit(solution)/shard_map/all_to_all | solution.py:438
  60.8 1.6 collective-permute-done.2
  62.4 4.1 %collective-permute-done.1 = bf16[102,1024]{1,0:T(8,128)(2,1)S(1)} collective-permute-done((bf16[102,1024]{1,0:T(8,128)(2,1)}, bf16[102,1024]{1,0:T(8,128)(2,1)S(1)}, u32[]{:S(2)}, u32[]{:S(2)}) %collective-permute-start.1) | collective-permute-done | bytes 208928 | tf_op jit(solution)/shard_map/ppermute | solution.py:394
  66.5 0.9 collective-permute-done
  67.6 1.5 copy.13
  69.1 2.6 collective-permute-done.3
  71.7 1.2 copy.14.refs_1_
  72.9 4.7 %all-to-all-done.2.parts_ref.refs_2_ = bf16[8,500,128]{2,1,0:T(8,128)(2,1)S(1)} async-done(((bf16[8,500,128]{2,1,0:T(8,128)(2,1)}), bf16[8,500,128]{2,1,0:T(8,128)(2,1)S(1)}, u32[]{:S(2)}, u32[]{:S(2)}) %all-to-all-start.2) | async-done | bytes 1024032 | tf_op jit(solution)/shard_map/all_to_all | solution.py:438
  77.6 1.0 copy-done.2
  78.6 13.5 %gather_coef.1 = f32[4,100,512]{2,1,0:T(8,128)} custom-call(s32[1]{0:T(128)} %bitcast.9.me_ref, bf16[4,102,1024]{2,1,0:T(8,128)(2,1)} %copy-done.3, bf16[4,102,1024]{2,1,0:T(8,128)(2,1)} %copy.14.refs_1_, bf16[8,500,128]{2,1,0:T(8,128)(2,1)} %copy-done.2), custom_call_target="tpu_custom_call" | custom-call | flops 1 | bytes 1 | tf_op jit(solution)/shard_map/gather_coef/pallas_call | solution.py:274
  92.1 25.3 %all_to_all.20 = f32[4,100,512]{2,1,0:T(8,128)} all-to-all(f32[4,100,512]{2,1,0:T(8,128)} %gather_coef.1), channel_id=1, replica_groups=mesh['grp'=4,'dev'=8] {'grp'}, dimensions={0} | all-to-all | bytes 1638400 | tf_op jit(solution)/shard_map/all_to_all | solution.py:442
  117.4 4.2 %all-to-all-start.1 = ((bf16[32,402,128]{2,1,0:T(8,128)(2,1)}), bf16[32,402,128]{2,1,0:T(8,128)(2,1)S(1)}, u32[]{:S(2)}, u32[]{:S(2)}) async-start(bf16[32,402,128]{2,1,0:T(8,128)(2,1)} %get-tuple-element.20), calls=%async_computation.1 | async-start | bytes 6684672 | tf_op jit(solution)/shard_map/all_to_all | solution.py:430
  121.6 1.2 reduce_sum.9
  122.8 84.0 %all-gather.1 = bf16[4,100,512]{2,1,0:T(8,128)(2,1)S(1)} all-gather(bf16[1,100,512]{2,1,0:T(8,128)(2,1)S(1)} %bitcast.31), channel_id=2, replica_groups=mesh['grp'=4,'dev'=8] {'grp'}, dimensions={0}, use_global_device_ids=true | all-gather | bytes 512000 | tf_op jit(solution)/shard_map/all_gather | solution.py:444
  206.8 1.1 collective-permute-start.4
  207.9 1.0 collective-permute-start.6
  208.9 1.4 collective-permute-start.5
  210.3 9.3 %collective-permute-done.4 = bf16[4,100,512]{2,1,0:T(8,128)(2,1)S(1)} collective-permute-done((bf16[4,100,512]{2,1,0:T(8,128)(2,1)S(1)}, bf16[4,100,512]{2,1,0:T(8,128)(2,1)S(1)}, u32[]{:S(2)}, u32[]{:S(2)}) %collective-permute-start.4) | collective-permute-done | bytes 409632 | tf_op jit(solution)/shard_map/ppermute | solution.py:394
  219.6 7.1 %collective-permute-done.6 = bf16[4,100,512]{2,1,0:T(8,128)(2,1)S(1)} collective-permute-done((bf16[4,100,512]{2,1,0:T(8,128)(2,1)S(1)}, bf16[4,100,512]{2,1,0:T(8,128)(2,1)S(1)}, u32[]{:S(2)}, u32[]{:S(2)}) %collective-permute-start.6) | collective-permute-done | bytes 409632 | tf_op jit(solution)/shard_map/ppermute | solution.py:394
  226.6 1.4 collective-permute-done.5
  229.8 2.9 %collective-permute-done.7 = bf16[4,4,100,512]{3,1,2,0:T(4,128)(2,1)S(1)} collective-permute-done((bf16[4,4,100,512]{3,1,2,0:T(4,128)(2,1)S(1)}, bf16[4,4,100,512]{3,1,2,0:T(4,128)(2,1)S(1)}, u32[]{:S(2)}, u32[]{:S(2)}) %collective-permute-start.7) | collective-permute-done | bytes 1638432 | tf_op jit(solution)/shard_map/ppermute | solution.py:397
  232.7 1.5 copy.16.b_ref
  234.2 8.5 %spread.1 = (f32[100,14824]{1,0:T(8,128)}, f32[100,400]{1,0:T(8,128)}) custom-call(s32[8]{0:T(128)} %get-tuple-element.36.where_ref, s32[8]{0:T(128)} %get-tuple-element.35.which_ref, bf16[4,4,100,512]{3,2,1,0:T(8,128)(2,1)} %copy-done, bf16[4,4,100,512]{3,2,1,0:T(8,128)(2,1)} %copy.16.b_ref), custom_call_target="tpu_custom_call" | custom-call | flops 1 | bytes 1 | tf_op jit(solution)/shard_map/spread/pallas_call | solution.py:325
  242.6 1.8 copy.17
  244.4 1.7 copy-done.1
  246.1 20.3 %add_rows.1 = f32[400,4096]{1,0:T(8,128)} custom-call(bf16[32,402,128]{2,1,0:T(8,128)(2,1)} %copy-done.1, bf16[8,500,128]{2,1,0:T(8,128)(2,1)} %copy-done.2, s32[1,128]{1,0:T(1,128)} %neg_ref.1), custom_call_target="tpu_custom_call" | custom-call | flops 1 | bytes 1 | tf_op jit(solution)/shard_map/add_rows/pallas_call | solution.py:373
  (20 shorter events, 3.4 us)
Async XLA Ops:
  5.2 22.0 %all-to-all-start = ((bf16[8,400,128]{2,1,0:T(8,128)(2,1)}), bf16[8,400,128]{2,1,0:T(8,128)(2,1)S(1)}, u32[]{:S(2)}, u32[]{:S(2)}) async-start(bf16[8,400,128]{2,1,0:T(8,128)(2,1)} %pick_negs.1), calls=%async_computation | async-start | bytes 1638400 | tf_op jit(solution)/shard_map/all_to_all | solution.py:421
  27.1 0.9 copy-start.4
  53.1 14.4 %copy-start.5 = (bf16[102,1024]{1,0:T(8,128)(2,1)S(1)}, bf16[102,1024]{1,0:T(8,128)(2,1)}, u32[]{:S(2)}) copy-start(bf16[102,1024]{1,0:T(8,128)(2,1)} %get-tuple-element.26) | copy-start | bytes 626692
  53.1 9.3 %collective-permute-start.2 = (bf16[102,1024]{1,0:T(8,128)(2,1)}, bf16[102,1024]{1,0:T(8,128)(2,1)S(1)}, u32[]{:S(2)}, u32[]{:S(2)}) collective-permute-start(bf16[102,1024]{1,0:T(8,128)(2,1)} %get-tuple-element.26), channel_id=1, source_target_pairs={{0,6},{1,7},{2,4},{3,5},{4,2},{5,3},{6,0},{7,1},{8,14},{9,15},{10,... | collective-permute-start | bytes 626696 | tf_op jit(solution)/shard_map/ppermute | solution.py:394
  56.0 10.5 %collective-permute-start.1 = (bf16[102,1024]{1,0:T(8,128)(2,1)}, bf16[102,1024]{1,0:T(8,128)(2,1)S(1)}, u32[]{:S(2)}, u32[]{:S(2)}) collective-permute-start(bf16[102,1024]{1,0:T(8,128)(2,1)} %get-tuple-element.26), channel_id=1, source_target_pairs={{0,4},{1,5},{2,6},{3,7},{4,0},{5,1},{6,2},{7,3},{8,12},{9,13},{10,... | collective-permute-start | bytes 626696 | tf_op jit(solution)/shard_map/ppermute | solution.py:394
  56.6 10.9 %collective-permute-start = (bf16[102,1024]{1,0:T(8,128)(2,1)}, bf16[102,1024]{1,0:T(8,128)(2,1)S(1)}, u32[]{:S(2)}, u32[]{:S(2)}) collective-permute-start(bf16[102,1024]{1,0:T(8,128)(2,1)} %get-tuple-element.26), channel_id=1, source_target_pairs={{0,2},{1,3},{2,0},{3,1},{4,6},{5,7},{6,4},{7,5},{8,10},{9,11},{10,... | collective-permute-start | bytes 626696 | tf_op jit(solution)/shard_map/ppermute | solution.py:394
  56.7 20.9 %all-to-all-start.2 = ((bf16[8,500,128]{2,1,0:T(8,128)(2,1)}), bf16[8,500,128]{2,1,0:T(8,128)(2,1)S(1)}, u32[]{:S(2)}, u32[]{:S(2)}) async-start(bf16[8,500,128]{2,1,0:T(8,128)(2,1)} %get-tuple-element.25), calls=%async_computation.2 | async-start | bytes 2064384 | tf_op jit(solution)/shard_map/all_to_all | solution.py:438
  67.6 10.0 %copy-start.3 = (bf16[4,102,1024]{2,1,0:T(8,128)(2,1)}, bf16[4,102,1024]{2,1,0:T(8,128)(2,1)S(1)}, u32[]{:S(2)}) copy-start(bf16[4,102,1024]{2,1,0:T(8,128)(2,1)S(1)} %pad_maximum_fusion.1.refs_0_) | copy-start | bytes 2506756
  69.1 2.6 collective-permute-start.3
  77.6 1.0 copy-start.2
  117.4 127.0 %all-to-all-start.1 = ((bf16[32,402,128]{2,1,0:T(8,128)(2,1)}), bf16[32,402,128]{2,1,0:T(8,128)(2,1)S(1)}, u32[]{:S(2)}, u32[]{:S(2)}) async-start(bf16[32,402,128]{2,1,0:T(8,128)(2,1)} %get-tuple-element.20), calls=%async_computation.1 | async-start | bytes 6684672 | tf_op jit(solution)/shard_map/all_to_all | solution.py:430
  206.8 12.8 %collective-permute-start.4 = (bf16[4,100,512]{2,1,0:T(8,128)(2,1)S(1)}, bf16[4,100,512]{2,1,0:T(8,128)(2,1)S(1)}, u32[]{:S(2)}, u32[]{:S(2)}) collective-permute-start(bf16[4,100,512]{2,1,0:T(8,128)(2,1)S(1)} %all-gather.1), channel_id=1, source_target_pairs={{0,2},{1,3},{2,0},{3,1},{4,6},{5,7},{6,4},{7,5},{8,10},{9,11},{10,... | collective-permute-start | bytes 1228808 | tf_op jit(solution)/shard_map/ppermute | solution.py:394
  207.9 18.7 %collective-permute-start.6 = (bf16[4,100,512]{2,1,0:T(8,128)(2,1)S(1)}, bf16[4,100,512]{2,1,0:T(8,128)(2,1)S(1)}, u32[]{:S(2)}, u32[]{:S(2)}) collective-permute-start(bf16[4,100,512]{2,1,0:T(8,128)(2,1)S(1)} %all-gather.1), channel_id=1, source_target_pairs={{0,6},{1,7},{2,4},{3,5},{4,2},{5,3},{6,0},{7,1},{8,14},{9,15},{10,... | collective-permute-start | bytes 1228808 | tf_op jit(solution)/shard_map/ppermute | solution.py:394
  208.9 19.1 %collective-permute-start.5 = (bf16[4,100,512]{2,1,0:T(8,128)(2,1)S(1)}, bf16[4,100,512]{2,1,0:T(8,128)(2,1)S(1)}, u32[]{:S(2)}, u32[]{:S(2)}) collective-permute-start(bf16[4,100,512]{2,1,0:T(8,128)(2,1)S(1)} %all-gather.1), channel_id=1, source_target_pairs={{0,4},{1,5},{2,6},{3,7},{4,0},{5,1},{6,2},{7,3},{8,12},{9,13},{10,... | collective-permute-start | bytes 1228808 | tf_op jit(solution)/shard_map/ppermute | solution.py:394
  228.2 5.9 %copy-start = (bf16[4,4,100,512]{3,2,1,0:T(8,128)(2,1)}, bf16[4,4,100,512]{3,2,1,0:T(8,128)(2,1)S(1)}, u32[]{:S(2)}) copy-start(bf16[4,4,100,512]{3,2,1,0:T(8,128)(2,1)S(1)} %pad_maximum_fusion.a_ref) | copy-start | bytes 4915204
  229.1 3.6 %collective-permute-start.7 = (bf16[4,4,100,512]{3,1,2,0:T(4,128)(2,1)S(1)}, bf16[4,4,100,512]{3,1,2,0:T(4,128)(2,1)S(1)}, u32[]{:S(2)}, u32[]{:S(2)}) collective-permute-start(bf16[4,4,100,512]{3,1,2,0:T(4,128)(2,1)S(1)} %copy.15), channel_id=1, source_target_pairs={{0,1},{1,0},{2,3},{3,2},{4,5},{5,4},{6,7},{7,6},{8,9},{9,8},{10,11... | collective-permute-start | bytes 4915208 | tf_op jit(solution)/shard_map/ppermute | solution.py:397
  244.4 1.7 copy-start.1

commit v2 on v1

v2 whole, which is shorter than its diff:
```python
import functools
import math

import jax
import jax.numpy as jnp
from jax import lax
from jax.experimental import pallas as pl
from jax.experimental.pallas import tpu as pltpu
from jax.sharding import PartitionSpec as P

F32, BF16, I32 = jnp.float32, jnp.bfloat16, jnp.int32
LANES = 128
PAD = 112
VMEM_BYTES = 56 * 1024 * 1024


def nt(a, b, **kw):
    return lax.dot_general(a, b, (((1,), (1,)), ((), ())), preferred_element_type=F32, **kw)


def tn(a, b, **kw):
    return lax.dot_general(a, b, (((0,), (0,)), ((), ())), preferred_element_type=F32, **kw)


def nn(a, b, **kw):
    return lax.dot_general(a, b, (((1,), (0,)), ((), ())), preferred_element_type=F32, **kw)


def split(x):
    top = x.astype(BF16)
    return top, (x - top.astype(F32)).astype(BF16)


def padded(x):
    more = -x.shape[0] % 16
    return jnp.concatenate([x, jnp.zeros((more, x.shape[1]), x.dtype)], axis=0) if more else x


def precise(product, a, b):
    rows = a.shape[0]
    a = padded(a)
    tall = a.shape[0]
    a_top, a_low = split(a)
    b_top, b_low = split(b)
    both = product(jnp.concatenate([a_top, a_low], axis=0), b_top)
    return (both[0:tall] + both[tall:] + product(a_top, b_low))[0:rows]


def params():
    return pltpu.CompilerParams(vmem_limit_bytes=VMEM_BYTES)


def cost(flops, nbytes):
    return pl.CostEstimate(flops=flops, bytes_accessed=nbytes, transcendentals=0)


def hits(ids, rows, first):
    row = lax.broadcasted_iota(I32, (rows, ids.shape[1]), 0)
    return jnp.where(row == ids - first, 1.0, 0.0).astype(BF16)


def pick_negs_kernel(ids_ref, ent_ref, out_ref, acc_ref):
    step = pl.program_id(0)
    width = ent_ref.shape[1]
    part = nn(ent_ref[...], hits(ids_ref[...], width, step * width))

    @pl.when(step == 0)
    def _():
        acc_ref[...] = part

    @pl.when(step > 0)
    def _():
        acc_ref[...] += part

    @pl.when(step == pl.num_programs(0) - 1)
    def _():
        rows = acc_ref[...].astype(BF16)
        for k in range(out_ref.shape[0]):
            out_ref[k] = rows


def pick_negs(ids, ent_t, group):
    cols, ent = ent_t.shape
    width = 1024
    return pl.pallas_call(
        pick_negs_kernel,
        grid=(ent // width,),
        in_specs=[
            pl.BlockSpec((1, ids.shape[1]), lambda i: (0, 0)),
            pl.BlockSpec((cols, width), lambda i: (0, i)),
        ],
        out_specs=pl.BlockSpec((group, cols, ids.shape[1]), lambda i: (0, 0, 0)),
        out_shape=jax.ShapeDtypeStruct((group, cols, ids.shape[1]), BF16),
        scratch_shapes=[pltpu.VMEM((cols, ids.shape[1]), F32)],
        compiler_params=params(),
        cost_estimate=cost(2 * cols * ent * 128, cols * ent * 2),
        name="pick_negs",
    )(ids, ent_t)


def up_to_here():
    rows = lax.broadcasted_iota(I32, (LANES, LANES), 0)
    cols = lax.broadcasted_iota(I32, (LANES, LANES), 1)
    return jnp.where(rows <= cols, 1.0, 0.0).astype(BF16)


def relation_kernel(nrel, devices, plan, rel_ref, coef_ref, bases_ref, head_ref, tail_ref,
                    picked_ref, vec_ref, gate_ref, tgrad_ref, place_ref, halves, acc):
    step = pl.program_id(0)
    width = coef_ref.shape[1]
    nb = coef_ref.shape[0]
    lane = lax.broadcasted_iota(I32, (nb, width), 1) + step * width
    block = jnp.where(lane < nrel, coef_ref[...], 0.0)
    low = block - block.astype(BF16).astype(F32)
    tall = acc.shape[0] // 2
    spare = [jnp.zeros((tall - nb, width), F32)] * (tall > nb)
    halves[...] = jnp.concatenate([block, *spare, low, *spare], axis=0).astype(BF16)

    @pl.when(step == 0)
    def _():
        acc[...] = jnp.zeros_like(acc)

    acc[...] += nn(halves[...], hits(rel_ref[...], width, step * width))

    @pl.when(step == pl.num_programs(0) - 1)
    def _():
        picked = acc[0:nb] + acc[tall:tall + nb]
        picked_ref[...] = picked
        vec = precise(nn, bases_ref[...], picked)
        vec_ref[...] = vec
        head = head_ref[...].astype(F32)
        head_vec = head * vec
        score = jnp.sum(head_vec * tail_ref[...].astype(F32), axis=0, keepdims=True)
        gate = jax.nn.sigmoid(-score)
        gate_ref[...] = gate
        tgrad_ref[...] = (-gate * head * vec).astype(BF16)
        triples = rel_ref.shape[1]
        upto = up_to_here()
        number = lax.broadcasted_iota(I32, (devices, LANES), 0)
        span, slots, room = plan
        rel = rel_ref[...]
        later = lax.broadcasted_iota(I32, (LANES, triples), 1)
        row = lax.broadcasted_iota(I32, (LANES, triples), 0)
        seen = jnp.zeros((1, triples), F32)
        same = []
        for b in range(triples // LANES):
            down = jnp.broadcast_to(
                rel[:, b * LANES:(b + 1) * LANES].astype(F32), (LANES, LANES)).T[:, 0:1]
            equal = jnp.where(down.astype(I32) == rel, 1.0, 0.0)
            same.append(equal.astype(BF16))
            before = jnp.where(row + b * LANES < later, equal, 0.0)
            seen = seen + jnp.sum(before, axis=0, keepdims=True)
        first = jnp.where(seen == 0.0, 1.0, 0.0)
        summer = rel // span
        marks = []
        for b in range(triples // LANES):
            lanes = slice(b * LANES, (b + 1) * LANES)
            marks.append(jnp.where(number == summer[:, lanes], first[:, lanes], 0.0))
        sums = nn(jnp.concatenate(marks, axis=0).astype(BF16), upto)
        carry = jnp.zeros((devices, 1), F32)
        lead = []
        for b, mark in enumerate(marks):
            part = sums[b * devices:(b + 1) * devices]
            lead.append(jnp.sum(mark * (part + carry - 1.0), axis=0, keepdims=True))
            carry = carry + part[:, LANES - 1:LANES]
        lead = jnp.minimum(jnp.concatenate(lead, axis=1), 255.0)
        lead = jnp.broadcast_to(lead, (16, triples)).astype(BF16)
        slot = nn(lead, jnp.concatenate(same, axis=0))[0:1].astype(I32)
        fits = slot < room
        place_ref[0:1] = jnp.where(fits, summer * slots + slot, -1)
        place_ref[1:2] = jnp.where(seen == 0.0, rel - summer * span, -1)
        over = jnp.max(jnp.where(fits, 0, 1), axis=1, keepdims=True)
        place_ref[2:3] = jnp.broadcast_to(over, (1, triples))


def relation_step(rel, coef_t, bases_t, head_t, tail_t, devices, plan):
    nb, nrel = coef_t.shape
    cols, triples = head_t.shape
    width = 1920
    steps = pl.cdiv(nrel, width)
    tall = pl.cdiv(nb, 8) * 8
    whole = lambda shape: pl.BlockSpec(shape, lambda i: (0,) * len(shape))
    outs = [((nb, triples), F32), ((cols, triples), F32), ((1, triples), F32),
            ((cols, triples), BF16), ((3, triples), I32)]
    return pl.pallas_call(
        functools.partial(relation_kernel, nrel, devices, plan),
        grid=(steps,),
        in_specs=[
            whole((1, triples)),
            pl.BlockSpec((nb, width), lambda i: (0, i)),
            whole((cols, nb)), whole((cols, triples)), whole((cols, triples)),
        ],
        out_specs=[whole(s) for s, _ in outs],
        out_shape=[jax.ShapeDtypeStruct(s, d) for s, d in outs],
        scratch_shapes=[pltpu.VMEM((2 * tall, width), BF16), pltpu.VMEM((2 * tall, triples), F32)],
        compiler_params=params(),
        cost_estimate=cost(2 * 2 * PAD * nrel * triples, nb * nrel * 4),
        name="relation_step",
    )(rel, coef_t, bases_t, head_t, tail_t)


def score_kernel(neg_count, negs_ref, vec_ref, head_ref, tail_ref, gate_ref, tgrad_ref, row_ref,
                 bases_ref, picked_ref, grads_ref, rows_ref, base_ref, probs_ref, hrel_ref):
    group, cols, per = negs_ref.shape
    triples = head_ref.shape[1]
    vec = vec_ref[...]
    head = head_ref[...].astype(F32)
    head_rel = (head * vec).astype(BF16)
    hrel_ref[...] = head_rel
    mix = jnp.zeros((cols, triples), F32)
    for first in range(0, group, 8):
        negs = jnp.concatenate([negs_ref[first + k] for k in range(8)], axis=1)
        probs = jax.nn.sigmoid(tn(negs, head_rel)).astype(BF16)
        probs_ref[first * per:(first + 8) * per] = probs
        mix = mix + nn(negs, probs)
    tail = tail_ref[...].astype(F32)
    gate = gate_ref[...]
    rel_grad = -gate * head * tail + head * mix / neg_count
    rows_ref[...] = precise(nn, bases_ref[...].T, rel_grad)
    base_ref[...] = precise(nt, picked_ref[...], rel_grad)
    grads_ref[0:cols, 0:triples] = (-gate * vec * tail + vec * mix / neg_count).astype(BF16)
    grads_ref[0:cols, triples:] = tgrad_ref[...]
    for side in range(2):
        ids = row_ref[side:side + 1]
        lanes = slice(side * triples, (side + 1) * triples)
        high = ids // 64
        pair = jnp.concatenate([high, ids - high * 64], axis=0).astype(F32)
        more = grads_ref.shape[0] - cols - 2
        if more:
            pair = jnp.concatenate([pair, jnp.zeros((more, triples), F32)], axis=0)
        grads_ref[cols:, lanes] = pair.astype(BF16)


def score_step(negs, vec, head_t, tail_t, gate, tgrad, rows, bases_t, picked, tall, neg_count):
    group, cols, per = negs.shape
    triples = head_t.shape[1]
    nb = bases_t.shape[1]
    outs = [((tall, 2 * triples), BF16), ((nb, triples), F32), ((nb, cols), F32),
            ((group * per, triples), BF16), ((cols, triples), BF16)]
    return pl.pallas_call(
        functools.partial(score_kernel, neg_count),
        out_shape=[jax.ShapeDtypeStruct(s, d) for s, d in outs],
        compiler_params=params(),
        cost_estimate=cost(2 * cols * triples * 2 * group * per, 16 << 20),
        name="score_step",
    )(negs, vec, head_t, tail_t, gate, tgrad, rows, bases_t, picked)


def band(rows, slots):
    bands = LANES // slots
    return rows if bands == 1 else pl.cdiv(pl.cdiv(rows, bands), 16) * 16


def order_kernel(devices, slots, grads_ref, owner_ref, send_ref, pos):
    owners, high, _ = send_ref.shape
    bands = LANES // slots
    step = pl.program_id(0)

    @pl.when(step == 0)
    def _():
        owner = owner_ref[...]
        triples = owner.shape[1]
        number = lax.broadcasted_iota(I32, (devices, LANES), 0)
        parts, marks = [], []
        for side in range(2):
            for b in range(triples // LANES):
                part = owner[side:side + 1, b * LANES:(b + 1) * LANES]
                parts.append(part)
                marks.append(jnp.where(number == part, 1.0, 0.0))
        sums = nn(jnp.concatenate(marks, axis=0).astype(BF16), up_to_here())
        carry = jnp.zeros((devices, 1), F32)
        for b, (part, mark) in enumerate(zip(parts, marks)):
            here = sums[b * devices:(b + 1) * devices]
            slot = jnp.sum(mark * (here + carry), axis=0, keepdims=True) - 1.0
            pos[:, b * LANES:(b + 1) * LANES] = part * slots + slot.astype(I32)
            carry = carry + here[:, LANES - 1:LANES]

    part = nt(grads_ref[...], hits(pos[...], owners * slots, step * owners * slots))
    part = part.astype(BF16)
    for o in range(owners):
        at = o * slots
        block = [part[b * high:(b + 1) * high, at:at + slots] for b in range(bands)]
        send_ref[o] = jnp.concatenate(block, axis=1)


def order_slots(grads, owner_t, devices, slots, rows):
    owners = 512 // slots
    high = band(rows, slots)
    whole = lambda shape: pl.BlockSpec(shape, lambda i: (0,) * len(shape))
    return pl.pallas_call(
        functools.partial(order_kernel, devices, slots),
        grid=(devices // owners,),
        in_specs=[whole(grads.shape), whole(owner_t.shape)],
        out_specs=pl.BlockSpec((owners, high, LANES), lambda i: (i, 0, 0)),
        out_shape=jax.ShapeDtypeStruct((devices, high, LANES), BF16),
        scratch_shapes=[pltpu.VMEM((1, grads.shape[1]), I32)],
        compiler_params=params(),
        cost_estimate=cost(rows * grads.shape[1] * devices * slots * 2, 4 << 20),
        name="order_slots",
    )(grads, owner_t)


def partial_kernel(neg_count, me_ref, probs_ref, hrel_ref, parts_ref, block):
    half, per = parts_ref.shape[1], parts_ref.shape[3]
    for first in range(0, 2 * half, 8):
        part = nt(hrel_ref[...], probs_ref[first * per:(first + 8) * per]) / neg_count
        block[...] = part
        for k in range(8):
            lane = pl.multiple_of((k ^ me_ref[0]) * per, per)
            parts_ref[k % 2, (first + k) // 2] = block[:, pl.ds(lane, per)].astype(BF16)


def partial_step(me, probs, hrel, group, neg_count):
    cols = hrel.shape[0]
    whole = lambda shape: pl.BlockSpec(shape, lambda i, me: (0,) * len(shape))
    shape = (2, group // 2, cols, LANES)
    return pl.pallas_call(
        functools.partial(partial_kernel, neg_count),
        grid_spec=pltpu.PrefetchScalarGridSpec(
            num_scalar_prefetch=1,
            grid=(1,),
            in_specs=[whole(probs.shape), whole(hrel.shape)],
            out_specs=whole(shape),
            scratch_shapes=[pltpu.VMEM((cols, 8 * LANES), F32)],
        ),
        out_shape=jax.ShapeDtypeStruct(shape, BF16),
        compiler_params=params(),
        cost_estimate=cost(1, 1),
        name="partial_step",
    )(me, probs, hrel)


def coef_order_kernel(plan, share, rows_ref, base_ref, place_ref, send_ref):
    span, slots, room = plan
    devices, high, _ = send_ref.shape
    nb, triples = rows_ref.shape
    cols = base_ref.shape[1]
    lanes = devices * slots

    def halves(block):
        spare = jnp.zeros((PAD - block.shape[0], block.shape[1]), F32)
        block = jnp.concatenate([block, spare], axis=0)
        top = block.astype(BF16)
        return jnp.concatenate([top, (block - top.astype(F32)).astype(BF16)], axis=0)

    local = place_ref[1:2]
    lead = local >= 0
    high_id = local // 64
    pair = jnp.concatenate([high_id, local - high_id * 64], axis=0)
    pair = jnp.where(lead, pair, 0).astype(F32)
    left = halves(jnp.concatenate([rows_ref[...], pair], axis=0))
    both = nt(left, hits(place_ref[0:1], lanes, 0))
    column = lax.broadcasted_iota(I32, (1, cols), 1)
    owner = column // share
    spots = owner * slots + room + column - owner * share
    both = both + nt(halves(base_ref[...]), hits(spots, lanes, 0))
    both = both[0:PAD] + both[PAD:]
    row = lax.broadcasted_iota(I32, (PAD, lanes), 0)
    both = jnp.where(row == nb + 2, place_ref[2:3, 0:1].astype(F32), both)
    bands = LANES // slots
    if bands * high > PAD:
        both = jnp.concatenate([both, jnp.zeros((bands * high - PAD, lanes), F32)], axis=0)
    for o in range(devices):
        block = [both[b * high:(b + 1) * high, o * slots:(o + 1) * slots] for b in range(bands)]
        send_ref[o] = jnp.concatenate(block, axis=1).astype(BF16)


def coef_order(rows, base, place, devices, plan, share):
    high = pl.cdiv(PAD * plan[1], 8 * LANES) * 8
    return pl.pallas_call(
        functools.partial(coef_order_kernel, plan, share),
        out_shape=jax.ShapeDtypeStruct((devices, high, LANES), BF16),
        compiler_params=params(),
        cost_estimate=cost(1, 1),
        name="coef_order",
    )(rows, base, place)


def coef_sum_kernel(nb, plan, recv_ref, out_ref, flag_ref, left):
    span, slots, room = plan
    sources, high, _ = recv_ref.shape
    bands = LANES // slots
    for s in range(0, sources, bands):
        lanes = slice(s * slots, (s + bands) * slots)
        tall = []
        for b in range(bands):
            block = [recv_ref[s + k, :, b * slots:(b + 1) * slots] for k in range(bands)]
            tall.append(jnp.concatenate(block, axis=1).astype(F32))
        left[:, lanes] = jnp.concatenate(tall, axis=0)[0:PAD].astype(BF16)
    extra = left[PAD - 16:PAD].astype(F32)
    at = nb - (PAD - 16)
    ids = (extra[at:at + 1] * 64.0 + extra[at + 1:at + 2]).astype(I32)
    lane = lax.broadcasted_iota(I32, ids.shape, 1)
    lane = lane - lane // slots * slots
    ids = jnp.where(lane < room, ids, span + lane - room)
    total = nt(left[0:PAD], hits(ids, out_ref.shape[1], 0))
    out_ref[...] = total[0:nb].astype(BF16)
    over = jnp.max(extra[at + 2:at + 3], axis=1, keepdims=True)
    flag_ref[...] = jnp.broadcast_to(over, flag_ref.shape).astype(I32)


def coef_sum(recv, nb, plan, width):
    sources = recv.shape[0]
    slots = plan[1]
    return pl.pallas_call(
        functools.partial(coef_sum_kernel, nb, plan),
        out_shape=[jax.ShapeDtypeStruct((nb, width), BF16), jax.ShapeDtypeStruct((1, LANES), I32)],
        scratch_shapes=[pltpu.VMEM((PAD, sources * slots), BF16)],
        compiler_params=params(),
        cost_estimate=cost(1, 1),
        name="coef_sum",
    )(recv)


def spread_kernel(span, share, place_ref, *refs):
    sets, (coef_ref, base_ref, pieces, strips) = refs[:-4], refs[-4:]
    step = pl.program_id(0)
    group, layers, nb, _ = pieces.shape

    @pl.when(step == 0)
    def _():
        number = 0
        for ref in sets:
            for s in range(ref.shape[0]):
                pieces[number ^ place_ref[0]] = ref[s]
                number += 1

    slab = lax.rem(place_ref[1] - step + layers, layers)
    row = [pieces[k, slab].astype(F32) for k in range(group)]
    coef_ref[...] = jnp.concatenate([r[:, 0:span] for r in row], axis=1)
    strip = jnp.concatenate([r[:, span:span + share] for r in row], axis=1)
    strips[step] = jnp.concatenate([strip, jnp.zeros((PAD - nb, strip.shape[1]), F32)], axis=0)

    @pl.when(step == layers - 1)
    def _():
        whole = jnp.concatenate([strips[g] for g in range(layers)], axis=1)
        base_ref[...] = whole[0:nb, 0:base_ref.shape[0]].T


def spread(me, layer, sets, span, share, nrel, cols):
    group = sum(s.shape[0] for s in sets)
    _, layers, nb, width = sets[0].shape
    whole = lambda shape: pl.BlockSpec(shape, lambda i, place: (0,) * len(shape))
    return pl.pallas_call(
        functools.partial(spread_kernel, span, share),
        grid_spec=pltpu.PrefetchScalarGridSpec(
            num_scalar_prefetch=1,
            grid=(layers,),
            in_specs=[whole(s.shape) for s in sets],
            out_specs=[
                pl.BlockSpec((nb, group * span), lambda i, place: (0, i)),
                whole((cols, nb)),
            ],
            scratch_shapes=[pltpu.VMEM((group, layers, nb, width), BF16),
                            pltpu.VMEM((layers, PAD, group * share), F32)],
        ),
        out_shape=[jax.ShapeDtypeStruct((nb, nrel), F32), jax.ShapeDtypeStruct((cols, nb), F32)],
        compiler_params=params(),
        cost_estimate=cost(1, 1),
        name="spread",
    )(jnp.concatenate([me, layer]), *sets)


def add_rows_kernel(slots, recv_ref, neg_ref, *refs):
    part_refs, (out_ref, grads, ids, sems) = refs[:-4], refs[-4:]
    step = pl.program_id(0)
    cols, width = out_ref.shape
    sources, high, _ = recv_ref.shape
    bands = LANES // slots
    lanes = sources * slots

    @pl.when(step == 0)
    def _():
        copies = []
        if bands == 1:
            for s in range(sources):
                to = grads.at[:, s * slots:(s + 1) * slots]
                copies.append(pltpu.make_async_copy(recv_ref.at[s], to, sems.at[s]))
        else:
            for s in range(0, sources, bands):
                at = slice(s * slots, (s + bands) * slots)
                for b in range(bands):
                    block = [recv_ref[s + k, :, b * slots:(b + 1) * slots] for k in range(bands)]
                    grads[b * high:(b + 1) * high, at] = jnp.concatenate(block, axis=1)
        for copy in copies:
            copy.start()
        total = jnp.zeros((cols, LANES), F32)
        for ref in part_refs:
            for k in range(ref.shape[0]):
                total = total + ref[k].astype(F32)
        top, low = split(total)
        grads[0:cols, lanes:lanes + LANES] = top
        grads[0:cols, lanes + LANES:] = low
        ids[:, lanes:lanes + LANES] = neg_ref[...]
        ids[:, lanes + LANES:] = neg_ref[...]
        for copy in copies:
            copy.wait()
        pair = grads[cols:cols + 2, 0:lanes].astype(F32)
        ids[:, 0:lanes] = (pair[0:1] * 64.0 + pair[1:2]).astype(I32)

    out_ref[...] = nt(grads[0:cols], hits(ids[...], width, step * width))


def add_rows(recv, slots, cols, ent, neg_ids, part_sets):
    sources, high, _ = recv.shape
    bands = LANES // slots
    width = 1024
    lanes = sources * slots + 2 * LANES
    whole = lambda shape: pl.BlockSpec(shape, lambda i: (0,) * len(shape))
    there = pl.BlockSpec(memory_space=pltpu.HBM) if bands == 1 else whole(recv.shape)
    return pl.pallas_call(
        functools.partial(add_rows_kernel, slots),
        grid=(ent // width,),
        in_specs=[there] + [whole(r.shape) for r in (neg_ids, *part_sets)],
        out_specs=pl.BlockSpec((cols, width), lambda i: (0, i)),
        out_shape=jax.ShapeDtypeStruct((cols, ent), F32),
        scratch_shapes=[pltpu.VMEM((bands * high, lanes), BF16),
                        pltpu.VMEM((1, lanes), I32),
                        pltpu.SemaphoreType.DMA((sources,))],
        compiler_params=params(),
        cost_estimate=cost(1, 1),
        name="add_rows",
    )(recv, neg_ids, *part_sets)


def from_group(block, group):
    block = block[None]
    if group != 8:
        return [lax.all_gather(block, "dev", axis=0, tiled=True)]
    swap = lambda x, far: lax.ppermute(x, "dev", [(i, i ^ far) for i in range(group)])
    blocks = {0: block, 2: swap(block, 2), 4: swap(block, 4), 6: swap(block, 6)}
    for far in (0, 2, 4, 6):
        blocks[far + 1] = swap(blocks[far], 1)
    return [blocks[t] for t in range(group)]


def sum_here(parts, group):
    if group != 8:
        parts = parts.swapaxes(0, 1).reshape((group,) + parts.shape[2:])
        return [lax.all_to_all(parts, "dev", 0, 0, tiled=True)]
    swap = lambda x, far: lax.ppermute(x, "dev", [(i, i ^ far) for i in range(group)])
    pairs = parts[0].astype(F32) + swap(parts[1], 1).astype(F32)
    pairs = pairs.astype(BF16)
    return [pairs[0:1]] + [swap(pairs[n:n + 1], 2 * n) for n in (1, 2, 3)]


def shift_layers(block, far, layers):
    return lax.ppermute(block, "grp", [(i, (i + far) % layers) for i in range(layers)])


def everywhere(values):
    for axis in ("dev", "grp"):
        count = lax.axis_size(axis)
        ring = [(i, (i + 1) % count) for i in range(count)]

        def turn(_, state):
            near = tuple(lax.ppermute(v, axis, ring) for v in state[0])
            return near, tuple(t + n for t, n in zip(state[1], near))

        values = lax.fori_loop(0, count - 1, turn, (values, values))[1]
    return values


def per_device(head_emb, tail_emb, relation, owners, owner_rows, entities, neg_rows, coef, bases):
    triples, cols = head_emb.shape
    group = lax.axis_size("dev")
    layers = lax.axis_size("grp")
    devices = layers * group
    neg_count = neg_rows.shape[1] * group
    ent_local = entities.shape[0]
    nrel, nb = coef.shape
    cap = 4 * triples // devices
    tall = LANES // cap * band(cols + 2, cap)
    share = pl.cdiv(cols, devices)
    step = LANES // math.gcd(group, LANES)
    span = pl.cdiv(pl.cdiv(nrel, devices), step) * step
    slots = 2 * triples // devices
    plan = (span, slots, slots - share)
    width = pl.cdiv(span + share, LANES) * LANES

    head_t, tail_t, owner_t, row_t = head_emb.T, tail_emb.T, owners.T, owner_rows.T
    coef_t, bases_t = coef.T, bases.T
    rel = relation.reshape(1, triples)

    sent_negs = pick_negs(neg_rows, entities.T, group)
    negs = lax.all_to_all(sent_negs, "dev", 0, 0, tiled=True)
    picked, vec, gate, tgrad, place = relation_step(
        rel, coef_t, bases_t, head_t, tail_t, devices, plan)
    grads, rows, base, probs, hrel = score_step(
        negs, vec, head_t, tail_t, gate, tgrad, row_t, bases_t, picked, tall, neg_count)
    coef_send = coef_order(rows, base, place, devices, plan, share)
    coef_recv = lax.all_to_all(coef_send, ("grp", "dev"), 0, 0, tiled=True)
    send = order_slots(grads, owner_t, devices, cap, cols + 2)
    send, coef_recv = lax.optimization_barrier((send, coef_recv))
    piece, flag = coef_sum(coef_recv, nb, plan, width)
    slabs = [piece] + [shift_layers(piece, far, layers) for far in range(1, layers)]
    send, slabs = lax.optimization_barrier((send, slabs))
    recv = lax.all_to_all(send, ("grp", "dev"), 0, 0, tiled=True)

    me = lax.axis_index("dev").astype(I32).reshape(1)
    layer = lax.axis_index("grp").astype(I32).reshape(1)
    at = me if group == 8 else jnp.zeros((1,), I32)
    pieces = from_group(jnp.stack(slabs), group)

    def packed():
        return tuple(spread(at, layer, pieces, span, share, nrel, cols))

    def dense():
        return everywhere((jnp.zeros((nb, nrel), F32).at[:, relation].add(rows), base.T))

    parts = sum_here(partial_step(at, probs, hrel, group, neg_count), group)
    parts, pieces = lax.optimization_barrier((parts, pieces))
    coef_grad, bases_grad = lax.cond(flag[0, 0] == 0, packed, dense)
    ent_grad = add_rows(recv, cap, cols, ent_local, neg_rows, parts)
    return ent_grad.T, coef_grad.T, bases_grad.T


def solution(mesh):
    return jax.shard_map(
        per_device,
        mesh=mesh,
        in_specs=(
            P(("grp", "dev"), None),
            P(("grp", "dev"), None),
            P(("grp", "dev")),
            P(("grp", "dev"), None),
            P(("grp", "dev"), None),
            P(("grp", "dev"), None),
            P(None, ("grp", "dev")),
            P(),
            P(),
        ),
        out_specs=(P(("grp", "dev"), None), P(), P()),
        check_vma=False,
    )
```

time: 267 us -> 186 us (0.70)
  the two profiles are of different devices: /device:TPU:0 before, /device:TPU:16 now
where the time goes in v2:
time: 186 us; the launch traced here: 185 us
  Pallas kernels  75.3 us (40%)
  waiting for transfers between devices  67.1 us (36%)
  starting transfers between devices  31.1 us (17%)
  local copies, waits for them, and re-layouts  7.12 us (4%)
  other arithmetic  3.53 us (2%)
    ppermute x7, waiting for transfers between devices, from_group(): lax.ppermute(x, 'dev', [(i, i ^ far) for i in range(group)])  43.7 us
    pallas_call x1, Pallas kernels, add_rows(): pl.pallas_call(functools.partial(add_rows_kernel, slots), grid=(ent // wi...  19.7 us
    pallas_call x1, Pallas kernels, relation_step(): pl.pallas_call(functools.partial(relation_kernel, nrel, devices, plan), g...  15.7 us
    ppermute x4, waiting for transfers between devices, sum_here(): lax.ppermute(x, 'dev', [(i, i ^ far) for i in range(group)])  13.6 us
    pallas_call x1, Pallas kernels, order_slots(): pl.pallas_call(functools.partial(order_kernel, devices, slots), grid=(dev...  11.3 us
    ppermute x3, waiting for transfers between devices, shift_layers(): lax.ppermute(block, 'grp', [(i, (i + far) % layers) for i in range(layers)])  9.21 us
    ppermute x4, starting transfers between devices, sum_here(): lax.ppermute(x, 'dev', [(i, i ^ far) for i in range(group)])  8.87 us
    pallas_call x1, Pallas kernels, score_step(): pl.pallas_call(functools.partial(score_kernel, neg_count), out_shape=[jax...  7.41 us
  transfers between devices with their start and end apart: 17, of which 10 were waited for; matrix products, arithmetic and copies ran while one was open for 3% of the time, Pallas kernels for 20%

profile of v2, /device:TPU:16, one launch (start us, length us, event | category | flops | bytes accessed | tf_op | source)
XLA Modules:
  0.0 185.1 jit_solution(10183462764658743813)
XLA Ops:
  0.6 4.5 %pick_negs.1 = bf16[8,400,128]{2,1,0:T(8,128)(2,1)} custom-call(s32[1,128]{1,0:T(1,128)} %neg_ref.1, bf16[400,4096]{1,0:T(8,128)(2,1)} %bitcast.39), custom_call_target="tpu_custom_call" | custom-call | flops 419430400 | bytes 3276800 | tf_op jit(solution)/shard_map/pick_negs/pallas_call | solution.py:85
  5.2 3.7 %all-to-all-start = ((bf16[8,400,128]{2,1,0:T(8,128)(2,1)}), bf16[8,400,128]{2,1,0:T(8,128)(2,1)S(1)}, u32[]{:S(2)}, u32[]{:S(2)}) async-start(bf16[8,400,128]{2,1,0:T(8,128)(2,1)} %pick_negs.1), calls=%async_computation | async-start | bytes 1638400 | tf_op jit(solution)/shard_map/all_to_all | solution.py:586
  8.9 15.7 %relation_step.1 = (f32[100,1024]{1,0:T(8,128)}, f32[400,1024]{1,0:T(8,128)}, f32[1,1024]{1,0:T(1,128)}, bf16[400,1024]{1,0:T(8,128)(2,1)}, s32[3,1024]{1,0:T(4,128)}) custom-call(s32[1,1024]{1,0:T(1,128)} %bitcast.43, f32[100,14824]{1,0:T(8,128)} %bitcast.44, f32[400,100]{1,0:T(8,128)} %bitcast.49, bf16[400,1024]{1,0:T(8,128)(2,1)} %bitcast.45, ...), custom_call_target="tpu_custom_call" | custom-call | flops 6800539648 | bytes 5929600 | tf_op jit(solution)/shard_map/relation_step/pallas_call | solution.py:185
  25.4 7.4 %score_step.1 = (bf16[402,2048]{1,0:T(8,128)(2,1)}, f32[100,1024]{1,0:T(8,128)S(1)}, f32[100,400]{1,0:T(8,128)S(1)}, bf16[1024,1024]{1,0:T(8,128)(2,1)}, bf16[400,1024]{1,0:T(8,128)(2,1)}) custom-call(bf16[8,400,128]{2,1,0:T(8,128)(2,1)} %copy-done.6, f32[400,1024]{1,0:T(8,128)} %get-tuple-element.132.vec_ref, bf16[400,1024]{1,0:T(8,128)(2,1)} %bitcast.46, ...), custom_call_target="tpu_custom_call" | custom-call | flops 1677721600 | bytes 16777216 | tf_op jit(solution)/shard_map/score_step/pallas_call | solution.py:240
  33.7 3.7 %coef_order.1 = bf16[32,56,128]{2,1,0:T(8,128)(2,1)} custom-call(f32[100,1024]{1,0:T(8,128)S(1)} %get-tuple-element.137.rows_ref, f32[100,400]{1,0:T(8,128)S(1)} %get-tuple-element.138.base_ref, s32[3,1024]{1,0:T(4,128)} %get-tuple-element.139.place_ref), custom_call_target="tpu_custom_call" | custom-call | flops 1 | bytes 1 | tf_op jit(solution)/shard_map/coef_order/pallas_call | solution.py:370
  37.4 6.4 %all-to-all-start.1 = ((bf16[32,56,128]{2,1,0:T(8,128)(2,1)}), bf16[32,56,128]{2,1,0:T(8,128)(2,1)S(1)}, u32[]{:S(2)}, u32[]{:S(2)}) async-start(bf16[32,56,128]{2,1,0:T(8,128)(2,1)} %coef_order.1), calls=%async_computation.1 | async-start | bytes 917504 | tf_op jit(solution)/shard_map/all_to_all | solution.py:592
  43.8 11.3 %order_slots.1 = bf16[32,402,128]{2,1,0:T(8,128)(2,1)} custom-call(bf16[402,2048]{1,0:T(8,128)(2,1)} %get-tuple-element.136.grads_ref, s32[2,1024]{1,0:T(2,128)} %bitcast.52), custom_call_target="tpu_custom_call" | custom-call | flops 6744440832 | bytes 4194304 | tf_op jit(solution)/shard_map/order_slots/pallas_call | solution.py:290
  56.5 2.6 %coef_sum.1 = (bf16[100,512]{1,0:T(8,128)(2,1)}, s32[1,128]{1,0:T(1,128)}) custom-call(bf16[32,56,128]{2,1,0:T(8,128)(2,1)} %copy-done.3), custom_call_target="tpu_custom_call" | custom-call | flops 1 | bytes 1 | tf_op jit(solution)/shard_map/coef_sum/pallas_call | solution.py:405
  59.1 2.5 %collective-permute-start.6 = (bf16[100,512]{1,0:T(8,128)(2,1)}, bf16[100,512]{1,0:T(8,128)(2,1)}, u32[]{:S(2)}, u32[]{:S(2)}) collective-permute-start(bf16[100,512]{1,0:T(8,128)(2,1)} %get-tuple-element.146), channel_id=1, source_target_pairs={{0,24},{8,0},{16,8},{24,16},{1,25},{9,1},{17,9},{25,17},{2,26},{10... | collective-permute-start | bytes 307208 | tf_op jit(solution)/shard_map/ppermute | solution.py:548
  61.5 1.4 collective-permute-start.5
  62.9 0.9 collective-permute-start.4
  63.9 5.5 %collective-permute-done.6 = bf16[100,512]{1,0:T(8,128)(2,1)} collective-permute-done((bf16[100,512]{1,0:T(8,128)(2,1)}, bf16[100,512]{1,0:T(8,128)(2,1)}, u32[]{:S(2)}, u32[]{:S(2)}) %collective-permute-start.6) | collective-permute-done | bytes 102432 | tf_op jit(solution)/shard_map/ppermute | solution.py:548
  69.4 1.6 collective-permute-done.5
  70.9 2.1 %collective-permute-done.4 = bf16[100,512]{1,0:T(8,128)(2,1)} collective-permute-done((bf16[100,512]{1,0:T(8,128)(2,1)}, bf16[100,512]{1,0:T(8,128)(2,1)}, u32[]{:S(2)}, u32[]{:S(2)}) %collective-permute-start.4) | collective-permute-done | bytes 102432 | tf_op jit(solution)/shard_map/ppermute | solution.py:548
  73.1 3.8 %all-to-all-start.2 = ((bf16[32,402,128]{2,1,0:T(8,128)(2,1)}), bf16[32,402,128]{2,1,0:T(8,128)(2,1)S(1)}, u32[]{:S(2)}, u32[]{:S(2)}) async-start(bf16[32,402,128]{2,1,0:T(8,128)(2,1)} %order_slots.1), calls=%async_computation.2 | async-start | bytes 6684672 | tf_op jit(solution)/shard_map/all_to_all | solution.py:598
  76.8 3.9 %partial_step.1 = bf16[2,4,400,128]{3,2,1,0:T(8,128)(2,1)} custom-call(s32[1]{0:T(128)} %bitcast.11.me_ref, bf16[1024,1024]{1,0:T(8,128)(2,1)} %get-tuple-element.144.probs_ref, bf16[400,1024]{1,0:T(8,128)(2,1)} %get-tuple-element.145.hrel_ref), custom_call_target="tpu_custom_call" | custom-call | flops 1 | bytes 1 | tf_op jit(solution)/shard_map/partial_step/pallas_call | solution.py:317
  80.8 1.0 slice_bitcast_fusion
  82.0 1.8 maximum_bitcast_fusion
  83.8 2.4 %collective-permute-start.16 = (bf16[1,4,100,512]{3,2,1,0:T(8,128)(2,1)}, bf16[1,4,100,512]{3,2,1,0:T(8,128)(2,1)}, u32[]{:S(2)}, u32[]{:S(2)}) collective-permute-start(bf16[1,4,100,512]{3,2,1,0:T(8,128)(2,1)} %maximum_bitcast_fusion), channel_id=1, source_target_pairs={{0,6},{1,7},{2,4},{3,5},{4,2},{5,3},{6,0},{7,1},{8,14},{9,15},{10,... | collective-permute-start | bytes 1228808 | tf_op jit(solution)/shard_map/ppermute | solution.py:530
  87.4 1.1 fusion.3
  88.5 32.8 %collective-permute-done.16 = bf16[1,4,100,512]{3,2,1,0:T(8,128)(2,1)} collective-permute-done((bf16[1,4,100,512]{3,2,1,0:T(8,128)(2,1)}, bf16[1,4,100,512]{3,2,1,0:T(8,128)(2,1)}, u32[]{:S(2)}, u32[]{:S(2)}) %collective-permute-start.16) | collective-permute-done | bytes 409632 | tf_op jit(solution)/shard_map/ppermute | solution.py:530
  121.3 5.4 %collective-permute-done.14 = bf16[1,4,100,512]{3,2,1,0:T(8,128)(2,1)} collective-permute-done((bf16[1,4,100,512]{3,2,1,0:T(8,128)(2,1)}, bf16[1,4,100,512]{3,2,1,0:T(8,128)(2,1)}, u32[]{:S(2)}, u32[]{:S(2)}) %collective-permute-start.14) | collective-permute-done | bytes 409632 | tf_op jit(solution)/shard_map/ppermute | solution.py:530
  126.8 5.5 %collective-permute-done.12 = bf16[1,4,100,512]{3,2,1,0:T(8,128)(2,1)} collective-permute-done((bf16[1,4,100,512]{3,2,1,0:T(8,128)(2,1)}, bf16[1,4,100,512]{3,2,1,0:T(8,128)(2,1)}, u32[]{:S(2)}, u32[]{:S(2)}) %collective-permute-start.12) | collective-permute-done | bytes 409632 | tf_op jit(solution)/shard_map/ppermute | solution.py:530
  132.9 5.2 %collective-permute-start.10 = (bf16[1,400,128]{2,1,0:T(8,128)(2,1)S(1)}, bf16[1,400,128]{2,1,0:T(8,128)(2,1)S(1)}, u32[]{:S(2)}, u32[]{:S(2)}) collective-permute-start(bf16[1,400,128]{2,1,0:T(8,128)(2,1)S(1)} %get-tuple-element.193), channel_id=1, source_target_pairs={{0,6},{1,7},{2,4},{3,5},{4,2},{5,3},{6,0},{7,1},{8,14},{9,15},{10,... | collective-permute-start | bytes 307208 | tf_op jit(solution)/shard_map/ppermute | solution.py:541
  138.1 4.7 %collective-permute-done.10.refs_3_ = bf16[1,400,128]{2,1,0:T(8,128)(2,1)S(1)} collective-permute-done((bf16[1,400,128]{2,1,0:T(8,128)(2,1)S(1)}, bf16[1,400,128]{2,1,0:T(8,128)(2,1)S(1)}, u32[]{:S(2)}, u32[]{:S(2)}) %collective-permute-start.10) | collective-permute-done | bytes 102432 | tf_op jit(solution)/shard_map/ppermute | solution.py:541
  142.8 3.2 %collective-permute-start.9 = (bf16[1,400,128]{2,1,0:T(8,128)(2,1)S(1)}, bf16[1,400,128]{2,1,0:T(8,128)(2,1)S(1)}, u32[]{:S(2)}, u32[]{:S(2)}) collective-permute-start(bf16[1,400,128]{2,1,0:T(8,128)(2,1)S(1)} %get-tuple-element.194), channel_id=1, source_target_pairs={{0,4},{1,5},{2,6},{3,7},{4,0},{5,1},{6,2},{7,3},{8,12},{9,13},{10,... | collective-permute-start | bytes 307208 | tf_op jit(solution)/shard_map/ppermute | solution.py:541
  146.0 4.5 %collective-permute-done.9.refs_2_ = bf16[1,400,128]{2,1,0:T(8,128)(2,1)S(1)} collective-permute-done((bf16[1,400,128]{2,1,0:T(8,128)(2,1)S(1)}, bf16[1,400,128]{2,1,0:T(8,128)(2,1)S(1)}, u32[]{:S(2)}, u32[]{:S(2)}) %collective-permute-start.9) | collective-permute-done | bytes 102432 | tf_op jit(solution)/shard_map/ppermute | solution.py:541
  151.5 4.4 %collective-permute-done.8.refs_1_ = bf16[1,400,128]{2,1,0:T(8,128)(2,1)S(1)} collective-permute-done((bf16[1,400,128]{2,1,0:T(8,128)(2,1)S(1)}, bf16[1,400,128]{2,1,0:T(8,128)(2,1)S(1)}, u32[]{:S(2)}, u32[]{:S(2)}) %collective-permute-start.8) | collective-permute-done | bytes 102432 | tf_op jit(solution)/shard_map/ppermute | solution.py:541
  156.5 7.1 %conditional.1 = ((f32[100,14824]{1,0:T(8,128)}, f32[400,100]{1,0:T(8,128)})) conditional(s32[]{:T(128)} %bitcast.20, (s32[1024]{0:T(1024)S(1)}, f32[100,1024]{1,0:T(8,128)}, f32[100,400]{1,0:T(8,128)}) %tuple.66, (s32[]{:T(128)}, s32[1]{0:T(128)}, bf16[1,4,100,512]{3,2,1,0:T(8,128)(2,1)}, bf16[1,4,100,512]{3,2,1,0:T(8,128)(2,1)}, ...), branch_computations={%region_0.0_spmd, %region_6.0_spmd} | conditional | flops 3150276 | bytes 239095040 | solution.py:613
  157.1 6.5 %spread.1 = (f32[100,14824]{1,0:T(8,128)}, f32[400,100]{1,0:T(8,128)}) custom-call(s32[2]{0:T(128)} %pad_add_fusion.place_ref, bf16[1,4,100,512]{3,2,1,0:T(8,128)(2,1)} %get-tuple-element.88.refs_0_, bf16[1,4,100,512]{3,2,1,0:T(8,128)(2,1)} %get-tuple-element.89.refs_1_, bf16[1,4,100,512]{3,2,1,0:T(8,128)(2,1)} %get-tuple-element.90.refs_2_, ...), custom_call_target="tpu_custom_call" | custom-call | flops 1 | bytes 1 | tf_op jit(solution)/shard_map/cond/branch_1_fun/spread/pallas_call | solution.py:444
  163.5 1.7 copy-done.2
  165.2 19.7 %add_rows.1 = f32[400,4096]{1,0:T(8,128)} custom-call(bf16[32,402,128]{2,1,0:T(8,128)(2,1)} %copy-done.2, s32[1,128]{1,0:T(1,128)} %neg_ref.1, bf16[1,400,128]{2,1,0:T(8,128)(2,1)} %get-tuple-element.150.refs_0_, bf16[1,400,128]{2,1,0:T(8,128)(2,1)} %copy-done.12, bf16[1,400,128]{2,1,0:T(8,128)(2,1)} %copy-done.11, bf16[1,400,128]{2,1,0:T(8,128)(2,1)} %copy-done.10), custom_call_target="tpu_custom_call" | custom-call | flops 1 | bytes 1 | tf_op jit(solution)/shard_map/add_rows/pallas_call | solution.py:511
  (39 shorter events, 7.3 us)
Async XLA Ops:
  5.2 19.4 %all-to-all-start = ((bf16[8,400,128]{2,1,0:T(8,128)(2,1)}), bf16[8,400,128]{2,1,0:T(8,128)(2,1)S(1)}, u32[]{:S(2)}, u32[]{:S(2)}) async-start(bf16[8,400,128]{2,1,0:T(8,128)(2,1)} %pick_negs.1), calls=%async_computation | async-start | bytes 1638400 | tf_op jit(solution)/shard_map/all_to_all | solution.py:586
  24.5 0.9 copy-start.6
  32.9 0.8 copy-start.4
  32.9 0.9 copy-start.5
  37.4 18.3 %all-to-all-start.1 = ((bf16[32,56,128]{2,1,0:T(8,128)(2,1)}), bf16[32,56,128]{2,1,0:T(8,128)(2,1)S(1)}, u32[]{:S(2)}, u32[]{:S(2)}) async-start(bf16[32,56,128]{2,1,0:T(8,128)(2,1)} %coef_order.1), calls=%async_computation.1 | async-start | bytes 917504 | tf_op jit(solution)/shard_map/all_to_all | solution.py:592
  55.7 0.8 copy-start.3
  59.1 22.9 %copy-start.9 = (bf16[100,512]{1,0:T(8,128)(2,1)S(1)}, bf16[100,512]{1,0:T(8,128)(2,1)}, u32[]{:S(2)}) copy-start(bf16[100,512]{1,0:T(8,128)(2,1)} %get-tuple-element.146) | copy-start | bytes 307204
  59.1 92.3 %copy-start.14 = (s32[1,128]{1,0:T(1,128)S(1)}, s32[1,128]{1,0:T(1,128)}, u32[]{:S(2)}) copy-start(s32[1,128]{1,0:T(1,128)} %get-tuple-element.154) | copy-start | bytes 1540
  59.1 96.8 %copy-start.13 = (s32[1024]{0:T(1024)S(1)}, s32[1024]{0:T(1024)}, u32[]{:S(2)}) copy-start(s32[1024]{0:T(1024)} %param.17) | copy-start | bytes 12292
  59.1 10.3 %collective-permute-start.6 = (bf16[100,512]{1,0:T(8,128)(2,1)}, bf16[100,512]{1,0:T(8,128)(2,1)}, u32[]{:S(2)}, u32[]{:S(2)}) collective-permute-start(bf16[100,512]{1,0:T(8,128)(2,1)} %get-tuple-element.146), channel_id=1, source_target_pairs={{0,24},{8,0},{16,8},{24,16},{1,25},{9,1},{17,9},{25,17},{2,26},{10... | collective-permute-start | bytes 307208 | tf_op jit(solution)/shard_map/ppermute | solution.py:548
  61.5 9.4 %collective-permute-start.5 = (bf16[100,512]{1,0:T(8,128)(2,1)}, bf16[100,512]{1,0:T(8,128)(2,1)}, u32[]{:S(2)}, u32[]{:S(2)}) collective-permute-start(bf16[100,512]{1,0:T(8,128)(2,1)} %get-tuple-element.146), channel_id=1, source_target_pairs={{0,16},{8,24},{16,0},{24,8},{1,17},{9,25},{17,1},{25,9},{2,18},{10... | collective-permute-start | bytes 307208 | tf_op jit(solution)/shard_map/ppermute | solution.py:548
  62.9 10.1 %collective-permute-start.4 = (bf16[100,512]{1,0:T(8,128)(2,1)}, bf16[100,512]{1,0:T(8,128)(2,1)}, u32[]{:S(2)}, u32[]{:S(2)}) collective-permute-start(bf16[100,512]{1,0:T(8,128)(2,1)} %get-tuple-element.146), channel_id=1, source_target_pairs={{0,8},{8,16},{16,24},{24,0},{1,9},{9,17},{17,25},{25,1},{2,10},{10... | collective-permute-start | bytes 307208 | tf_op jit(solution)/shard_map/ppermute | solution.py:548
  73.1 90.5 %all-to-all-start.2 = ((bf16[32,402,128]{2,1,0:T(8,128)(2,1)}), bf16[32,402,128]{2,1,0:T(8,128)(2,1)S(1)}, u32[]{:S(2)}, u32[]{:S(2)}) async-start(bf16[32,402,128]{2,1,0:T(8,128)(2,1)} %order_slots.1), calls=%async_computation.2 | async-start | bytes 6684672 | tf_op jit(solution)/shard_map/all_to_all | solution.py:598
  81.8 5.6 %collective-permute-start.7 = (bf16[4,400,128]{2,1,0:T(8,128)(2,1)S(1)}, bf16[4,400,128]{2,1,0:T(8,128)(2,1)S(1)}, u32[]{:S(2)}, u32[]{:S(2)}) collective-permute-start(bf16[4,400,128]{2,1,0:T(8,128)(2,1)S(1)} %slice_bitcast_fusion), channel_id=1, source_target_pairs={{0,1},{1,0},{2,3},{3,2},{4,5},{5,4},{6,7},{7,6},{8,9},{9,8},{10,11... | collective-permute-start | bytes 1228808 | tf_op jit(solution)/shard_map/ppermute | solution.py:541
  83.8 37.5 %collective-permute-start.16 = (bf16[1,4,100,512]{3,2,1,0:T(8,128)(2,1)}, bf16[1,4,100,512]{3,2,1,0:T(8,128)(2,1)}, u32[]{:S(2)}, u32[]{:S(2)}) collective-permute-start(bf16[1,4,100,512]{3,2,1,0:T(8,128)(2,1)} %maximum_bitcast_fusion), channel_id=1, source_target_pairs={{0,6},{1,7},{2,4},{3,5},{4,2},{5,3},{6,0},{7,1},{8,14},{9,15},{10,... | collective-permute-start | bytes 1228808 | tf_op jit(solution)/shard_map/ppermute | solution.py:530
  86.3 40.5 %collective-permute-start.14 = (bf16[1,4,100,512]{3,2,1,0:T(8,128)(2,1)}, bf16[1,4,100,512]{3,2,1,0:T(8,128)(2,1)}, u32[]{:S(2)}, u32[]{:S(2)}) collective-permute-start(bf16[1,4,100,512]{3,2,1,0:T(8,128)(2,1)} %maximum_bitcast_fusion), channel_id=1, source_target_pairs={{0,4},{1,5},{2,6},{3,7},{4,0},{5,1},{6,2},{7,3},{8,12},{9,13},{10,... | collective-permute-start | bytes 1228808 | tf_op jit(solution)/shard_map/ppermute | solution.py:530
  86.8 45.4 %collective-permute-start.12 = (bf16[1,4,100,512]{3,2,1,0:T(8,128)(2,1)}, bf16[1,4,100,512]{3,2,1,0:T(8,128)(2,1)}, u32[]{:S(2)}, u32[]{:S(2)}) collective-permute-start(bf16[1,4,100,512]{3,2,1,0:T(8,128)(2,1)} %maximum_bitcast_fusion), channel_id=1, source_target_pairs={{0,2},{1,3},{2,0},{3,1},{4,6},{5,7},{6,4},{7,5},{8,10},{9,11},{10,... | collective-permute-start | bytes 1228808 | tf_op jit(solution)/shard_map/ppermute | solution.py:530
  88.5 67.4 %collective-permute-start.11 = (bf16[1,4,100,512]{3,2,1,0:T(8,128)(2,1)}, bf16[1,4,100,512]{3,2,1,0:T(8,128)(2,1)}, u32[]{:S(2)}, u32[]{:S(2)}) collective-permute-start(bf16[1,4,100,512]{3,2,1,0:T(8,128)(2,1)} %maximum_bitcast_fusion), channel_id=1, source_target_pairs={{0,1},{1,0},{2,3},{3,2},{4,5},{5,4},{6,7},{7,6},{8,9},{9,8},{10,11... | collective-permute-start | bytes 1228808 | tf_op jit(solution)/shard_map/ppermute | solution.py:530
  121.3 34.5 %collective-permute-start.17 = (bf16[1,4,100,512]{3,2,1,0:T(8,128)(2,1)}, bf16[1,4,100,512]{3,2,1,0:T(8,128)(2,1)}, u32[]{:S(2)}, u32[]{:S(2)}) collective-permute-start(bf16[1,4,100,512]{3,2,1,0:T(8,128)(2,1)} %collective-permute-done.16), channel_id=1, source_target_pairs={{0,1},{1,0},{2,3},{3,2},{4,5},{5,4},{6,7},{7,6},{8,9},{9,8},{10,11... | collective-permute-start | bytes 1228808 | tf_op jit(solution)/shard_map/ppermute | solution.py:530
  126.8 29.1 %collective-permute-start.15 = (bf16[1,4,100,512]{3,2,1,0:T(8,128)(2,1)}, bf16[1,4,100,512]{3,2,1,0:T(8,128)(2,1)}, u32[]{:S(2)}, u32[]{:S(2)}) collective-permute-start(bf16[1,4,100,512]{3,2,1,0:T(8,128)(2,1)} %collective-permute-done.14), channel_id=1, source_target_pairs={{0,1},{1,0},{2,3},{3,2},{4,5},{5,4},{6,7},{7,6},{8,9},{9,8},{10,11... | collective-permute-start | bytes 1228808 | tf_op jit(solution)/shard_map/ppermute | solution.py:530
  132.2 23.6 %collective-permute-start.13 = (bf16[1,4,100,512]{3,2,1,0:T(8,128)(2,1)}, bf16[1,4,100,512]{3,2,1,0:T(8,128)(2,1)}, u32[]{:S(2)}, u32[]{:S(2)}) collective-permute-start(bf16[1,4,100,512]{3,2,1,0:T(8,128)(2,1)} %collective-permute-done.12), channel_id=1, source_target_pairs={{0,1},{1,0},{2,3},{3,2},{4,5},{5,4},{6,7},{7,6},{8,9},{9,8},{10,11... | collective-permute-start | bytes 1228808 | tf_op jit(solution)/shard_map/ppermute | solution.py:530
  132.9 9.8 %collective-permute-start.10 = (bf16[1,400,128]{2,1,0:T(8,128)(2,1)S(1)}, bf16[1,400,128]{2,1,0:T(8,128)(2,1)S(1)}, u32[]{:S(2)}, u32[]{:S(2)}) collective-permute-start(bf16[1,400,128]{2,1,0:T(8,128)(2,1)S(1)} %get-tuple-element.193), channel_id=1, source_target_pairs={{0,6},{1,7},{2,4},{3,5},{4,2},{5,3},{6,0},{7,1},{8,14},{9,15},{10,... | collective-permute-start | bytes 307208 | tf_op jit(solution)/shard_map/ppermute | solution.py:541
  142.7 7.8 %copy-start.10 = (bf16[1,400,128]{2,1,0:T(8,128)(2,1)}, bf16[1,400,128]{2,1,0:T(8,128)(2,1)S(1)}, u32[]{:S(2)}) copy-start(bf16[1,400,128]{2,1,0:T(8,128)(2,1)S(1)} %collective-permute-done.10.refs_3_) | copy-start | bytes 307204
  142.8 7.8 %collective-permute-start.9 = (bf16[1,400,128]{2,1,0:T(8,128)(2,1)S(1)}, bf16[1,400,128]{2,1,0:T(8,128)(2,1)S(1)}, u32[]{:S(2)}, u32[]{:S(2)}) collective-permute-start(bf16[1,400,128]{2,1,0:T(8,128)(2,1)S(1)} %get-tuple-element.194), channel_id=1, source_target_pairs={{0,4},{1,5},{2,6},{3,7},{4,0},{5,1},{6,2},{7,3},{8,12},{9,13},{10,... | collective-permute-start | bytes 307208 | tf_op jit(solution)/shard_map/ppermute | solution.py:541
  150.5 0.6 copy-start.11
  151.2 4.7 %collective-permute-start.8 = (bf16[1,400,128]{2,1,0:T(8,128)(2,1)S(1)}, bf16[1,400,128]{2,1,0:T(8,128)(2,1)S(1)}, u32[]{:S(2)}, u32[]{:S(2)}) collective-permute-start(bf16[1,400,128]{2,1,0:T(8,128)(2,1)S(1)} %get-tuple-element.195), channel_id=1, source_target_pairs={{0,2},{1,3},{2,0},{3,1},{4,6},{5,7},{6,4},{7,5},{8,10},{9,11},{10,... | collective-permute-start | bytes 307208 | tf_op jit(solution)/shard_map/ppermute | solution.py:541
  155.8 0.6 copy-start.12
  163.5 1.7 copy-start.2

commit v3 on v2

--- a/solution.py
+++ b/solution.py
@@ -11,7 +11,6 @@
 F32, BF16, I32 = jnp.float32, jnp.bfloat16, jnp.int32
 LANES = 128
 PAD = 112
-VMEM_BYTES = 56 * 1024 * 1024
 
 
 def nt(a, b, **kw):
@@ -46,8 +45,8 @@
     return (both[0:tall] + both[tall:] + product(a_top, b_low))[0:rows]
 
 
-def params():
-    return pltpu.CompilerParams(vmem_limit_bytes=VMEM_BYTES)
+def params(mib=56):
+    return pltpu.CompilerParams(vmem_limit_bytes=mib * 1024 * 1024)
 
 
 def cost(flops, nbytes):
@@ -104,11 +103,20 @@
     return jnp.where(rows <= cols, 1.0, 0.0).astype(BF16)
 
 
-def relation_kernel(nrel, devices, plan, rel_ref, coef_ref, bases_ref, head_ref, tail_ref,
-                    picked_ref, vec_ref, gate_ref, tgrad_ref, place_ref, halves, acc):
+def up_to_here():
+    rows = lax.broadcasted_iota(I32, (LANES, LANES), 0)
+    cols = lax.broadcasted_iota(I32, (LANES, LANES), 1)
+    return jnp.where(rows <= cols, 1.0, 0.0).astype(BF16)
+
+
+def band(rows, slots):
+    bands = LANES // slots
+    return rows if bands == 1 else pl.cdiv(pl.cdiv(rows, bands), 16) * 16
+
+
+def pick_coef_kernel(nrel, rel_ref, coef_ref, picked_ref, halves, acc):
     step = pl.program_id(0)
-    width = coef_ref.shape[1]
-    nb = coef_ref.shape[0]
+    nb, width = coef_ref.shape
     lane = lax.broadcasted_iota(I32, (nb, width), 1) + step * width
     block = jnp.where(lane < nrel, coef_ref[...], 0.0)
     low = block - block.astype(BF16).astype(F32)
@@ -124,88 +132,103 @@
 
     @pl.when(step == pl.num_programs(0) - 1)
     def _():
-        picked = acc[0:nb] + acc[tall:tall + nb]
-        picked_ref[...] = picked
-        vec = precise(nn, bases_ref[...], picked)
-        vec_ref[...] = vec
-        head = head_ref[...].astype(F32)
-        head_vec = head * vec
-        score = jnp.sum(head_vec * tail_ref[...].astype(F32), axis=0, keepdims=True)
-        gate = jax.nn.sigmoid(-score)
-        gate_ref[...] = gate
-        tgrad_ref[...] = (-gate * head * vec).astype(BF16)
-        triples = rel_ref.shape[1]
-        upto = up_to_here()
-        number = lax.broadcasted_iota(I32, (devices, LANES), 0)
-        span, slots, room = plan
-        rel = rel_ref[...]
-        later = lax.broadcasted_iota(I32, (LANES, triples), 1)
-        row = lax.broadcasted_iota(I32, (LANES, triples), 0)
-        seen = jnp.zeros((1, triples), F32)
-        same = []
-        for b in range(triples // LANES):
-            down = jnp.broadcast_to(
-                rel[:, b * LANES:(b + 1) * LANES].astype(F32), (LANES, LANES)).T[:, 0:1]
-            equal = jnp.where(down.astype(I32) == rel, 1.0, 0.0)
-            same.append(equal.astype(BF16))
-            before = jnp.where(row + b * LANES < later, equal, 0.0)
-            seen = seen + jnp.sum(before, axis=0, keepdims=True)
-        first = jnp.where(seen == 0.0, 1.0, 0.0)
-        summer = rel // span
-        marks = []
-        for b in range(triples // LANES):
-            lanes = slice(b * LANES, (b + 1) * LANES)
-            marks.append(jnp.where(number == summer[:, lanes], first[:, lanes], 0.0))
-        sums = nn(jnp.concatenate(marks, axis=0).astype(BF16), upto)
-        carry = jnp.zeros((devices, 1), F32)
-        lead = []
-        for b, mark in enumerate(marks):
-            part = sums[b * devices:(b + 1) * devices]
-            lead.append(jnp.sum(mark * (part + carry - 1.0), axis=0, keepdims=True))
-            carry = carry + part[:, LANES - 1:LANES]
-        lead = jnp.minimum(jnp.concatenate(lead, axis=1), 255.0)
-        lead = jnp.broadcast_to(lead, (16, triples)).astype(BF16)
-        slot = nn(lead, jnp.concatenate(same, axis=0))[0:1].astype(I32)
-        fits = slot < room
-        place_ref[0:1] = jnp.where(fits, summer * slots + slot, -1)
-        place_ref[1:2] = jnp.where(seen == 0.0, rel - summer * span, -1)
-        over = jnp.max(jnp.where(fits, 0, 1), axis=1, keepdims=True)
-        place_ref[2:3] = jnp.broadcast_to(over, (1, triples))
-
-
-def relation_step(rel, coef_t, bases_t, head_t, tail_t, devices, plan):
+        picked_ref[...] = acc[0:nb] + acc[tall:tall + nb]
+
+
+def pick_coef(rel, coef_t):
     nb, nrel = coef_t.shape
-    cols, triples = head_t.shape
+    triples = rel.shape[1]
     width = 1920
-    steps = pl.cdiv(nrel, width)
     tall = pl.cdiv(nb, 8) * 8
-    whole = lambda shape: pl.BlockSpec(shape, lambda i: (0,) * len(shape))
-    outs = [((nb, triples), F32), ((cols, triples), F32), ((1, triples), F32),
-            ((cols, triples), BF16), ((3, triples), I32)]
-    return pl.pallas_call(
-        functools.partial(relation_kernel, nrel, devices, plan),
-        grid=(steps,),
+    return pl.pallas_call(
+        functools.partial(pick_coef_kernel, nrel),
+        grid=(pl.cdiv(nrel, width),),
         in_specs=[
-            whole((1, triples)),
+            pl.BlockSpec((1, triples), lambda i: (0, 0)),
             pl.BlockSpec((nb, width), lambda i: (0, i)),
-            whole((cols, nb)), whole((cols, triples)), whole((cols, triples)),
         ],
-        out_specs=[whole(s) for s, _ in outs],
-        out_shape=[jax.ShapeDtypeStruct(s, d) for s, d in outs],
+        out_specs=pl.BlockSpec((nb, triples), lambda i: (0, 0)),
+        out_shape=jax.ShapeDtypeStruct((nb, triples), F32),
         scratch_shapes=[pltpu.VMEM((2 * tall, width), BF16), pltpu.VMEM((2 * tall, triples), F32)],
         compiler_params=params(),
-        cost_estimate=cost(2 * 2 * PAD * nrel * triples, nb * nrel * 4),
-        name="relation_step",
-    )(rel, coef_t, bases_t, head_t, tail_t)
-
-
-def score_kernel(neg_count, negs_ref, vec_ref, head_ref, tail_ref, gate_ref, tgrad_ref, row_ref,
-                 bases_ref, picked_ref, grads_ref, rows_ref, base_ref, probs_ref, hrel_ref):
+        cost_estimate=cost(4 * tall * nrel * triples, nb * nrel * 4),
+        name="pick_coef",
+    )(rel, coef_t)
+
+
+def slot_of_relation(rel, devices, plan):
+    span, slots, room = plan
+    triples = rel.shape[1]
+    number = lax.broadcasted_iota(I32, (devices, LANES), 0)
+    later = lax.broadcasted_iota(I32, (LANES, triples), 1)
+    row = lax.broadcasted_iota(I32, (LANES, triples), 0)
+    seen = jnp.zeros((1, triples), F32)
+    same = []
+    for b in range(triples // LANES):
+        down = jnp.broadcast_to(
+            rel[:, b * LANES:(b + 1) * LANES].astype(F32), (LANES, LANES)).T[:, 0:1]
+        equal = jnp.where(down.astype(I32) == rel, 1.0, 0.0)
+        same.append(equal.astype(BF16))
+        before = jnp.where(row + b * LANES < later, equal, 0.0)
+        seen = seen + jnp.sum(before, axis=0, keepdims=True)
+    first = jnp.where(seen == 0.0, 1.0, 0.0)
+    summer = rel // span
+    marks = []
+    for b in range(triples // LANES):
+        lanes = slice(b * LANES, (b + 1) * LANES)
+        marks.append(jnp.where(number == summer[:, lanes], first[:, lanes], 0.0))
+    sums = nn(jnp.concatenate(marks, axis=0).astype(BF16), up_to_here())
+    carry = jnp.zeros((devices, 1), F32)
+    lead = []
+    for b, mark in enumerate(marks):
+        part = sums[b * devices:(b + 1) * devices]
+        lead.append(jnp.sum(mark * (part + carry - 1.0), axis=0, keepdims=True))
+        carry = carry + part[:, LANES - 1:LANES]
+    lead = jnp.minimum(jnp.concatenate(lead, axis=1), 255.0)
+    lead = jnp.broadcast_to(lead, (16, triples)).astype(BF16)
+    slot = nn(lead, jnp.concatenate(same, axis=0))[0:1].astype(I32)
+    fits = slot < room
+    place = jnp.where(fits, summer * slots + slot, -1)
+    local = jnp.where(seen == 0.0, rel - summer * span, -1)
+    over = jnp.max(jnp.where(fits, 0.0, 1.0), axis=1, keepdims=True)
+    return place, local, over
+
+
+def coef_blocks(rows, base, place, local, over, devices, plan, share):
+    span, slots, room = plan
+    nb = rows.shape[0]
+    cols = base.shape[1]
+    lanes = devices * slots
+
+    def halves(block):
+        spare = jnp.zeros((PAD - block.shape[0], block.shape[1]), F32)
+        return jnp.concatenate(split(jnp.concatenate([block, spare], axis=0)), axis=0)
+
+    high = local // 64
+    pair = jnp.concatenate([high, local - high * 64], axis=0)
+    pair = jnp.where(local >= 0, pair, 0).astype(F32)
+    both = nt(halves(jnp.concatenate([rows, pair], axis=0)), hits(place, lanes, 0))
+    column = lax.broadcasted_iota(I32, (1, cols), 1)
+    owner = column // share
+    spots = owner * slots + room + column - owner * share
+    both = both + nt(halves(base), hits(spots, lanes, 0))
+    row = lax.broadcasted_iota(I32, (PAD, lanes), 0)
+    return jnp.where(row == nb + 2, over, both[0:PAD] + both[PAD:])
+
+
+def score_kernel(neg_count, plan, share, rel_ref, picked_ref, negs_ref, head_ref, tail_ref,
+                 row_ref, bases_ref, send_ref, grads_ref, rows_ref, base_ref, probs_ref, hrel_ref):
     group, cols, per = negs_ref.shape
     triples = head_ref.shape[1]
-    vec = vec_ref[...]
+    devices, high, _ = send_ref.shape
+    slots = plan[1]
+    picked = picked_ref[...]
+    vec = precise(nn, bases_ref[...], picked)
     head = head_ref[...].astype(F32)
-    head_rel = (head * vec).astype(BF16)
+    tail = tail_ref[...].astype(F32)
+    head_vec = head * vec
+    gate = jax.nn.sigmoid(-jnp.sum(head_vec * tail, axis=0, keepdims=True))
+    head_rel = head_vec.astype(BF16)
     hrel_ref[...] = head_rel
     mix = jnp.zeros((cols, triples), F32)
     for first in range(0, group, 8):
@@ -213,42 +236,48 @@
         probs = jax.nn.sigmoid(tn(negs, head_rel)).astype(BF16)
         probs_ref[first * per:(first + 8) * per] = probs
         mix = mix + nn(negs, probs)
-    tail = tail_ref[...].astype(F32)
-    gate = gate_ref[...]
     rel_grad = -gate * head * tail + head * mix / neg_count
-    rows_ref[...] = precise(nn, bases_ref[...].T, rel_grad)
-    base_ref[...] = precise(nt, picked_ref[...], rel_grad)
+    rows = precise(nn, bases_ref[...].T, rel_grad)
+    base = precise(nt, picked, rel_grad)
+    rows_ref[...] = rows
+    base_ref[...] = base
+    place, local, over = slot_of_relation(rel_ref[...], devices, plan)
+    both = coef_blocks(rows, base, place, local, over, devices, plan, share)
+    bands = LANES // slots
+    if bands * high > PAD:
+        spare = jnp.zeros((bands * high - PAD, both.shape[1]), F32)
+        both = jnp.concatenate([both, spare], axis=0)
+    for o in range(devices):
+        block = [both[b * high:(b + 1) * high, o * slots:(o + 1) * slots] for b in range(bands)]
+        send_ref[o] = jnp.concatenate(block, axis=1).astype(BF16)
     grads_ref[0:cols, 0:triples] = (-gate * vec * tail + vec * mix / neg_count).astype(BF16)
-    grads_ref[0:cols, triples:] = tgrad_ref[...]
+    grads_ref[0:cols, triples:] = (-gate * head * vec).astype(BF16)
     for side in range(2):
         ids = row_ref[side:side + 1]
         lanes = slice(side * triples, (side + 1) * triples)
-        high = ids // 64
-        pair = jnp.concatenate([high, ids - high * 64], axis=0).astype(F32)
+        upper = ids // 64
+        pair = jnp.concatenate([upper, ids - upper * 64], axis=0).astype(F32)
         more = grads_ref.shape[0] - cols - 2
         if more:
             pair = jnp.concatenate([pair, jnp.zeros((more, triples), F32)], axis=0)
         grads_ref[cols:, lanes] = pair.astype(BF16)
 
 
-def score_step(negs, vec, head_t, tail_t, gate, tgrad, rows, bases_t, picked, tall, neg_count):
+def score_step(rel, picked, negs, head_t, tail_t, rows, bases_t, tall, neg_count, devices, plan,
+               share):
     group, cols, per = negs.shape
     triples = head_t.shape[1]
     nb = bases_t.shape[1]
-    outs = [((tall, 2 * triples), BF16), ((nb, triples), F32), ((nb, cols), F32),
-            ((group * per, triples), BF16), ((cols, triples), BF16)]
-    return pl.pallas_call(
-        functools.partial(score_kernel, neg_count),
+    high = pl.cdiv(PAD * plan[1], 8 * LANES) * 8
+    outs = [((devices, high, LANES), BF16), ((tall, 2 * triples), BF16), ((nb, triples), F32),
+            ((nb, cols), F32), ((group * per, triples), BF16), ((cols, triples), BF16)]
+    return pl.pallas_call(
+        functools.partial(score_kernel, neg_count, plan, share),
         out_shape=[jax.ShapeDtypeStruct(s, d) for s, d in outs],
         compiler_params=params(),
         cost_estimate=cost(2 * cols * triples * 2 * group * per, 16 << 20),
         name="score_step",
-    )(negs, vec, head_t, tail_t, gate, tgrad, rows, bases_t, picked)
-
-
-def band(rows, slots):
-    bands = LANES // slots
-    return rows if bands == 1 else pl.cdiv(pl.cdiv(rows, bands), 16) * 16
+    )(rel, picked, negs, head_t, tail_t, rows, bases_t)
 
 
 def order_kernel(devices, slots, grads_ref, owner_ref, send_ref, pos):
@@ -328,52 +357,6 @@
         cost_estimate=cost(1, 1),
         name="partial_step",
     )(me, probs, hrel)
-
-
-def coef_order_kernel(plan, share, rows_ref, base_ref, place_ref, send_ref):
-    span, slots, room = plan
-    devices, high, _ = send_ref.shape
-    nb, triples = rows_ref.shape
-    cols = base_ref.shape[1]
-    lanes = devices * slots
-
-    def halves(block):
-        spare = jnp.zeros((PAD - block.shape[0], block.shape[1]), F32)
-        block = jnp.concatenate([block, spare], axis=0)
-        top = block.astype(BF16)
-        return jnp.concatenate([top, (block - top.astype(F32)).astype(BF16)], axis=0)
-
-    local = place_ref[1:2]
-    lead = local >= 0
-    high_id = local // 64
-    pair = jnp.concatenate([high_id, local - high_id * 64], axis=0)
-    pair = jnp.where(lead, pair, 0).astype(F32)
-    left = halves(jnp.concatenate([rows_ref[...], pair], axis=0))
-    both = nt(left, hits(place_ref[0:1], lanes, 0))
-    column = lax.broadcasted_iota(I32, (1, cols), 1)
-    owner = column // share
-    spots = owner * slots + room + column - owner * share
-    both = both + nt(halves(base_ref[...]), hits(spots, lanes, 0))
-    both = both[0:PAD] + both[PAD:]
-    row = lax.broadcasted_iota(I32, (PAD, lanes), 0)
-    both = jnp.where(row == nb + 2, place_ref[2:3, 0:1].astype(F32), both)
-    bands = LANES // slots
-    if bands * high > PAD:
-        both = jnp.concatenate([both, jnp.zeros((bands * high - PAD, lanes), F32)], axis=0)
-    for o in range(devices):
-        block = [both[b * high:(b + 1) * high, o * slots:(o + 1) * slots] for b in range(bands)]
-        send_ref[o] = jnp.concatenate(block, axis=1).astype(BF16)
-
-
-def coef_order(rows, base, place, devices, plan, share):
-    high = pl.cdiv(PAD * plan[1], 8 * LANES) * 8
-    return pl.pallas_call(
-        functools.partial(coef_order_kernel, plan, share),
-        out_shape=jax.ShapeDtypeStruct((devices, high, LANES), BF16),
-        compiler_params=params(),
-        cost_estimate=cost(1, 1),
-        name="coef_order",
-    )(rows, base, place)
 
 
 def coef_sum_kernel(nb, plan, recv_ref, out_ref, flag_ref, left):
@@ -406,7 +389,7 @@
         functools.partial(coef_sum_kernel, nb, plan),
         out_shape=[jax.ShapeDtypeStruct((nb, width), BF16), jax.ShapeDtypeStruct((1, LANES), I32)],
         scratch_shapes=[pltpu.VMEM((PAD, sources * slots), BF16)],
-        compiler_params=params(),
+        compiler_params=params(20),
         cost_estimate=cost(1, 1),
         name="coef_sum",
     )(recv)
@@ -507,7 +490,7 @@
     width = 1024
     lanes = sources * slots + 2 * LANES
     whole = lambda shape: pl.BlockSpec(shape, lambda i: (0,) * len(shape))
-    there = pl.BlockSpec(memory_space=pltpu.HBM) if bands == 1 else whole(recv.shape)
+    there = pl.BlockSpec(memory_space=pl.ANY) if bands == 1 else whole(recv.shape)
     return pl.pallas_call(
         functools.partial(add_rows_kernel, slots),
         grid=(ent // width,),
@@ -517,7 +500,7 @@
         scratch_shapes=[pltpu.VMEM((bands * high, lanes), BF16),
                         pltpu.VMEM((1, lanes), I32),
                         pltpu.SemaphoreType.DMA((sources,))],
-        compiler_params=params(),
+        compiler_params=params(32),
         cost_estimate=cost(1, 1),
         name="add_rows",
     )(recv, neg_ids, *part_sets)
@@ -584,11 +567,9 @@
 
     sent_negs = pick_negs(neg_rows, entities.T, group)
     negs = lax.all_to_all(sent_negs, "dev", 0, 0, tiled=True)
-    picked, vec, gate, tgrad, place = relation_step(
-        rel, coef_t, bases_t, head_t, tail_t, devices, plan)
-    grads, rows, base, probs, hrel = score_step(
-        negs, vec, head_t, tail_t, gate, tgrad, row_t, bases_t, picked, tall, neg_count)
-    coef_send = coef_order(rows, base, place, devices, plan, share)
+    picked = pick_coef(rel, coef_t)
+    coef_send, grads, rows, base, probs, hrel = score_step(
+        rel, picked, negs, head_t, tail_t, row_t, bases_t, tall, neg_count, devices, plan, share)
     coef_recv = lax.all_to_all(coef_send, ("grp", "dev"), 0, 0, tiled=True)
     send = order_slots(grads, owner_t, devices, cap, cols + 2)
     send, coef_recv = lax.optimization_barrier((send, coef_recv))

time: 186 us -> 176 us (0.946)
  Pallas kernels: 75.3 us -> 67.8 us
  local copies, waits for them, and re-layouts: 7.12 us -> 4.78 us
    pallas_call x3 -> x2, Pallas kernels: 26.8 us -> 22.4 us  [the longest x1 12.2 us: pick_coef(): pl.pallas_call(functools.partial(pick_coef_kernel, nrel), grid=(pl.cdiv(n...]
    unnamed x22 -> x16, local copies, waits for them, and re-layouts: 5.43 us -> 3.08 us
  transfers between devices with their start and end apart: 17 -> 17, of which waited for: 10 -> 11; matrix products, arithmetic and copies ran while one was open for 3% -> 3% of each run, Pallas kernels for 20% -> 19%
where the time goes in v3:
time: 176 us; the launch traced here: 175 us
  waiting for transfers between devices  67.9 us (39%)
  Pallas kernels  67.8 us (39%)
  starting transfers between devices  30.4 us (17%)
  local copies, waits for them, and re-layouts  4.78 us (3%)
  other arithmetic  3.55 us (2%)
    ppermute x7, waiting for transfers between devices, from_group(): lax.ppermute(x, 'dev', [(i, i ^ far) for i in range(group)])  43.7 us
    pallas_call x1, Pallas kernels, add_rows(): pl.pallas_call(functools.partial(add_rows_kernel, slots), grid=(ent // wi...  18.3 us
    ppermute x4, waiting for transfers between devices, sum_here(): lax.ppermute(x, 'dev', [(i, i ^ far) for i in range(group)])  13.9 us
    pallas_call x1, Pallas kernels, pick_coef(): pl.pallas_call(functools.partial(pick_coef_kernel, nrel), grid=(pl.cdiv(n...  12.2 us
    pallas_call x1, Pallas kernels, order_slots(): pl.pallas_call(functools.partial(order_kernel, devices, slots), grid=(dev...  11.3 us
    pallas_call x1, Pallas kernels, score_step(): pl.pallas_call(functools.partial(score_kernel, neg_count, plan, share), o...  10.2 us
    ppermute x3, waiting for transfers between devices, shift_layers(): lax.ppermute(block, 'grp', [(i, (i + far) % layers) for i in range(layers)])  8.88 us
    ppermute x4, starting transfers between devices, sum_here(): lax.ppermute(x, 'dev', [(i, i ^ far) for i in range(group)])  8.86 us
  transfers between devices with their start and end apart: 17, of which 11 were waited for; matrix products, arithmetic and copies ran while one was open for 3% of the time, Pallas kernels for 19%

profile of v3, /device:TPU:16, one launch (start us, length us, event | category | flops | bytes accessed | tf_op | source)
XLA Modules:
  0.0 175.4 jit_solution(3553324633921396450)
XLA Ops:
  0.6 4.5 %pick_negs.1 = bf16[8,400,128]{2,1,0:T(8,128)(2,1)} custom-call(s32[1,128]{1,0:T(1,128)} %neg_ref.1, bf16[400,4096]{1,0:T(8,128)(2,1)} %bitcast.41), custom_call_target="tpu_custom_call" | custom-call | flops 419430400 | bytes 3276800 | tf_op jit(solution)/shard_map/pick_negs/pallas_call | solution.py:84
  5.2 3.7 %all-to-all-start = ((bf16[8,400,128]{2,1,0:T(8,128)(2,1)}), bf16[8,400,128]{2,1,0:T(8,128)(2,1)S(1)}, u32[]{:S(2)}, u32[]{:S(2)}) async-start(bf16[8,400,128]{2,1,0:T(8,128)(2,1)} %pick_negs.1), calls=%async_computation | async-start | bytes 1638400 | tf_op jit(solution)/shard_map/all_to_all | solution.py:569
  8.9 12.2 %pick_coef.1.picked_ref = f32[100,1024]{1,0:T(8,128)} custom-call(s32[1,1024]{1,0:T(1,128)} %bitcast.47, f32[100,14824]{1,0:T(8,128)} %bitcast.49), custom_call_target="tpu_custom_call" | custom-call | flops 6314786816 | bytes 5929600 | tf_op jit(solution)/shard_map/pick_coef/pallas_call | solution.py:143
  21.8 0.9 copy-done.5
  22.7 10.2 %score_step.1 = (bf16[32,56,128]{2,1,0:T(8,128)(2,1)}, bf16[402,2048]{1,0:T(8,128)(2,1)}, f32[100,1024]{1,0:T(8,128)}, f32[100,400]{1,0:T(8,128)}, bf16[1024,102...) custom-call(s32[1,1024]{1,0:T(1,128)S(1)} %bitcast.48, f32[100,1024]{1,0:T(8,128)} %pick_coef.1.picked_ref, ...), custom_call_target="tpu_custom_call" | custom-call | flops 1677721600 | bytes 16777216 | tf_op jit(solution)/shard_map/score_step/pallas_call | solution.py:274
  33.0 5.6 %all-to-all-start.1 = ((bf16[32,56,128]{2,1,0:T(8,128)(2,1)}), bf16[32,56,128]{2,1,0:T(8,128)(2,1)S(1)}, u32[]{:S(2)}, u32[]{:S(2)}) async-start(bf16[32,56,128]{2,1,0:T(8,128)(2,1)} %get-tuple-element.129), calls=%async_computation.1 | async-start | bytes 917504 | tf_op jit(solution)/shard_map/all_to_all | solution.py:573
  38.6 11.3 %order_slots.1 = bf16[32,402,128]{2,1,0:T(8,128)(2,1)} custom-call(bf16[402,2048]{1,0:T(8,128)(2,1)} %get-tuple-element.128.grads_ref, s32[2,1024]{1,0:T(2,128)} %bitcast.54), custom_call_target="tpu_custom_call" | custom-call | flops 6744440832 | bytes 4194304 | tf_op jit(solution)/shard_map/order_slots/pallas_call | solution.py:319
  50.5 0.9 coef_sum.1
  51.4 2.5 %collective-permute-start.6 = (bf16[100,512]{1,0:T(8,128)(2,1)S(1)}, bf16[100,512]{1,0:T(8,128)(2,1)S(1)}, u32[]{:S(2)}, u32[]{:S(2)}) collective-permute-start(bf16[100,512]{1,0:T(8,128)(2,1)S(1)} %get-tuple-element.136), channel_id=1, source_target_pairs={{0,24},{8,0},{16,8},{24,16},{1,25},{9,1},{17,9},{25,17},{2,26},{10... | collective-permute-start | bytes 307208 | tf_op jit(solution)/shard_map/ppermute | solution.py:531
  53.9 1.4 collective-permute-start.5
  55.3 0.9 collective-permute-start.4
  56.2 5.2 %collective-permute-done.6 = bf16[100,512]{1,0:T(8,128)(2,1)S(1)} collective-permute-done((bf16[100,512]{1,0:T(8,128)(2,1)S(1)}, bf16[100,512]{1,0:T(8,128)(2,1)S(1)}, u32[]{:S(2)}, u32[]{:S(2)}) %collective-permute-start.6) | collective-permute-done | bytes 102432 | tf_op jit(solution)/shard_map/ppermute | solution.py:531
  61.4 1.6 collective-permute-done.5
  62.9 2.1 %collective-permute-done.4 = bf16[100,512]{1,0:T(8,128)(2,1)S(1)} collective-permute-done((bf16[100,512]{1,0:T(8,128)(2,1)S(1)}, bf16[100,512]{1,0:T(8,128)(2,1)S(1)}, u32[]{:S(2)}, u32[]{:S(2)}) %collective-permute-start.4) | collective-permute-done | bytes 102432 | tf_op jit(solution)/shard_map/ppermute | solution.py:531
  65.7 3.8 %all-to-all-start.2 = ((bf16[32,402,128]{2,1,0:T(8,128)(2,1)}), bf16[32,402,128]{2,1,0:T(8,128)(2,1)S(1)}, u32[]{:S(2)}, u32[]{:S(2)}) async-start(bf16[32,402,128]{2,1,0:T(8,128)(2,1)} %order_slots.1), calls=%async_computation.2 | async-start | bytes 6684672 | tf_op jit(solution)/shard_map/all_to_all | solution.py:579
  69.5 3.9 %partial_step.1 = bf16[2,4,400,128]{3,2,1,0:T(8,128)(2,1)} custom-call(s32[1]{0:T(128)} %bitcast.11.me_ref, bf16[1024,1024]{1,0:T(8,128)(2,1)} %get-tuple-element.134.probs_ref, bf16[400,1024]{1,0:T(8,128)(2,1)} %get-tuple-element.135.hrel_ref), custom_call_target="tpu_custom_call" | custom-call | flops 1 | bytes 1 | tf_op jit(solution)/shard_map/partial_step/pallas_call | solution.py:346
  73.5 1.0 slice_bitcast_fusion
  74.7 1.8 %maximum_bitcast_fusion = bf16[1,4,100,512]{3,2,1,0:T(8,128)(2,1)} fusion(bf16[1,100,512]{2,1,0:T(8,128)(2,1)} %bitcast.44, bf16[1,100,512]{2,1,0:T(8,128)(2,1)} %bitcast.45, bf16[1,100,512]{2,1,0:T(8,128)(2,1)} %bitcast.46, bf16[1,100,512]{2,1,0:T(8,128)(2,1)S(1)} %bitcast.32), kind=kLoop, calls=%fused_computation.8 | loop fusion | flops 614400 | bytes 819200 | tf_op jit(solution)/shard_map/broadcast_in_dim | solution.py:510
  76.5 2.4 %collective-permute-start.16 = (bf16[1,4,100,512]{3,2,1,0:T(8,128)(2,1)}, bf16[1,4,100,512]{3,2,1,0:T(8,128)(2,1)}, u32[]{:S(2)}, u32[]{:S(2)}) collective-permute-start(bf16[1,4,100,512]{3,2,1,0:T(8,128)(2,1)} %maximum_bitcast_fusion), channel_id=1, source_target_pairs={{0,6},{1,7},{2,4},{3,5},{4,2},{5,3},{6,0},{7,1},{8,14},{9,15},{10,... | collective-permute-start | bytes 1228808 | tf_op jit(solution)/shard_map/ppermute | solution.py:513
  80.0 1.1 fusion.3
  81.3 32.8 %collective-permute-done.16 = bf16[1,4,100,512]{3,2,1,0:T(8,128)(2,1)} collective-permute-done((bf16[1,4,100,512]{3,2,1,0:T(8,128)(2,1)}, bf16[1,4,100,512]{3,2,1,0:T(8,128)(2,1)}, u32[]{:S(2)}, u32[]{:S(2)}) %collective-permute-start.16) | collective-permute-done | bytes 409632 | tf_op jit(solution)/shard_map/ppermute | solution.py:513
  114.0 5.4 %collective-permute-done.14 = bf16[1,4,100,512]{3,2,1,0:T(8,128)(2,1)} collective-permute-done((bf16[1,4,100,512]{3,2,1,0:T(8,128)(2,1)}, bf16[1,4,100,512]{3,2,1,0:T(8,128)(2,1)}, u32[]{:S(2)}, u32[]{:S(2)}) %collective-permute-start.14) | collective-permute-done | bytes 409632 | tf_op jit(solution)/shard_map/ppermute | solution.py:513
  119.5 5.5 %collective-permute-done.12 = bf16[1,4,100,512]{3,2,1,0:T(8,128)(2,1)} collective-permute-done((bf16[1,4,100,512]{3,2,1,0:T(8,128)(2,1)}, bf16[1,4,100,512]{3,2,1,0:T(8,128)(2,1)}, u32[]{:S(2)}, u32[]{:S(2)}) %collective-permute-start.12) | collective-permute-done | bytes 409632 | tf_op jit(solution)/shard_map/ppermute | solution.py:513
  125.6 5.1 %collective-permute-start.10 = (bf16[1,400,128]{2,1,0:T(8,128)(2,1)S(1)}, bf16[1,400,128]{2,1,0:T(8,128)(2,1)S(1)}, u32[]{:S(2)}, u32[]{:S(2)}) collective-permute-start(bf16[1,400,128]{2,1,0:T(8,128)(2,1)S(1)} %get-tuple-element.185), channel_id=1, source_target_pairs={{0,6},{1,7},{2,4},{3,5},{4,2},{5,3},{6,0},{7,1},{8,14},{9,15},{10,... | collective-permute-start | bytes 307208 | tf_op jit(solution)/shard_map/ppermute | solution.py:524
  130.8 4.7 %collective-permute-done.10.refs_3_ = bf16[1,400,128]{2,1,0:T(8,128)(2,1)S(1)} collective-permute-done((bf16[1,400,128]{2,1,0:T(8,128)(2,1)S(1)}, bf16[1,400,128]{2,1,0:T(8,128)(2,1)S(1)}, u32[]{:S(2)}, u32[]{:S(2)}) %collective-permute-start.10) | collective-permute-done | bytes 102432 | tf_op jit(solution)/shard_map/ppermute | solution.py:524
  135.4 3.3 %collective-permute-start.9 = (bf16[1,400,128]{2,1,0:T(8,128)(2,1)S(1)}, bf16[1,400,128]{2,1,0:T(8,128)(2,1)S(1)}, u32[]{:S(2)}, u32[]{:S(2)}) collective-permute-start(bf16[1,400,128]{2,1,0:T(8,128)(2,1)S(1)} %get-tuple-element.186), channel_id=1, source_target_pairs={{0,4},{1,5},{2,6},{3,7},{4,0},{5,1},{6,2},{7,3},{8,12},{9,13},{10,... | collective-permute-start | bytes 307208 | tf_op jit(solution)/shard_map/ppermute | solution.py:524
  138.7 4.5 %collective-permute-done.9.refs_2_ = bf16[1,400,128]{2,1,0:T(8,128)(2,1)S(1)} collective-permute-done((bf16[1,400,128]{2,1,0:T(8,128)(2,1)S(1)}, bf16[1,400,128]{2,1,0:T(8,128)(2,1)S(1)}, u32[]{:S(2)}, u32[]{:S(2)}) %collective-permute-start.9) | collective-permute-done | bytes 102432 | tf_op jit(solution)/shard_map/ppermute | solution.py:524
  144.2 4.7 %collective-permute-done.8.refs_1_ = bf16[1,400,128]{2,1,0:T(8,128)(2,1)} collective-permute-done((bf16[1,400,128]{2,1,0:T(8,128)(2,1)}, bf16[1,400,128]{2,1,0:T(8,128)(2,1)}, u32[]{:S(2)}, u32[]{:S(2)}) %collective-permute-start.8) | collective-permute-done | bytes 102432 | tf_op jit(solution)/shard_map/ppermute | solution.py:524
  148.9 7.1 %conditional.1 = ((f32[100,14824]{1,0:T(8,128)}, f32[400,100]{1,0:T(8,128)})) conditional(s32[]{:T(128)} %bitcast.20, (s32[1024]{0:T(1024)S(1)}, f32[100,1024]{1,0:T(8,128)}, f32[100,400]{1,0:T(8,128)}) %tuple.64, (s32[]{:T(128)}, s32[1]{0:T(128)}, bf16[1,4,100,512]{3,2,1,0:T(8,128)(2,1)}, bf16[1,4,100,512]{3,2,1,0:T(8,128)(2,1)}, ...), branch_computations={%region_0.0_spmd, %region_6.0_spmd} | conditional | flops 3150276 | bytes 237930176 | solution.py:594
  149.5 6.5 %spread.1 = (f32[100,14824]{1,0:T(8,128)}, f32[400,100]{1,0:T(8,128)}) custom-call(s32[2]{0:T(128)} %pad_add_fusion.place_ref, bf16[1,4,100,512]{3,2,1,0:T(8,128)(2,1)} %get-tuple-element.88.refs_0_, bf16[1,4,100,512]{3,2,1,0:T(8,128)(2,1)} %get-tuple-element.89.refs_1_, bf16[1,4,100,512]{3,2,1,0:T(8,128)(2,1)} %get-tuple-element.90.refs_2_, ...), custom_call_target="tpu_custom_call" | custom-call | flops 1 | bytes 1 | tf_op jit(solution)/shard_map/cond/branch_1_fun/spread/pallas_call | solution.py:427
  156.0 0.9 copy-done.1
  156.9 18.3 %add_rows.1 = f32[400,4096]{1,0:T(8,128)} custom-call(bf16[32,402,128]{2,1,0:T(8,128)(2,1)S(1)} %all-to-all-done.2.recv_ref, s32[1,128]{1,0:T(1,128)S(1)} %copy-done.2, bf16[1,400,128]{2,1,0:T(8,128)(2,1)S(1)} %get-tuple-element.140.refs_0_, bf16[1,400,128]{2,1,0:T(8,128)(2,1)} %collective-permute-done.8.refs_1_, bf16[1,400,128]{2,1,0:T(8,128)(2,1)S(1)} %copy-done.1, ...), custom_call_target="tpu_custom_call" | custom-call | flops 1 | bytes 1 | tf_op jit(solution)/shard_map/add_rows/pallas_call | solution.py:494
  (32 shorter events, 5.6 us)
Async XLA Ops:
  5.2 16.7 %all-to-all-start = ((bf16[8,400,128]{2,1,0:T(8,128)(2,1)}), bf16[8,400,128]{2,1,0:T(8,128)(2,1)S(1)}, u32[]{:S(2)}, u32[]{:S(2)}) async-start(bf16[8,400,128]{2,1,0:T(8,128)(2,1)} %pick_negs.1), calls=%async_computation | async-start | bytes 1638400 | tf_op jit(solution)/shard_map/all_to_all | solution.py:569
  8.9 13.9 %copy-start.9 = (s32[1024]{0:T(1024)S(1)}, s32[1024]{0:T(1024)}, u32[]{:S(2)}) copy-start(s32[1024]{0:T(1024)} %param.17) | copy-start | bytes 12292
  21.8 0.9 copy-start.5
  33.0 17.5 %all-to-all-start.1 = ((bf16[32,56,128]{2,1,0:T(8,128)(2,1)}), bf16[32,56,128]{2,1,0:T(8,128)(2,1)S(1)}, u32[]{:S(2)}, u32[]{:S(2)}) async-start(bf16[32,56,128]{2,1,0:T(8,128)(2,1)} %get-tuple-element.129), calls=%async_computation.1 | async-start | bytes 917504 | tf_op jit(solution)/shard_map/all_to_all | solution.py:573
  51.4 10.0 %collective-permute-start.6 = (bf16[100,512]{1,0:T(8,128)(2,1)S(1)}, bf16[100,512]{1,0:T(8,128)(2,1)S(1)}, u32[]{:S(2)}, u32[]{:S(2)}) collective-permute-start(bf16[100,512]{1,0:T(8,128)(2,1)S(1)} %get-tuple-element.136), channel_id=1, source_target_pairs={{0,24},{8,0},{16,8},{24,16},{1,25},{9,1},{17,9},{25,17},{2,26},{10... | collective-permute-start | bytes 307208 | tf_op jit(solution)/shard_map/ppermute | solution.py:531
  53.9 9.1 %collective-permute-start.5 = (bf16[100,512]{1,0:T(8,128)(2,1)S(1)}, bf16[100,512]{1,0:T(8,128)(2,1)S(1)}, u32[]{:S(2)}, u32[]{:S(2)}) collective-permute-start(bf16[100,512]{1,0:T(8,128)(2,1)S(1)} %get-tuple-element.136), channel_id=1, source_target_pairs={{0,16},{8,24},{16,0},{24,8},{1,17},{9,25},{17,1},{25,9},{2,18},{10... | collective-permute-start | bytes 307208 | tf_op jit(solution)/shard_map/ppermute | solution.py:531
  55.3 9.8 %collective-permute-start.4 = (bf16[100,512]{1,0:T(8,128)(2,1)S(1)}, bf16[100,512]{1,0:T(8,128)(2,1)S(1)}, u32[]{:S(2)}, u32[]{:S(2)}) collective-permute-start(bf16[100,512]{1,0:T(8,128)(2,1)S(1)} %get-tuple-element.136), channel_id=1, source_target_pairs={{0,8},{8,16},{16,24},{24,0},{1,9},{9,17},{17,25},{25,1},{2,10},{10... | collective-permute-start | bytes 307208 | tf_op jit(solution)/shard_map/ppermute | solution.py:531
  61.4 3.7 %copy-start.6 = (bf16[100,512]{1,0:T(8,128)(2,1)}, bf16[100,512]{1,0:T(8,128)(2,1)S(1)}, u32[]{:S(2)}) copy-start(bf16[100,512]{1,0:T(8,128)(2,1)S(1)} %collective-permute-done.6) | copy-start | bytes 307204
  62.9 2.1 %copy-start.7 = (bf16[100,512]{1,0:T(8,128)(2,1)}, bf16[100,512]{1,0:T(8,128)(2,1)S(1)}, u32[]{:S(2)}) copy-start(bf16[100,512]{1,0:T(8,128)(2,1)S(1)} %collective-permute-done.5) | copy-start | bytes 307204
  65.1 0.6 copy-start.8
  65.7 90.3 %all-to-all-start.2 = ((bf16[32,402,128]{2,1,0:T(8,128)(2,1)}), bf16[32,402,128]{2,1,0:T(8,128)(2,1)S(1)}, u32[]{:S(2)}, u32[]{:S(2)}) async-start(bf16[32,402,128]{2,1,0:T(8,128)(2,1)} %order_slots.1), calls=%async_computation.2 | async-start | bytes 6684672 | tf_op jit(solution)/shard_map/all_to_all | solution.py:579
  74.5 5.6 %collective-permute-start.7 = (bf16[4,400,128]{2,1,0:T(8,128)(2,1)S(1)}, bf16[4,400,128]{2,1,0:T(8,128)(2,1)S(1)}, u32[]{:S(2)}, u32[]{:S(2)}) collective-permute-start(bf16[4,400,128]{2,1,0:T(8,128)(2,1)S(1)} %slice_bitcast_fusion), channel_id=1, source_target_pairs={{0,1},{1,0},{2,3},{3,2},{4,5},{5,4},{6,7},{7,6},{8,9},{9,8},{10,11... | collective-permute-start | bytes 1228808 | tf_op jit(solution)/shard_map/ppermute | solution.py:524
  76.5 37.5 %collective-permute-start.16 = (bf16[1,4,100,512]{3,2,1,0:T(8,128)(2,1)}, bf16[1,4,100,512]{3,2,1,0:T(8,128)(2,1)}, u32[]{:S(2)}, u32[]{:S(2)}) collective-permute-start(bf16[1,4,100,512]{3,2,1,0:T(8,128)(2,1)} %maximum_bitcast_fusion), channel_id=1, source_target_pairs={{0,6},{1,7},{2,4},{3,5},{4,2},{5,3},{6,0},{7,1},{8,14},{9,15},{10,... | collective-permute-start | bytes 1228808 | tf_op jit(solution)/shard_map/ppermute | solution.py:513
  79.0 40.5 %collective-permute-start.14 = (bf16[1,4,100,512]{3,2,1,0:T(8,128)(2,1)}, bf16[1,4,100,512]{3,2,1,0:T(8,128)(2,1)}, u32[]{:S(2)}, u32[]{:S(2)}) collective-permute-start(bf16[1,4,100,512]{3,2,1,0:T(8,128)(2,1)} %maximum_bitcast_fusion), channel_id=1, source_target_pairs={{0,4},{1,5},{2,6},{3,7},{4,0},{5,1},{6,2},{7,3},{8,12},{9,13},{10,... | collective-permute-start | bytes 1228808 | tf_op jit(solution)/shard_map/ppermute | solution.py:513
  79.5 45.5 %collective-permute-start.12 = (bf16[1,4,100,512]{3,2,1,0:T(8,128)(2,1)}, bf16[1,4,100,512]{3,2,1,0:T(8,128)(2,1)}, u32[]{:S(2)}, u32[]{:S(2)}) collective-permute-start(bf16[1,4,100,512]{3,2,1,0:T(8,128)(2,1)} %maximum_bitcast_fusion), channel_id=1, source_target_pairs={{0,2},{1,3},{2,0},{3,1},{4,6},{5,7},{6,4},{7,5},{8,10},{9,11},{10,... | collective-permute-start | bytes 1228808 | tf_op jit(solution)/shard_map/ppermute | solution.py:513
  81.2 67.7 %collective-permute-start.11 = (bf16[1,4,100,512]{3,2,1,0:T(8,128)(2,1)}, bf16[1,4,100,512]{3,2,1,0:T(8,128)(2,1)}, u32[]{:S(2)}, u32[]{:S(2)}) collective-permute-start(bf16[1,4,100,512]{3,2,1,0:T(8,128)(2,1)} %maximum_bitcast_fusion), channel_id=1, source_target_pairs={{0,1},{1,0},{2,3},{3,2},{4,5},{5,4},{6,7},{7,6},{8,9},{9,8},{10,11... | collective-permute-start | bytes 1228808 | tf_op jit(solution)/shard_map/ppermute | solution.py:513
  114.0 34.8 %collective-permute-start.17 = (bf16[1,4,100,512]{3,2,1,0:T(8,128)(2,1)}, bf16[1,4,100,512]{3,2,1,0:T(8,128)(2,1)}, u32[]{:S(2)}, u32[]{:S(2)}) collective-permute-start(bf16[1,4,100,512]{3,2,1,0:T(8,128)(2,1)} %collective-permute-done.16), channel_id=1, source_target_pairs={{0,1},{1,0},{2,3},{3,2},{4,5},{5,4},{6,7},{7,6},{8,9},{9,8},{10,11... | collective-permute-start | bytes 1228808 | tf_op jit(solution)/shard_map/ppermute | solution.py:513
  119.4 29.4 %collective-permute-start.15 = (bf16[1,4,100,512]{3,2,1,0:T(8,128)(2,1)}, bf16[1,4,100,512]{3,2,1,0:T(8,128)(2,1)}, u32[]{:S(2)}, u32[]{:S(2)}) collective-permute-start(bf16[1,4,100,512]{3,2,1,0:T(8,128)(2,1)} %collective-permute-done.14), channel_id=1, source_target_pairs={{0,1},{1,0},{2,3},{3,2},{4,5},{5,4},{6,7},{7,6},{8,9},{9,8},{10,11... | collective-permute-start | bytes 1228808 | tf_op jit(solution)/shard_map/ppermute | solution.py:513
  125.0 23.9 %collective-permute-start.13 = (bf16[1,4,100,512]{3,2,1,0:T(8,128)(2,1)}, bf16[1,4,100,512]{3,2,1,0:T(8,128)(2,1)}, u32[]{:S(2)}, u32[]{:S(2)}) collective-permute-start(bf16[1,4,100,512]{3,2,1,0:T(8,128)(2,1)} %collective-permute-done.12), channel_id=1, source_target_pairs={{0,1},{1,0},{2,3},{3,2},{4,5},{5,4},{6,7},{7,6},{8,9},{9,8},{10,11... | collective-permute-start | bytes 1228808 | tf_op jit(solution)/shard_map/ppermute | solution.py:513
  125.6 9.8 %collective-permute-start.10 = (bf16[1,400,128]{2,1,0:T(8,128)(2,1)S(1)}, bf16[1,400,128]{2,1,0:T(8,128)(2,1)S(1)}, u32[]{:S(2)}, u32[]{:S(2)}) collective-permute-start(bf16[1,400,128]{2,1,0:T(8,128)(2,1)S(1)} %get-tuple-element.185), channel_id=1, source_target_pairs={{0,6},{1,7},{2,4},{3,5},{4,2},{5,3},{6,0},{7,1},{8,14},{9,15},{10,... | collective-permute-start | bytes 307208 | tf_op jit(solution)/shard_map/ppermute | solution.py:524
  135.4 7.8 %collective-permute-start.9 = (bf16[1,400,128]{2,1,0:T(8,128)(2,1)S(1)}, bf16[1,400,128]{2,1,0:T(8,128)(2,1)S(1)}, u32[]{:S(2)}, u32[]{:S(2)}) collective-permute-start(bf16[1,400,128]{2,1,0:T(8,128)(2,1)S(1)} %get-tuple-element.186), channel_id=1, source_target_pairs={{0,4},{1,5},{2,6},{3,7},{4,0},{5,1},{6,2},{7,3},{8,12},{9,13},{10,... | collective-permute-start | bytes 307208 | tf_op jit(solution)/shard_map/ppermute | solution.py:524
  143.3 0.6 copy-start
  143.9 5.0 %collective-permute-start.8 = (bf16[1,400,128]{2,1,0:T(8,128)(2,1)}, bf16[1,400,128]{2,1,0:T(8,128)(2,1)}, u32[]{:S(2)}, u32[]{:S(2)}) collective-permute-start(bf16[1,400,128]{2,1,0:T(8,128)(2,1)} %get-tuple-element.187), channel_id=1, source_target_pairs={{0,2},{1,3},{2,0},{3,1},{4,6},{5,7},{6,4},{7,5},{8,10},{9,11},{10,... | collective-permute-start | bytes 307208 | tf_op jit(solution)/shard_map/ppermute | solution.py:524
  148.9 7.1 %copy-start.2 = (s32[1,128]{1,0:T(1,128)S(1)}, s32[1,128]{1,0:T(1,128)}, u32[]{:S(2)}) copy-start(s32[1,128]{1,0:T(1,128)} %neg_ref.1) | copy-start | bytes 1540
  156.0 0.9 copy-start.1

commit v4 on v3

--- a/solution.py
+++ b/solution.py
@@ -114,34 +114,49 @@
     return rows if bands == 1 else pl.cdiv(pl.cdiv(rows, bands), 16) * 16
 
 
-def pick_coef_kernel(nrel, rel_ref, coef_ref, picked_ref, halves, acc):
+def pick_coef_kernel(nrel, fold, rel_ref, coef_ref, picked_ref, halves, acc):
     step = pl.program_id(0)
     nb, width = coef_ref.shape
-    lane = lax.broadcasted_iota(I32, (nb, width), 1) + step * width
-    block = jnp.where(lane < nrel, coef_ref[...], 0.0)
-    low = block - block.astype(BF16).astype(F32)
-    tall = acc.shape[0] // 2
-    spare = [jnp.zeros((tall - nb, width), F32)] * (tall > nb)
-    halves[...] = jnp.concatenate([block, *spare, low, *spare], axis=0).astype(BF16)
+    part = width // fold
+    tall = acc.shape[0]
+    half = tall // 2
+    lane = lax.broadcasted_iota(I32, (nb, part), 1) + step * width
+    spare = [jnp.zeros((half - nb, part), F32)] * (half > nb)
+    for f in range(fold):
+        block = coef_ref[:, f * part:(f + 1) * part]
+        block = jnp.where(lane < nrel - f * part, block, 0.0)
+        low = block - block.astype(BF16).astype(F32)
+        both = jnp.concatenate([block, *spare, low, *spare], axis=0)
+        halves[f * tall:(f + 1) * tall] = both.astype(BF16)
+    here = rel_ref[...] - step * width
+    where = here // part
+    here = jnp.where((here >= 0) & (here < width), here - where * part, -1)
+    found = nn(halves[...], hits(here, part, 0))
+    total = jnp.where(where == 0, found[0:tall], 0.0)
+    for f in range(1, fold):
+        total = jnp.where(where == f, found[f * tall:(f + 1) * tall], total)
 
     @pl.when(step == 0)
     def _():
-        acc[...] = jnp.zeros_like(acc)
-
-    acc[...] += nn(halves[...], hits(rel_ref[...], width, step * width))
+        acc[...] = total
+
+    @pl.when(step > 0)
+    def _():
+        acc[...] += total
 
     @pl.when(step == pl.num_programs(0) - 1)
     def _():
-        picked_ref[...] = acc[0:nb] + acc[tall:tall + nb]
+        picked_ref[...] = acc[0:nb] + acc[half:half + nb]
 
 
 def pick_coef(rel, coef_t):
     nb, nrel = coef_t.shape
     triples = rel.shape[1]
-    width = 1920
-    tall = pl.cdiv(nb, 8) * 8
-    return pl.pallas_call(
-        functools.partial(pick_coef_kernel, nrel),
+    fold = 2
+    width = fold * 1920
+    tall = 2 * (pl.cdiv(nb, 8) * 8)
+    return pl.pallas_call(
+        functools.partial(pick_coef_kernel, nrel, fold),
         grid=(pl.cdiv(nrel, width),),
         in_specs=[
             pl.BlockSpec((1, triples), lambda i: (0, 0)),
@@ -149,9 +164,10 @@
         ],
         out_specs=pl.BlockSpec((nb, triples), lambda i: (0, 0)),
         out_shape=jax.ShapeDtypeStruct((nb, triples), F32),
-        scratch_shapes=[pltpu.VMEM((2 * tall, width), BF16), pltpu.VMEM((2 * tall, triples), F32)],
+        scratch_shapes=[pltpu.VMEM((fold * tall, width // fold), BF16),
+                        pltpu.VMEM((tall, triples), F32)],
         compiler_params=params(),
-        cost_estimate=cost(4 * tall * nrel * triples, nb * nrel * 4),
+        cost_estimate=cost(2 * tall * nrel * triples, nb * nrel * 4),
         name="pick_coef",
     )(rel, coef_t)
 
@@ -233,7 +249,7 @@
     mix = jnp.zeros((cols, triples), F32)
     for first in range(0, group, 8):
         negs = jnp.concatenate([negs_ref[first + k] for k in range(8)], axis=1)
-        probs = jax.nn.sigmoid(tn(negs, head_rel)).astype(BF16)
+        probs = (0.5 * jnp.tanh(0.5 * tn(negs, head_rel)) + 0.5).astype(BF16)
         probs_ref[first * per:(first + 8) * per] = probs
         mix = mix + nn(negs, probs)
     rel_grad = -gate * head * tail + head * mix / neg_count
@@ -444,8 +460,7 @@
     )(jnp.concatenate([me, layer]), *sets)
 
 
-def add_rows_kernel(slots, recv_ref, neg_ref, *refs):
-    part_refs, (out_ref, grads, ids, sems) = refs[:-4], refs[-4:]
+def add_rows_kernel(slots, recv_ref, neg_ref, own_ref, out_ref, grads, ids, sems):
     step = pl.program_id(0)
     cols, width = out_ref.shape
     sources, high, _ = recv_ref.shape
@@ -467,11 +482,7 @@
                     grads[b * high:(b + 1) * high, at] = jnp.concatenate(block, axis=1)
         for copy in copies:
             copy.start()
-        total = jnp.zeros((cols, LANES), F32)
-        for ref in part_refs:
-            for k in range(ref.shape[0]):
-                total = total + ref[k].astype(F32)
-        top, low = split(total)
+        top, low = split(own_ref[...])
         grads[0:cols, lanes:lanes + LANES] = top
         grads[0:cols, lanes + LANES:] = low
         ids[:, lanes:lanes + LANES] = neg_ref[...]
@@ -484,7 +495,7 @@
     out_ref[...] = nt(grads[0:cols], hits(ids[...], width, step * width))
 
 
-def add_rows(recv, slots, cols, ent, neg_ids, part_sets):
+def add_rows(recv, slots, cols, ent, neg_ids, own_neg):
     sources, high, _ = recv.shape
     bands = LANES // slots
     width = 1024
@@ -494,7 +505,7 @@
     return pl.pallas_call(
         functools.partial(add_rows_kernel, slots),
         grid=(ent // width,),
-        in_specs=[there] + [whole(r.shape) for r in (neg_ids, *part_sets)],
+        in_specs=[there, whole(neg_ids.shape), whole(own_neg.shape)],
         out_specs=pl.BlockSpec((cols, width), lambda i: (0, i)),
         out_shape=jax.ShapeDtypeStruct((cols, ent), F32),
         scratch_shapes=[pltpu.VMEM((bands * high, lanes), BF16),
@@ -503,28 +514,26 @@
         compiler_params=params(32),
         cost_estimate=cost(1, 1),
         name="add_rows",
-    )(recv, neg_ids, *part_sets)
-
-
-def from_group(block, group):
+    )(recv, neg_ids, own_neg)
+
+
+def from_group(block, pairs, group):
     block = block[None]
     if group != 8:
-        return [lax.all_gather(block, "dev", axis=0, tiled=True)]
+        parts = lax.all_to_all(pairs, "dev", 0, 0, tiled=True)
+        return [lax.all_gather(block, "dev", axis=0, tiled=True)], [parts]
     swap = lambda x, far: lax.ppermute(x, "dev", [(i, i ^ far) for i in range(group)])
-    blocks = {0: block, 2: swap(block, 2), 4: swap(block, 4), 6: swap(block, 6)}
-    for far in (0, 2, 4, 6):
-        blocks[far + 1] = swap(blocks[far], 1)
-    return [blocks[t] for t in range(group)]
-
-
-def sum_here(parts, group):
+    even = [block] + [swap(block, far) for far in (2, 4, 6)]
+    parts = [pairs[0:1]] + [swap(pairs[n:n + 1], 2 * n) for n in (1, 2, 3)]
+    even, parts = lax.optimization_barrier((even, parts))
+    return [b for e in even for b in (e, swap(e, 1))], parts
+
+
+def sum_pairs(parts, group):
     if group != 8:
-        parts = parts.swapaxes(0, 1).reshape((group,) + parts.shape[2:])
-        return [lax.all_to_all(parts, "dev", 0, 0, tiled=True)]
-    swap = lambda x, far: lax.ppermute(x, "dev", [(i, i ^ far) for i in range(group)])
-    pairs = parts[0].astype(F32) + swap(parts[1], 1).astype(F32)
-    pairs = pairs.astype(BF16)
-    return [pairs[0:1]] + [swap(pairs[n:n + 1], 2 * n) for n in (1, 2, 3)]
+        return parts.swapaxes(0, 1).reshape((group,) + parts.shape[2:])
+    near = lax.ppermute(parts[1], "dev", [(i, i ^ 1) for i in range(group)])
+    return (parts[0].astype(F32) + near.astype(F32)).astype(BF16)
 
 
 def shift_layers(block, far, layers):
@@ -575,13 +584,15 @@
     send, coef_recv = lax.optimization_barrier((send, coef_recv))
     piece, flag = coef_sum(coef_recv, nb, plan, width)
     slabs = [piece] + [shift_layers(piece, far, layers) for far in range(1, layers)]
-    send, slabs = lax.optimization_barrier((send, slabs))
-    recv = lax.all_to_all(send, ("grp", "dev"), 0, 0, tiled=True)
-
     me = lax.axis_index("dev").astype(I32).reshape(1)
     layer = lax.axis_index("grp").astype(I32).reshape(1)
     at = me if group == 8 else jnp.zeros((1,), I32)
-    pieces = from_group(jnp.stack(slabs), group)
+    send, slabs = lax.optimization_barrier((send, slabs))
+    recv = lax.all_to_all(send, ("grp", "dev"), 0, 0, tiled=True)
+    pairs = sum_pairs(partial_step(at, probs, hrel, group, neg_count), group)
+    pieces, parts = from_group(jnp.stack(slabs), pairs, group)
+    own_neg = sum(part.astype(F32).sum(axis=0) for part in parts)
+    pieces, own_neg = lax.optimization_barrier((pieces, own_neg))
 
     def packed():
         return tuple(spread(at, layer, pieces, span, share, nrel, cols))
@@ -589,10 +600,8 @@
     def dense():
         return everywhere((jnp.zeros((nb, nrel), F32).at[:, relation].add(rows), base.T))
 
-    parts = sum_here(partial_step(at, probs, hrel, group, neg_count), group)
-    parts, pieces = lax.optimization_barrier((parts, pieces))
     coef_grad, bases_grad = lax.cond(flag[0, 0] == 0, packed, dense)
-    ent_grad = add_rows(recv, cap, cols, ent_local, neg_rows, parts)
+    ent_grad = add_rows(recv, cap, cols, ent_local, neg_rows, own_neg)
     return ent_grad.T, coef_grad.T, bases_grad.T
 
 

time: 176 us -> 167 us (0.949)
  the two profiles are of different devices: /device:TPU:16 before, /device:TPU:0 now
where the time goes in v4:
time: 167 us; the launch traced here: 165 us
  Pallas kernels  66.2 us (40%)
  waiting for transfers between devices  64.3 us (39%)
  starting transfers between devices  25.7 us (15%)
  other arithmetic  4.65 us (3%)
  local copies, waits for them, and re-layouts  3.31 us (2%)
    ppermute x10, waiting for transfers between devices, from_group(): lax.ppermute(x, 'dev', [(i, i ^ far) for i in range(group)])  43.9 us
    pallas_call x1, Pallas kernels, add_rows(): pl.pallas_call(functools.partial(add_rows_kernel, slots), grid=(ent // wi...  17.3 us
    pallas_call x1, Pallas kernels, pick_coef(): pl.pallas_call(functools.partial(pick_coef_kernel, nrel, fold), grid=(pl....  11.4 us
    pallas_call x1, Pallas kernels, order_slots(): pl.pallas_call(functools.partial(order_kernel, devices, slots), grid=(dev...  11.3 us
    pallas_call x1, Pallas kernels, score_step(): pl.pallas_call(functools.partial(score_kernel, neg_count, plan, share), o...  10.3 us
    ppermute x10, starting transfers between devices, from_group(): lax.ppermute(x, 'dev', [(i, i ^ far) for i in range(group)])  9.98 us
    ppermute x3, waiting for transfers between devices, shift_layers(): lax.ppermute(block, 'grp', [(i, (i + far) % layers) for i in range(layers)])  9.52 us
    pallas_call x1, Pallas kernels, spread(): pl.pallas_call(functools.partial(spread_kernel, span, share), grid_spec=p...  6.48 us
  transfers between devices with their start and end apart: 17, of which 12 were waited for; matrix products, arithmetic and copies ran while one was open for 4% of the time, Pallas kernels for 20%

profile of v4, /device:TPU:0, one launch (start us, length us, event | category | flops | bytes accessed | tf_op | source)
XLA Modules:
  0.0 165.0 jit_solution(4015225400424931154)
XLA Ops:
  0.6 4.5 %pick_negs.1 = bf16[8,400,128]{2,1,0:T(8,128)(2,1)} custom-call(s32[1,128]{1,0:T(1,128)} %neg_ref.1, bf16[400,4096]{1,0:T(8,128)(2,1)} %bitcast.43), custom_call_target="tpu_custom_call" | custom-call | flops 419430400 | bytes 3276800 | tf_op jit(solution)/shard_map/pick_negs/pallas_call | solution.py:84
  5.2 5.2 %all-to-all-start = ((bf16[8,400,128]{2,1,0:T(8,128)(2,1)}), bf16[8,400,128]{2,1,0:T(8,128)(2,1)S(1)}, u32[]{:S(2)}, u32[]{:S(2)}) async-start(bf16[8,400,128]{2,1,0:T(8,128)(2,1)} %pick_negs.1), calls=%async_computation | async-start | bytes 1638400 | tf_op jit(solution)/shard_map/all_to_all | solution.py:578
  10.3 11.4 %pick_coef.1.picked_ref = f32[100,1024]{1,0:T(8,128)} custom-call(s32[1,1024]{1,0:T(1,128)} %bitcast.49, f32[100,14824]{1,0:T(8,128)} %bitcast.51), custom_call_target="tpu_custom_call" | custom-call | flops 6314786816 | bytes 5929600 | tf_op jit(solution)/shard_map/pick_coef/pallas_call | solution.py:158
  21.8 1.5 all-to-all-done.negs_ref
  23.3 0.9 copy-done.3
  24.2 10.3 %score_step.1 = (bf16[32,56,128]{2,1,0:T(8,128)(2,1)}, bf16[402,2048]{1,0:T(8,128)(2,1)}, f32[100,1024]{1,0:T(8,128)}, f32[100,400]{1,0:T(8,128)}, bf16[1024,102...) custom-call(s32[1,1024]{1,0:T(1,128)S(1)} %bitcast.50, f32[100,1024]{1,0:T(8,128)} %pick_coef.1.picked_ref, ...), custom_call_target="tpu_custom_call" | custom-call | flops 1677721600 | bytes 16777216 | tf_op jit(solution)/shard_map/score_step/pallas_call | solution.py:290
  34.5 4.8 %all-to-all-start.1 = ((bf16[32,56,128]{2,1,0:T(8,128)(2,1)}), bf16[32,56,128]{2,1,0:T(8,128)(2,1)S(1)}, u32[]{:S(2)}, u32[]{:S(2)}) async-start(bf16[32,56,128]{2,1,0:T(8,128)(2,1)} %get-tuple-element.134), calls=%async_computation.1 | async-start | bytes 917504 | tf_op jit(solution)/shard_map/all_to_all | solution.py:582
  39.3 11.3 %order_slots.1 = bf16[32,402,128]{2,1,0:T(8,128)(2,1)} custom-call(bf16[402,2048]{1,0:T(8,128)(2,1)} %get-tuple-element.133.grads_ref, s32[2,1024]{1,0:T(2,128)} %bitcast.56), custom_call_target="tpu_custom_call" | custom-call | flops 6744440832 | bytes 4194304 | tf_op jit(solution)/shard_map/order_slots/pallas_call | solution.py:335
  50.6 3.1 %all-to-all-done.1.recv_ref = bf16[32,56,128]{2,1,0:T(8,128)(2,1)S(1)} async-done(((bf16[32,56,128]{2,1,0:T(8,128)(2,1)}), bf16[32,56,128]{2,1,0:T(8,128)(2,1)S(1)}, u32[]{:S(2)}, u32[]{:S(2)}) %all-to-all-start.1) | async-done | bytes 458784 | tf_op jit(solution)/shard_map/all_to_all | solution.py:582
  53.7 0.9 coef_sum.1
  54.6 1.2 collective-permute-start.6
  55.7 1.5 collective-permute-start.5
  57.3 2.3 %collective-permute-done.6 = bf16[100,512]{1,0:T(8,128)(2,1)S(1)} collective-permute-done((bf16[100,512]{1,0:T(8,128)(2,1)S(1)}, bf16[100,512]{1,0:T(8,128)(2,1)S(1)}, u32[]{:S(2)}, u32[]{:S(2)}) %collective-permute-start.6) | collective-permute-done | bytes 102432 | tf_op jit(solution)/shard_map/ppermute | solution.py:540
  59.6 7.2 %collective-permute-done.5 = bf16[100,512]{1,0:T(8,128)(2,1)S(1)} collective-permute-done((bf16[100,512]{1,0:T(8,128)(2,1)S(1)}, bf16[100,512]{1,0:T(8,128)(2,1)S(1)}, u32[]{:S(2)}, u32[]{:S(2)}) %collective-permute-start.5) | collective-permute-done | bytes 102432 | tf_op jit(solution)/shard_map/ppermute | solution.py:540
  66.8 0.6 copy-done.5
  67.5 3.0 %all-to-all-start.2 = ((bf16[32,402,128]{2,1,0:T(8,128)(2,1)}), bf16[32,402,128]{2,1,0:T(8,128)(2,1)S(1)}, u32[]{:S(2)}, u32[]{:S(2)}) async-start(bf16[32,402,128]{2,1,0:T(8,128)(2,1)} %order_slots.1), calls=%async_computation.2 | async-start | bytes 6684672 | tf_op jit(solution)/shard_map/all_to_all | solution.py:591
  70.4 3.9 %partial_step.1 = bf16[2,4,400,128]{3,2,1,0:T(8,128)(2,1)} custom-call(s32[1]{0:T(128)} %bitcast.16.me_ref, bf16[1024,1024]{1,0:T(8,128)(2,1)} %get-tuple-element.143.probs_ref, bf16[400,1024]{1,0:T(8,128)(2,1)} %get-tuple-element.144.hrel_ref), custom_call_target="tpu_custom_call" | custom-call | flops 1 | bytes 1 | tf_op jit(solution)/shard_map/partial_step/pallas_call | solution.py:362
  74.4 1.0 slice_bitcast_fusion
  75.5 1.7 %collective-permute-done.10 = bf16[4,400,128]{2,1,0:T(8,128)(2,1)S(1)} collective-permute-done((bf16[4,400,128]{2,1,0:T(8,128)(2,1)S(1)}, bf16[4,400,128]{2,1,0:T(8,128)(2,1)S(1)}, u32[]{:S(2)}, u32[]{:S(2)}) %collective-permute-start.10) | collective-permute-done | bytes 409632 | tf_op jit(solution)/shard_map/ppermute | solution.py:535
  77.2 1.1 fusion.3
  78.4 1.8 %maximum_bitcast_fusion = bf16[1,4,100,512]{3,2,1,0:T(8,128)(2,1)} fusion(bf16[1,100,512]{2,1,0:T(8,128)(2,1)} %bitcast.46, bf16[1,100,512]{2,1,0:T(8,128)(2,1)} %bitcast.47, bf16[1,100,512]{2,1,0:T(8,128)(2,1)} %bitcast.48, bf16[1,100,512]{2,1,0:T(8,128)(2,1)S(1)} %bitcast.34), kind=kLoop, calls=%fused_computation.8 | loop fusion | flops 614400 | bytes 819200 | tf_op jit(solution)/shard_map/broadcast_in_dim | solution.py:521
  80.2 2.4 %collective-permute-start.9 = (bf16[1,4,100,512]{3,2,1,0:T(8,128)(2,1)}, bf16[1,4,100,512]{3,2,1,0:T(8,128)(2,1)}, u32[]{:S(2)}, u32[]{:S(2)}) collective-permute-start(bf16[1,4,100,512]{3,2,1,0:T(8,128)(2,1)} %maximum_bitcast_fusion), channel_id=1, source_target_pairs={{0,6},{1,7},{2,4},{3,5},{4,2},{5,3},{6,0},{7,1},{8,14},{9,15},{10,... | collective-permute-start | bytes 1228808 | tf_op jit(solution)/shard_map/ppermute | solution.py:525
  83.7 0.7 fusion.4
  84.3 2.4 %collective-permute-start.13 = (bf16[1,400,128]{2,1,0:T(8,128)(2,1)S(1)}, bf16[1,400,128]{2,1,0:T(8,128)(2,1)S(1)}, u32[]{:S(2)}, u32[]{:S(2)}) collective-permute-start(bf16[1,400,128]{2,1,0:T(8,128)(2,1)S(1)} %get-tuple-element.195), channel_id=1, source_target_pairs={{0,6},{1,7},{2,4},{3,5},{4,2},{5,3},{6,0},{7,1},{8,14},{9,15},{10,... | collective-permute-start | bytes 307208 | tf_op jit(solution)/shard_map/ppermute | solution.py:525
  87.3 39.2 %collective-permute-done.13 = bf16[1,400,128]{2,1,0:T(8,128)(2,1)S(1)} collective-permute-done((bf16[1,400,128]{2,1,0:T(8,128)(2,1)S(1)}, bf16[1,400,128]{2,1,0:T(8,128)(2,1)S(1)}, u32[]{:S(2)}, u32[]{:S(2)}) %collective-permute-start.13) | collective-permute-done | bytes 102432 | tf_op jit(solution)/shard_map/ppermute | solution.py:525
  126.5 2.5 %collective-permute-start.11 = (bf16[1,400,128]{2,1,0:T(8,128)(2,1)S(1)}, bf16[1,400,128]{2,1,0:T(8,128)(2,1)}, u32[]{:S(2)}, u32[]{:S(2)}) collective-permute-start(bf16[1,400,128]{2,1,0:T(8,128)(2,1)S(1)} %get-tuple-element.197), channel_id=1, source_target_pairs={{0,2},{1,3},{2,0},{3,1},{4,6},{5,7},{6,4},{7,5},{8,10},{9,11},{10,... | collective-permute-start | bytes 307208 | tf_op jit(solution)/shard_map/ppermute | solution.py:525
  129.2 2.7 %collective-permute-done.11 = bf16[1,400,128]{2,1,0:T(8,128)(2,1)} collective-permute-done((bf16[1,400,128]{2,1,0:T(8,128)(2,1)S(1)}, bf16[1,400,128]{2,1,0:T(8,128)(2,1)}, u32[]{:S(2)}, u32[]{:S(2)}) %collective-permute-start.11) | collective-permute-done | bytes 102432 | tf_op jit(solution)/shard_map/ppermute | solution.py:525
  133.1 1.1 add_bitcast_fusion.own_ref
  135.9 7.1 %conditional.1 = ((f32[100,14824]{1,0:T(8,128)}, f32[400,100]{1,0:T(8,128)})) conditional(s32[]{:T(128)} %bitcast.21, (s32[1024]{0:T(1024)S(1)}, f32[100,1024]{1,0:T(8,128)}, f32[100,400]{1,0:T(8,128)}) %tuple.66, (s32[]{:T(128)}, s32[1]{0:T(128)}, bf16[1,4,100,512]{3,2,1,0:T(8,128)(2,1)}, bf16[1,4,100,512]{3,2,1,0:T(8,128)(2,1)}, ...), branch_computations={%region_0.6_spmd, %region_6.7_spmd} | conditional | flops 3150276 | bytes 237930176 | solution.py:603
  136.5 6.5 %spread.1 = (f32[100,14824]{1,0:T(8,128)}, f32[400,100]{1,0:T(8,128)}) custom-call(s32[2]{0:T(128)} %pad_add_fusion.place_ref, bf16[1,4,100,512]{3,2,1,0:T(8,128)(2,1)} %get-tuple-element.88.refs_0_, bf16[1,4,100,512]{3,2,1,0:T(8,128)(2,1)} %get-tuple-element.89.refs_1_, bf16[1,4,100,512]{3,2,1,0:T(8,128)(2,1)} %get-tuple-element.90.refs_2_, ...), custom_call_target="tpu_custom_call" | custom-call | flops 1 | bytes 1 | tf_op jit(solution)/shard_map/cond/branch_1_fun/spread/pallas_call | solution.py:443
  143.0 4.5 %all-to-all-done.2.recv_ref = bf16[32,402,128]{2,1,0:T(8,128)(2,1)S(1)} async-done(((bf16[32,402,128]{2,1,0:T(8,128)(2,1)}), bf16[32,402,128]{2,1,0:T(8,128)(2,1)S(1)}, u32[]{:S(2)}, u32[]{:S(2)}) %all-to-all-start.2) | async-done | bytes 3293216 | tf_op jit(solution)/shard_map/all_to_all | solution.py:591
  147.5 17.3 %add_rows.1 = f32[400,4096]{1,0:T(8,128)} custom-call(bf16[32,402,128]{2,1,0:T(8,128)(2,1)S(1)} %all-to-all-done.2.recv_ref, s32[1,128]{1,0:T(1,128)S(1)} %copy-done, f32[400,128]{1,0:T(8,128)S(1)} %add_bitcast_fusion.own_ref), custom_call_target="tpu_custom_call" | custom-call | flops 1 | bytes 1 | tf_op jit(solution)/shard_map/add_rows/pallas_call | solution.py:505
  (33 shorter events, 5.4 us)
Async XLA Ops:
  5.2 18.1 %all-to-all-start = ((bf16[8,400,128]{2,1,0:T(8,128)(2,1)}), bf16[8,400,128]{2,1,0:T(8,128)(2,1)S(1)}, u32[]{:S(2)}, u32[]{:S(2)}) async-start(bf16[8,400,128]{2,1,0:T(8,128)(2,1)} %pick_negs.1), calls=%async_computation | async-start | bytes 1638400 | tf_op jit(solution)/shard_map/all_to_all | solution.py:578
  10.3 13.9 %copy-start.9 = (s32[1024]{0:T(1024)S(1)}, s32[1024]{0:T(1024)}, u32[]{:S(2)}) copy-start(s32[1024]{0:T(1024)} %param.17) | copy-start | bytes 12292
  23.3 0.9 copy-start.3
  34.5 19.2 %all-to-all-start.1 = ((bf16[32,56,128]{2,1,0:T(8,128)(2,1)}), bf16[32,56,128]{2,1,0:T(8,128)(2,1)S(1)}, u32[]{:S(2)}, u32[]{:S(2)}) async-start(bf16[32,56,128]{2,1,0:T(8,128)(2,1)} %get-tuple-element.134), calls=%async_computation.1 | async-start | bytes 917504 | tf_op jit(solution)/shard_map/all_to_all | solution.py:582
  54.6 5.0 %collective-permute-start.6 = (bf16[100,512]{1,0:T(8,128)(2,1)S(1)}, bf16[100,512]{1,0:T(8,128)(2,1)S(1)}, u32[]{:S(2)}, u32[]{:S(2)}) collective-permute-start(bf16[100,512]{1,0:T(8,128)(2,1)S(1)} %get-tuple-element.139), channel_id=1, source_target_pairs={{0,24},{8,0},{16,8},{24,16},{1,25},{9,1},{17,9},{25,17},{2,26},{10... | collective-permute-start | bytes 307208 | tf_op jit(solution)/shard_map/ppermute | solution.py:540
  55.7 11.0 %collective-permute-start.5 = (bf16[100,512]{1,0:T(8,128)(2,1)S(1)}, bf16[100,512]{1,0:T(8,128)(2,1)S(1)}, u32[]{:S(2)}, u32[]{:S(2)}) collective-permute-start(bf16[100,512]{1,0:T(8,128)(2,1)S(1)} %get-tuple-element.139), channel_id=1, source_target_pairs={{0,16},{8,24},{16,0},{24,8},{1,17},{9,25},{17,1},{25,9},{2,18},{10... | collective-permute-start | bytes 307208 | tf_op jit(solution)/shard_map/ppermute | solution.py:540
  57.3 9.5 %collective-permute-start.4 = (bf16[100,512]{1,0:T(8,128)(2,1)S(1)}, bf16[100,512]{1,0:T(8,128)(2,1)S(1)}, u32[]{:S(2)}, u32[]{:S(2)}) collective-permute-start(bf16[100,512]{1,0:T(8,128)(2,1)S(1)} %get-tuple-element.139), channel_id=1, source_target_pairs={{0,8},{8,16},{16,24},{24,0},{1,9},{9,17},{17,25},{25,1},{2,10},{10... | collective-permute-start | bytes 307208 | tf_op jit(solution)/shard_map/ppermute | solution.py:540
  59.6 7.2 %copy-start.4 = (bf16[100,512]{1,0:T(8,128)(2,1)}, bf16[100,512]{1,0:T(8,128)(2,1)S(1)}, u32[]{:S(2)}) copy-start(bf16[100,512]{1,0:T(8,128)(2,1)S(1)} %collective-permute-done.6) | copy-start | bytes 307204
  66.8 0.6 copy-start.5
  66.8 0.7 copy-start.6
  67.5 80.0 %all-to-all-start.2 = ((bf16[32,402,128]{2,1,0:T(8,128)(2,1)}), bf16[32,402,128]{2,1,0:T(8,128)(2,1)S(1)}, u32[]{:S(2)}, u32[]{:S(2)}) async-start(bf16[32,402,128]{2,1,0:T(8,128)(2,1)} %order_slots.1), calls=%async_computation.2 | async-start | bytes 6684672 | tf_op jit(solution)/shard_map/all_to_all | solution.py:591
  75.4 1.8 %collective-permute-start.10 = (bf16[4,400,128]{2,1,0:T(8,128)(2,1)S(1)}, bf16[4,400,128]{2,1,0:T(8,128)(2,1)S(1)}, u32[]{:S(2)}, u32[]{:S(2)}) collective-permute-start(bf16[4,400,128]{2,1,0:T(8,128)(2,1)S(1)} %slice_bitcast_fusion), channel_id=1, source_target_pairs={{0,1},{1,0},{2,3},{3,2},{4,5},{5,4},{6,7},{7,6},{8,9},{9,8},{10,11... | collective-permute-start | bytes 1228808 | tf_op jit(solution)/shard_map/ppermute | solution.py:535
  80.2 51.7 %collective-permute-start.9 = (bf16[1,4,100,512]{3,2,1,0:T(8,128)(2,1)}, bf16[1,4,100,512]{3,2,1,0:T(8,128)(2,1)}, u32[]{:S(2)}, u32[]{:S(2)}) collective-permute-start(bf16[1,4,100,512]{3,2,1,0:T(8,128)(2,1)} %maximum_bitcast_fusion), channel_id=1, source_target_pairs={{0,6},{1,7},{2,4},{3,5},{4,2},{5,3},{6,0},{7,1},{8,14},{9,15},{10,... | collective-permute-start | bytes 1228808 | tf_op jit(solution)/shard_map/ppermute | solution.py:525
  82.6 49.3 %collective-permute-start.8 = (bf16[1,4,100,512]{3,2,1,0:T(8,128)(2,1)}, bf16[1,4,100,512]{3,2,1,0:T(8,128)(2,1)}, u32[]{:S(2)}, u32[]{:S(2)}) collective-permute-start(bf16[1,4,100,512]{3,2,1,0:T(8,128)(2,1)} %maximum_bitcast_fusion), channel_id=1, source_target_pairs={{0,4},{1,5},{2,6},{3,7},{4,0},{5,1},{6,2},{7,3},{8,12},{9,13},{10,... | collective-permute-start | bytes 1228808 | tf_op jit(solution)/shard_map/ppermute | solution.py:525
  83.1 48.8 %collective-permute-start.7 = (bf16[1,4,100,512]{3,2,1,0:T(8,128)(2,1)}, bf16[1,4,100,512]{3,2,1,0:T(8,128)(2,1)}, u32[]{:S(2)}, u32[]{:S(2)}) collective-permute-start(bf16[1,4,100,512]{3,2,1,0:T(8,128)(2,1)} %maximum_bitcast_fusion), channel_id=1, source_target_pairs={{0,2},{1,3},{2,0},{3,1},{4,6},{5,7},{6,4},{7,5},{8,10},{9,11},{10,... | collective-permute-start | bytes 1228808 | tf_op jit(solution)/shard_map/ppermute | solution.py:525
  84.3 42.1 %collective-permute-start.13 = (bf16[1,400,128]{2,1,0:T(8,128)(2,1)S(1)}, bf16[1,400,128]{2,1,0:T(8,128)(2,1)S(1)}, u32[]{:S(2)}, u32[]{:S(2)}) collective-permute-start(bf16[1,400,128]{2,1,0:T(8,128)(2,1)S(1)} %get-tuple-element.195), channel_id=1, source_target_pairs={{0,6},{1,7},{2,4},{3,5},{4,2},{5,3},{6,0},{7,1},{8,14},{9,15},{10,... | collective-permute-start | bytes 307208 | tf_op jit(solution)/shard_map/ppermute | solution.py:525
  86.7 42.4 %collective-permute-start.12 = (bf16[1,400,128]{2,1,0:T(8,128)(2,1)S(1)}, bf16[1,400,128]{2,1,0:T(8,128)(2,1)S(1)}, u32[]{:S(2)}, u32[]{:S(2)}) collective-permute-start(bf16[1,400,128]{2,1,0:T(8,128)(2,1)S(1)} %get-tuple-element.196), channel_id=1, source_target_pairs={{0,4},{1,5},{2,6},{3,7},{4,0},{5,1},{6,2},{7,3},{8,12},{9,13},{10,... | collective-permute-start | bytes 307208 | tf_op jit(solution)/shard_map/ppermute | solution.py:525
  126.5 6.6 %copy-start.7 = (bf16[1,400,128]{2,1,0:T(8,128)(2,1)}, bf16[1,400,128]{2,1,0:T(8,128)(2,1)S(1)}, u32[]{:S(2)}) copy-start(bf16[1,400,128]{2,1,0:T(8,128)(2,1)S(1)} %collective-permute-done.13) | copy-start | bytes 307204
  126.5 5.4 %collective-permute-start.11 = (bf16[1,400,128]{2,1,0:T(8,128)(2,1)S(1)}, bf16[1,400,128]{2,1,0:T(8,128)(2,1)}, u32[]{:S(2)}, u32[]{:S(2)}) collective-permute-start(bf16[1,400,128]{2,1,0:T(8,128)(2,1)S(1)} %get-tuple-element.197), channel_id=1, source_target_pairs={{0,2},{1,3},{2,0},{3,1},{4,6},{5,7},{6,4},{7,5},{8,10},{9,11},{10,... | collective-permute-start | bytes 307208 | tf_op jit(solution)/shard_map/ppermute | solution.py:525
  129.2 3.9 %copy-start.8 = (bf16[1,400,128]{2,1,0:T(8,128)(2,1)}, bf16[1,400,128]{2,1,0:T(8,128)(2,1)S(1)}, u32[]{:S(2)}) copy-start(bf16[1,400,128]{2,1,0:T(8,128)(2,1)S(1)} %collective-permute-done.12) | copy-start | bytes 307204
  131.9 2.3 %collective-permute-start.14 = (bf16[1,4,100,512]{3,2,1,0:T(8,128)(2,1)}, bf16[1,4,100,512]{3,2,1,0:T(8,128)(2,1)}, u32[]{:S(2)}, u32[]{:S(2)}) collective-permute-start(bf16[1,4,100,512]{3,2,1,0:T(8,128)(2,1)} %maximum_bitcast_fusion), channel_id=1, source_target_pairs={{0,1},{1,0},{2,3},{3,2},{4,5},{5,4},{6,7},{7,6},{8,9},{9,8},{10,11... | collective-permute-start | bytes 1228808 | tf_op jit(solution)/shard_map/ppermute | solution.py:525
  132.0 2.7 %collective-permute-start.15 = (bf16[1,4,100,512]{3,2,1,0:T(8,128)(2,1)}, bf16[1,4,100,512]{3,2,1,0:T(8,128)(2,1)}, u32[]{:S(2)}, u32[]{:S(2)}) collective-permute-start(bf16[1,4,100,512]{3,2,1,0:T(8,128)(2,1)} %collective-permute-done.7), channel_id=1, source_target_pairs={{0,1},{1,0},{2,3},{3,2},{4,5},{5,4},{6,7},{7,6},{8,9},{9,8},{10,11... | collective-permute-start | bytes 1228808 | tf_op jit(solution)/shard_map/ppermute | solution.py:525
  132.5 2.8 %collective-permute-start.16 = (bf16[1,4,100,512]{3,2,1,0:T(8,128)(2,1)}, bf16[1,4,100,512]{3,2,1,0:T(8,128)(2,1)}, u32[]{:S(2)}, u32[]{:S(2)}) collective-permute-start(bf16[1,4,100,512]{3,2,1,0:T(8,128)(2,1)} %collective-permute-done.8), channel_id=1, source_target_pairs={{0,1},{1,0},{2,3},{3,2},{4,5},{5,4},{6,7},{7,6},{8,9},{9,8},{10,11... | collective-permute-start | bytes 1228808 | tf_op jit(solution)/shard_map/ppermute | solution.py:525
  132.6 3.3 %collective-permute-start.17 = (bf16[1,4,100,512]{3,2,1,0:T(8,128)(2,1)}, bf16[1,4,100,512]{3,2,1,0:T(8,128)(2,1)}, u32[]{:S(2)}, u32[]{:S(2)}) collective-permute-start(bf16[1,4,100,512]{3,2,1,0:T(8,128)(2,1)} %collective-permute-done.9), channel_id=1, source_target_pairs={{0,1},{1,0},{2,3},{3,2},{4,5},{5,4},{6,7},{7,6},{8,9},{9,8},{10,11... | collective-permute-start | bytes 1228808 | tf_op jit(solution)/shard_map/ppermute | solution.py:525
  135.9 11.6 %copy-start = (s32[1,128]{1,0:T(1,128)S(1)}, s32[1,128]{1,0:T(1,128)}, u32[]{:S(2)}) copy-start(s32[1,128]{1,0:T(1,128)} %neg_ref.1) | copy-start | bytes 1540

commit v5 on v4

--- a/solution.py
+++ b/solution.py
@@ -80,7 +80,7 @@
 
 def pick_negs(ids, ent_t, group):
     cols, ent = ent_t.shape
-    width = 1024
+    width = 2048
     return pl.pallas_call(
         pick_negs_kernel,
         grid=(ent // width,),
@@ -543,13 +543,12 @@
 def everywhere(values):
     for axis in ("dev", "grp"):
         count = lax.axis_size(axis)
-        ring = [(i, (i + 1) % count) for i in range(count)]
-
-        def turn(_, state):
-            near = tuple(lax.ppermute(v, axis, ring) for v in state[0])
-            return near, tuple(t + n for t, n in zip(state[1], near))
-
-        values = lax.fori_loop(0, count - 1, turn, (values, values))[1]
+        assert count & (count - 1) == 0
+        far = 1
+        while far < count:
+            swap = [(i, i ^ far) for i in range(count)]
+            values = tuple(v + lax.ppermute(v, axis, swap) for v in values)
+            far *= 2
     return values
 
 

time: 167 us -> 163 us (0.976); the launches traced: 165 us -> 163 us
  waiting for transfers between devices: 64.3 us -> 60.2 us
  starting transfers between devices: 25.7 us -> 28.5 us
    ppermute x3, waiting for transfers between devices: 9.52 us -> 7.37 us  [shift_layers(): lax.ppermute(block, 'grp', [(i, (i + far) % layers) for i in range(layers)])]
    all_to_all x1, waiting for transfers between devices: 4.51 us -> 2.66 us  [per_device(): recv = lax.all_to_all(send, ('grp', 'dev'), 0, 0, tiled=True)]
  transfers between devices with their start and end apart: 17 -> 17, of which waited for: 12 -> 11; matrix products, arithmetic and copies ran while one was open for 4% -> 4% of each run, Pallas kernels for 20% -> 20%
where the time goes in v5:
time: 163 us
  Pallas kernels  65.3 us (40%)
  waiting for transfers between devices  60.2 us (37%)
  starting transfers between devices  28.5 us (17%)
  other arithmetic  4.67 us (3%)
  local copies, waits for them, and re-layouts  3.26 us (2%)
    ppermute x10, waiting for transfers between devices, from_group(): lax.ppermute(x, 'dev', [(i, i ^ far) for i in range(group)])  43.8 us
    pallas_call x1, Pallas kernels, add_rows(): pl.pallas_call(functools.partial(add_rows_kernel, slots), grid=(ent // wi...  17.3 us
    pallas_call x1, Pallas kernels, pick_coef(): pl.pallas_call(functools.partial(pick_coef_kernel, nrel, fold), grid=(pl....  11.4 us
    pallas_call x1, Pallas kernels, order_slots(): pl.pallas_call(functools.partial(order_kernel, devices, slots), grid=(dev...  11.3 us
    ppermute x10, starting transfers between devices, from_group(): lax.ppermute(x, 'dev', [(i, i ^ far) for i in range(group)])  10.8 us
    pallas_call x1, Pallas kernels, score_step(): pl.pallas_call(functools.partial(score_kernel, neg_count, plan, share), o...  10.3 us
    ppermute x3, waiting for transfers between devices, shift_layers(): lax.ppermute(block, 'grp', [(i, (i + far) % layers) for i in range(layers)])  7.37 us
    pallas_call x1, Pallas kernels, spread(): pl.pallas_call(functools.partial(spread_kernel, span, share), grid_spec=p...  6.48 us
  transfers between devices with their start and end apart: 17, of which 11 were waited for; matrix products, arithmetic and copies ran while one was open for 4% of the time, Pallas kernels for 20%

profile of v5, /device:TPU:0, one launch (start us, length us, event | category | flops | bytes accessed | tf_op | source)
XLA Modules:
  0.0 162.9 jit_solution(6924986239722037323)
XLA Ops:
  0.6 3.6 %pick_negs.1 = bf16[8,400,128]{2,1,0:T(8,128)(2,1)} custom-call(s32[1,128]{1,0:T(1,128)} %neg_ref.1, bf16[400,4096]{1,0:T(8,128)(2,1)} %bitcast.39), custom_call_target="tpu_custom_call" | custom-call | flops 419430400 | bytes 3276800 | tf_op jit(solution)/shard_map/pick_negs/pallas_call | solution.py:84
  4.2 5.2 %all-to-all-start = ((bf16[8,400,128]{2,1,0:T(8,128)(2,1)}), bf16[8,400,128]{2,1,0:T(8,128)(2,1)S(1)}, u32[]{:S(2)}, u32[]{:S(2)}) async-start(bf16[8,400,128]{2,1,0:T(8,128)(2,1)} %pick_negs.1), calls=%async_computation | async-start | bytes 1638400 | tf_op jit(solution)/shard_map/all_to_all | solution.py:577
  9.4 11.4 %pick_coef.1.picked_ref = f32[100,1024]{1,0:T(8,128)} custom-call(s32[1,1024]{1,0:T(1,128)} %bitcast.45, f32[100,14824]{1,0:T(8,128)} %bitcast.47), custom_call_target="tpu_custom_call" | custom-call | flops 6314786816 | bytes 5929600 | tf_op jit(solution)/shard_map/pick_coef/pallas_call | solution.py:158
  20.8 1.5 all-to-all-done.negs_ref
  22.4 0.9 copy-done.1
  23.3 10.3 %score_step.1 = (bf16[32,56,128]{2,1,0:T(8,128)(2,1)}, bf16[402,2048]{1,0:T(8,128)(2,1)}, f32[100,1024]{1,0:T(8,128)}, f32[100,400]{1,0:T(8,128)}, bf16[1024,102...) custom-call(s32[1,1024]{1,0:T(1,128)S(1)} %bitcast.46, f32[100,1024]{1,0:T(8,128)} %pick_coef.1.picked_ref, ...), custom_call_target="tpu_custom_call" | custom-call | flops 1677721600 | bytes 16777216 | tf_op jit(solution)/shard_map/score_step/pallas_call | solution.py:290
  33.6 4.8 %all-to-all-start.1 = ((bf16[32,56,128]{2,1,0:T(8,128)(2,1)}), bf16[32,56,128]{2,1,0:T(8,128)(2,1)S(1)}, u32[]{:S(2)}, u32[]{:S(2)}) async-start(bf16[32,56,128]{2,1,0:T(8,128)(2,1)} %get-tuple-element.78), calls=%async_computation.1 | async-start | bytes 917504 | tf_op jit(solution)/shard_map/all_to_all | solution.py:581
  38.4 11.3 %order_slots.1 = bf16[32,402,128]{2,1,0:T(8,128)(2,1)} custom-call(bf16[402,2048]{1,0:T(8,128)(2,1)} %get-tuple-element.77.grads_ref, s32[2,1024]{1,0:T(2,128)} %bitcast.52), custom_call_target="tpu_custom_call" | custom-call | flops 6744440832 | bytes 4194304 | tf_op jit(solution)/shard_map/order_slots/pallas_call | solution.py:335
  49.7 3.1 %all-to-all-done.1.recv_ref = bf16[32,56,128]{2,1,0:T(8,128)(2,1)S(1)} async-done(((bf16[32,56,128]{2,1,0:T(8,128)(2,1)}), bf16[32,56,128]{2,1,0:T(8,128)(2,1)S(1)}, u32[]{:S(2)}, u32[]{:S(2)}) %all-to-all-start.1) | async-done | bytes 458784 | tf_op jit(solution)/shard_map/all_to_all | solution.py:581
  52.8 0.9 coef_sum.1
  53.7 1.2 collective-permute-start.10
  55.4 2.2 %collective-permute-start.12 = (bf16[100,512]{1,0:T(8,128)(2,1)S(1)}, bf16[100,512]{1,0:T(8,128)(2,1)S(1)}, u32[]{:S(2)}, u32[]{:S(2)}) collective-permute-start(bf16[100,512]{1,0:T(8,128)(2,1)S(1)} %get-tuple-element.83), channel_id=1, source_target_pairs={{0,24},{8,0},{16,8},{24,16},{1,25},{9,1},{17,9},{25,17},{2,26},{10... | collective-permute-start | bytes 307208 | tf_op jit(solution)/shard_map/ppermute | solution.py:540
  57.5 3.9 %collective-permute-done.10 = bf16[100,512]{1,0:T(8,128)(2,1)S(1)} collective-permute-done((bf16[100,512]{1,0:T(8,128)(2,1)S(1)}, bf16[100,512]{1,0:T(8,128)(2,1)S(1)}, u32[]{:S(2)}, u32[]{:S(2)}) %collective-permute-start.10) | collective-permute-done | bytes 102432 | tf_op jit(solution)/shard_map/ppermute | solution.py:540
  61.4 3.5 %collective-permute-done.11 = bf16[100,512]{1,0:T(8,128)(2,1)S(1)} collective-permute-done((bf16[100,512]{1,0:T(8,128)(2,1)S(1)}, bf16[100,512]{1,0:T(8,128)(2,1)S(1)}, u32[]{:S(2)}, u32[]{:S(2)}) %collective-permute-start.11) | collective-permute-done | bytes 102432 | tf_op jit(solution)/shard_map/ppermute | solution.py:540
  65.6 3.8 %all-to-all-start.2 = ((bf16[32,402,128]{2,1,0:T(8,128)(2,1)}), bf16[32,402,128]{2,1,0:T(8,128)(2,1)S(1)}, u32[]{:S(2)}, u32[]{:S(2)}) async-start(bf16[32,402,128]{2,1,0:T(8,128)(2,1)} %order_slots.1), calls=%async_computation.2 | async-start | bytes 6684672 | tf_op jit(solution)/shard_map/all_to_all | solution.py:590
  69.4 3.9 %partial_step.1 = bf16[2,4,400,128]{3,2,1,0:T(8,128)(2,1)} custom-call(s32[1]{0:T(128)} %bitcast.16.me_ref, bf16[1024,1024]{1,0:T(8,128)(2,1)} %get-tuple-element.87.probs_ref, bf16[400,1024]{1,0:T(8,128)(2,1)} %get-tuple-element.88.hrel_ref), custom_call_target="tpu_custom_call" | custom-call | flops 1 | bytes 1 | tf_op jit(solution)/shard_map/partial_step/pallas_call | solution.py:362
  73.3 1.0 slice_bitcast_fusion
  74.5 1.7 %collective-permute-done.16 = bf16[4,400,128]{2,1,0:T(8,128)(2,1)S(1)} collective-permute-done((bf16[4,400,128]{2,1,0:T(8,128)(2,1)S(1)}, bf16[4,400,128]{2,1,0:T(8,128)(2,1)S(1)}, u32[]{:S(2)}, u32[]{:S(2)}) %collective-permute-start.16) | collective-permute-done | bytes 409632 | tf_op jit(solution)/shard_map/ppermute | solution.py:535
  76.2 1.1 fusion.3
  77.3 1.9 %maximum_bitcast_fusion = bf16[1,4,100,512]{3,2,1,0:T(8,128)(2,1)} fusion(bf16[1,100,512]{2,1,0:T(8,128)(2,1)} %bitcast.44, bf16[1,100,512]{2,1,0:T(8,128)(2,1)} %bitcast.43, bf16[1,100,512]{2,1,0:T(8,128)(2,1)} %bitcast.42, bf16[1,100,512]{2,1,0:T(8,128)(2,1)S(1)} %bitcast.35), kind=kLoop, calls=%fused_computation.9 | loop fusion | flops 614400 | bytes 819200 | tf_op jit(solution)/shard_map/broadcast_in_dim | solution.py:521
  79.1 1.6 collective-permute-start.13
  80.7 1.5 collective-permute-start.14
  83.3 1.6 collective-permute-start.17
  84.9 1.5 collective-permute-start.18
  86.3 39.2 %collective-permute-done.17 = bf16[1,400,128]{2,1,0:T(8,128)(2,1)} collective-permute-done((bf16[1,400,128]{2,1,0:T(8,128)(2,1)S(1)}, bf16[1,400,128]{2,1,0:T(8,128)(2,1)}, u32[]{:S(2)}, u32[]{:S(2)}) %collective-permute-start.17) | collective-permute-done | bytes 102432 | tf_op jit(solution)/shard_map/ppermute | solution.py:525
  125.5 3.2 %collective-permute-start.19 = (bf16[1,400,128]{2,1,0:T(8,128)(2,1)S(1)}, bf16[1,400,128]{2,1,0:T(8,128)(2,1)}, u32[]{:S(2)}, u32[]{:S(2)}) collective-permute-start(bf16[1,400,128]{2,1,0:T(8,128)(2,1)S(1)} %get-tuple-element.127), channel_id=1, source_target_pairs={{0,6},{1,7},{2,4},{3,5},{4,2},{5,3},{6,0},{7,1},{8,14},{9,15},{10,... | collective-permute-start | bytes 307208 | tf_op jit(solution)/shard_map/ppermute | solution.py:525
  128.7 2.9 %collective-permute-done.19 = bf16[1,400,128]{2,1,0:T(8,128)(2,1)} collective-permute-done((bf16[1,400,128]{2,1,0:T(8,128)(2,1)S(1)}, bf16[1,400,128]{2,1,0:T(8,128)(2,1)}, u32[]{:S(2)}, u32[]{:S(2)}) %collective-permute-start.19) | collective-permute-done | bytes 102432 | tf_op jit(solution)/shard_map/ppermute | solution.py:525
  132.7 1.1 add_bitcast_fusion.own_ref
  135.6 7.1 %conditional.1 = ((f32[100,14824]{1,0:T(8,128)}, f32[400,100]{1,0:T(8,128)})) conditional(s32[]{:T(128)} %bitcast.21, (s32[1024]{0:T(1024)S(1)}, f32[100,1024]{1,0:T(8,128)}, f32[100,400]{1,0:T(8,128)}) %tuple.41, (s32[]{:T(128)}, s32[1]{0:T(128)}, bf16[1,4,100,512]{3,2,1,0:T(8,128)(2,1)}, bf16[1,4,100,512]{3,2,1,0:T(8,128)(2,1)}, ...), branch_computations={%region_0.2_spmd, %region_2.0_spmd} | conditional | flops 7717472 | bytes 233237408 | solution.py:602
  136.2 6.5 %spread.1 = (f32[100,14824]{1,0:T(8,128)}, f32[400,100]{1,0:T(8,128)}) custom-call(s32[2]{0:T(128)} %pad_add_fusion.place_ref, bf16[1,4,100,512]{3,2,1,0:T(8,128)(2,1)} %get-tuple-element.32.refs_0_, bf16[1,4,100,512]{3,2,1,0:T(8,128)(2,1)} %get-tuple-element.33.refs_1_, bf16[1,4,100,512]{3,2,1,0:T(8,128)(2,1)} %get-tuple-element.34.refs_2_, ...), custom_call_target="tpu_custom_call" | custom-call | flops 1 | bytes 1 | tf_op jit(solution)/shard_map/cond/branch_1_fun/spread/pallas_call | solution.py:443
  142.7 2.7 %all-to-all-done.2.recv_ref = bf16[32,402,128]{2,1,0:T(8,128)(2,1)S(1)} async-done(((bf16[32,402,128]{2,1,0:T(8,128)(2,1)}), bf16[32,402,128]{2,1,0:T(8,128)(2,1)S(1)}, u32[]{:S(2)}, u32[]{:S(2)}) %all-to-all-start.2) | async-done | bytes 3293216 | tf_op jit(solution)/shard_map/all_to_all | solution.py:590
  145.3 17.3 %add_rows.1 = f32[400,4096]{1,0:T(8,128)} custom-call(bf16[32,402,128]{2,1,0:T(8,128)(2,1)S(1)} %all-to-all-done.2.recv_ref, s32[1,128]{1,0:T(1,128)S(1)} %copy-done, f32[400,128]{1,0:T(8,128)S(1)} %add_bitcast_fusion.own_ref), custom_call_target="tpu_custom_call" | custom-call | flops 1 | bytes 1 | tf_op jit(solution)/shard_map/add_rows/pallas_call | solution.py:505
  (29 shorter events, 5.9 us)
Async XLA Ops:
  4.2 18.1 %all-to-all-start = ((bf16[8,400,128]{2,1,0:T(8,128)(2,1)}), bf16[8,400,128]{2,1,0:T(8,128)(2,1)S(1)}, u32[]{:S(2)}, u32[]{:S(2)}) async-start(bf16[8,400,128]{2,1,0:T(8,128)(2,1)} %pick_negs.1), calls=%async_computation | async-start | bytes 1638400 | tf_op jit(solution)/shard_map/all_to_all | solution.py:577
  9.4 13.8 %copy-start.6 = (s32[1024]{0:T(1024)S(1)}, s32[1024]{0:T(1024)}, u32[]{:S(2)}) copy-start(s32[1024]{0:T(1024)} %param.13) | copy-start | bytes 12292
  22.4 0.9 copy-start.1
  33.6 19.2 %all-to-all-start.1 = ((bf16[32,56,128]{2,1,0:T(8,128)(2,1)}), bf16[32,56,128]{2,1,0:T(8,128)(2,1)S(1)}, u32[]{:S(2)}, u32[]{:S(2)}) async-start(bf16[32,56,128]{2,1,0:T(8,128)(2,1)} %get-tuple-element.78), calls=%async_computation.1 | async-start | bytes 917504 | tf_op jit(solution)/shard_map/all_to_all | solution.py:581
  53.7 7.8 %collective-permute-start.10 = (bf16[100,512]{1,0:T(8,128)(2,1)S(1)}, bf16[100,512]{1,0:T(8,128)(2,1)S(1)}, u32[]{:S(2)}, u32[]{:S(2)}) collective-permute-start(bf16[100,512]{1,0:T(8,128)(2,1)S(1)} %get-tuple-element.83), channel_id=1, source_target_pairs={{0,8},{8,16},{16,24},{24,0},{1,9},{9,17},{17,25},{25,1},{2,10},{10... | collective-permute-start | bytes 307208 | tf_op jit(solution)/shard_map/ppermute | solution.py:540
  54.9 10.0 %collective-permute-start.11 = (bf16[100,512]{1,0:T(8,128)(2,1)S(1)}, bf16[100,512]{1,0:T(8,128)(2,1)S(1)}, u32[]{:S(2)}, u32[]{:S(2)}) collective-permute-start(bf16[100,512]{1,0:T(8,128)(2,1)S(1)} %get-tuple-element.83), channel_id=1, source_target_pairs={{0,16},{8,24},{16,0},{24,8},{1,17},{9,25},{17,1},{25,9},{2,18},{10... | collective-permute-start | bytes 307208 | tf_op jit(solution)/shard_map/ppermute | solution.py:540
  55.4 9.5 %collective-permute-start.12 = (bf16[100,512]{1,0:T(8,128)(2,1)S(1)}, bf16[100,512]{1,0:T(8,128)(2,1)S(1)}, u32[]{:S(2)}, u32[]{:S(2)}) collective-permute-start(bf16[100,512]{1,0:T(8,128)(2,1)S(1)} %get-tuple-element.83), channel_id=1, source_target_pairs={{0,24},{8,0},{16,8},{24,16},{1,25},{9,1},{17,9},{25,17},{2,26},{10... | collective-permute-start | bytes 307208 | tf_op jit(solution)/shard_map/ppermute | solution.py:540
  61.4 3.5 %copy-start.3 = (bf16[100,512]{1,0:T(8,128)(2,1)}, bf16[100,512]{1,0:T(8,128)(2,1)S(1)}, u32[]{:S(2)}) copy-start(bf16[100,512]{1,0:T(8,128)(2,1)S(1)} %collective-permute-done.10) | copy-start | bytes 307204
  64.9 0.6 copy-start.4
  64.9 0.7 copy-start.5
  65.6 79.8 %all-to-all-start.2 = ((bf16[32,402,128]{2,1,0:T(8,128)(2,1)}), bf16[32,402,128]{2,1,0:T(8,128)(2,1)S(1)}, u32[]{:S(2)}, u32[]{:S(2)}) async-start(bf16[32,402,128]{2,1,0:T(8,128)(2,1)} %order_slots.1), calls=%async_computation.2 | async-start | bytes 6684672 | tf_op jit(solution)/shard_map/all_to_all | solution.py:590
  74.3 1.8 %collective-permute-start.16 = (bf16[4,400,128]{2,1,0:T(8,128)(2,1)S(1)}, bf16[4,400,128]{2,1,0:T(8,128)(2,1)S(1)}, u32[]{:S(2)}, u32[]{:S(2)}) collective-permute-start(bf16[4,400,128]{2,1,0:T(8,128)(2,1)S(1)} %slice_bitcast_fusion), channel_id=1, source_target_pairs={{0,1},{1,0},{2,3},{3,2},{4,5},{5,4},{6,7},{7,6},{8,9},{9,8},{10,11... | collective-permute-start | bytes 1228808 | tf_op jit(solution)/shard_map/ppermute | solution.py:535
  79.1 52.5 %collective-permute-start.13 = (bf16[1,4,100,512]{3,2,1,0:T(8,128)(2,1)}, bf16[1,4,100,512]{3,2,1,0:T(8,128)(2,1)}, u32[]{:S(2)}, u32[]{:S(2)}) collective-permute-start(bf16[1,4,100,512]{3,2,1,0:T(8,128)(2,1)} %maximum_bitcast_fusion), channel_id=1, source_target_pairs={{0,2},{1,3},{2,0},{3,1},{4,6},{5,7},{6,4},{7,5},{8,10},{9,11},{10,... | collective-permute-start | bytes 1228808 | tf_op jit(solution)/shard_map/ppermute | solution.py:525
  80.7 50.9 %collective-permute-start.14 = (bf16[1,4,100,512]{3,2,1,0:T(8,128)(2,1)}, bf16[1,4,100,512]{3,2,1,0:T(8,128)(2,1)}, u32[]{:S(2)}, u32[]{:S(2)}) collective-permute-start(bf16[1,4,100,512]{3,2,1,0:T(8,128)(2,1)} %maximum_bitcast_fusion), channel_id=1, source_target_pairs={{0,4},{1,5},{2,6},{3,7},{4,0},{5,1},{6,2},{7,3},{8,12},{9,13},{10,... | collective-permute-start | bytes 1228808 | tf_op jit(solution)/shard_map/ppermute | solution.py:525
  82.2 49.4 %collective-permute-start.15 = (bf16[1,4,100,512]{3,2,1,0:T(8,128)(2,1)}, bf16[1,4,100,512]{3,2,1,0:T(8,128)(2,1)}, u32[]{:S(2)}, u32[]{:S(2)}) collective-permute-start(bf16[1,4,100,512]{3,2,1,0:T(8,128)(2,1)} %maximum_bitcast_fusion), channel_id=1, source_target_pairs={{0,6},{1,7},{2,4},{3,5},{4,2},{5,3},{6,0},{7,1},{8,14},{9,15},{10,... | collective-permute-start | bytes 1228808 | tf_op jit(solution)/shard_map/ppermute | solution.py:525
  83.3 42.3 %collective-permute-start.17 = (bf16[1,400,128]{2,1,0:T(8,128)(2,1)S(1)}, bf16[1,400,128]{2,1,0:T(8,128)(2,1)}, u32[]{:S(2)}, u32[]{:S(2)}) collective-permute-start(bf16[1,400,128]{2,1,0:T(8,128)(2,1)S(1)} %get-tuple-element.129), channel_id=1, source_target_pairs={{0,2},{1,3},{2,0},{3,1},{4,6},{5,7},{6,4},{7,5},{8,10},{9,11},{10,... | collective-permute-start | bytes 307208 | tf_op jit(solution)/shard_map/ppermute | solution.py:525
  84.9 43.8 %collective-permute-start.18 = (bf16[1,400,128]{2,1,0:T(8,128)(2,1)S(1)}, bf16[1,400,128]{2,1,0:T(8,128)(2,1)}, u32[]{:S(2)}, u32[]{:S(2)}) collective-permute-start(bf16[1,400,128]{2,1,0:T(8,128)(2,1)S(1)} %get-tuple-element.128), channel_id=1, source_target_pairs={{0,4},{1,5},{2,6},{3,7},{4,0},{5,1},{6,2},{7,3},{8,12},{9,13},{10,... | collective-permute-start | bytes 307208 | tf_op jit(solution)/shard_map/ppermute | solution.py:525
  125.5 6.0 %collective-permute-start.19 = (bf16[1,400,128]{2,1,0:T(8,128)(2,1)S(1)}, bf16[1,400,128]{2,1,0:T(8,128)(2,1)}, u32[]{:S(2)}, u32[]{:S(2)}) collective-permute-start(bf16[1,400,128]{2,1,0:T(8,128)(2,1)S(1)} %get-tuple-element.127), channel_id=1, source_target_pairs={{0,6},{1,7},{2,4},{3,5},{4,2},{5,3},{6,0},{7,1},{8,14},{9,15},{10,... | collective-permute-start | bytes 307208 | tf_op jit(solution)/shard_map/ppermute | solution.py:525
  131.6 2.2 %collective-permute-start.20 = (bf16[1,4,100,512]{3,2,1,0:T(8,128)(2,1)}, bf16[1,4,100,512]{3,2,1,0:T(8,128)(2,1)}, u32[]{:S(2)}, u32[]{:S(2)}) collective-permute-start(bf16[1,4,100,512]{3,2,1,0:T(8,128)(2,1)} %maximum_bitcast_fusion), channel_id=1, source_target_pairs={{0,1},{1,0},{2,3},{3,2},{4,5},{5,4},{6,7},{7,6},{8,9},{9,8},{10,11... | collective-permute-start | bytes 1228808 | tf_op jit(solution)/shard_map/ppermute | solution.py:525
  131.7 2.7 %collective-permute-start.21 = (bf16[1,4,100,512]{3,2,1,0:T(8,128)(2,1)}, bf16[1,4,100,512]{3,2,1,0:T(8,128)(2,1)}, u32[]{:S(2)}, u32[]{:S(2)}) collective-permute-start(bf16[1,4,100,512]{3,2,1,0:T(8,128)(2,1)} %collective-permute-done.13), channel_id=1, source_target_pairs={{0,1},{1,0},{2,3},{3,2},{4,5},{5,4},{6,7},{7,6},{8,9},{9,8},{10,11... | collective-permute-start | bytes 1228808 | tf_op jit(solution)/shard_map/ppermute | solution.py:525
  132.2 2.8 %collective-permute-start.22 = (bf16[1,4,100,512]{3,2,1,0:T(8,128)(2,1)}, bf16[1,4,100,512]{3,2,1,0:T(8,128)(2,1)}, u32[]{:S(2)}, u32[]{:S(2)}) collective-permute-start(bf16[1,4,100,512]{3,2,1,0:T(8,128)(2,1)} %collective-permute-done.14), channel_id=1, source_target_pairs={{0,1},{1,0},{2,3},{3,2},{4,5},{5,4},{6,7},{7,6},{8,9},{9,8},{10,11... | collective-permute-start | bytes 1228808 | tf_op jit(solution)/shard_map/ppermute | solution.py:525
  132.2 3.3 %collective-permute-start.23 = (bf16[1,4,100,512]{3,2,1,0:T(8,128)(2,1)}, bf16[1,4,100,512]{3,2,1,0:T(8,128)(2,1)}, u32[]{:S(2)}, u32[]{:S(2)}) collective-permute-start(bf16[1,4,100,512]{3,2,1,0:T(8,128)(2,1)} %collective-permute-done.15), channel_id=1, source_target_pairs={{0,1},{1,0},{2,3},{3,2},{4,5},{5,4},{6,7},{7,6},{8,9},{9,8},{10,11... | collective-permute-start | bytes 1228808 | tf_op jit(solution)/shard_map/ppermute | solution.py:525
  135.6 9.8 %copy-start = (s32[1,128]{1,0:T(1,128)S(1)}, s32[1,128]{1,0:T(1,128)}, u32[]{:S(2)}) copy-start(s32[1,128]{1,0:T(1,128)} %neg_ref.1) | copy-start | bytes 1540

commit v6 on v5

--- a/solution.py
+++ b/solution.py
@@ -216,20 +216,22 @@
     cols = base.shape[1]
     lanes = devices * slots
 
-    def halves(block):
-        spare = jnp.zeros((PAD - block.shape[0], block.shape[1]), F32)
-        return jnp.concatenate(split(jnp.concatenate([block, spare], axis=0)), axis=0)
-
     high = local // 64
     pair = jnp.concatenate([high, local - high * 64], axis=0)
     pair = jnp.where(local >= 0, pair, 0).astype(F32)
-    both = nt(halves(jnp.concatenate([rows, pair], axis=0)), hits(place, lanes, 0))
+    tall = pl.cdiv(nb + 3, 8) * 8
+    left = jnp.concatenate([rows, pair, jnp.zeros((tall - nb - 2, rows.shape[1]), F32)], axis=0)
+    right = jnp.concatenate([base, jnp.zeros((tall - nb, cols), F32)], axis=0)
+    both = jnp.concatenate([left, right], axis=1)
+    low = both - both.astype(BF16).astype(F32)
     column = lax.broadcasted_iota(I32, (1, cols), 1)
     owner = column // share
     spots = owner * slots + room + column - owner * share
-    both = both + nt(halves(base), hits(spots, lanes, 0))
-    row = lax.broadcasted_iota(I32, (PAD, lanes), 0)
-    return jnp.where(row == nb + 2, over, both[0:PAD] + both[PAD:])
+    spots = jnp.concatenate([place, spots], axis=1)
+    both = nt(jnp.concatenate([both, low], axis=0).astype(BF16), hits(spots, lanes, 0))
+    row = lax.broadcasted_iota(I32, (tall, lanes), 0)
+    both = jnp.where(row == nb + 2, over, both[0:tall] + both[tall:])
+    return jnp.concatenate([both, jnp.zeros((PAD - tall, lanes), F32)], axis=0)
 
 
 def score_kernel(neg_count, plan, share, rel_ref, picked_ref, negs_ref, head_ref, tail_ref,

time: 163 us -> 164 us (level)
  no operation moved by 1% of the time
where the time goes in v6:
time: 164 us; the launch traced here: 163 us
  Pallas kernels  65.4 us (40%)
  waiting for transfers between devices  60.2 us (37%)
  starting transfers between devices  28.5 us (17%)
  other arithmetic  4.67 us (3%)
  local copies, waits for them, and re-layouts  3.26 us (2%)
    ppermute x10, waiting for transfers between devices, from_group(): lax.ppermute(x, 'dev', [(i, i ^ far) for i in range(group)])  43.9 us
    pallas_call x1, Pallas kernels, add_rows(): pl.pallas_call(functools.partial(add_rows_kernel, slots), grid=(ent // wi...  17.4 us
    pallas_call x1, Pallas kernels, pick_coef(): pl.pallas_call(functools.partial(pick_coef_kernel, nrel, fold), grid=(pl....  11.4 us
    pallas_call x1, Pallas kernels, order_slots(): pl.pallas_call(functools.partial(order_kernel, devices, slots), grid=(dev...  11.3 us
    ppermute x10, starting transfers between devices, from_group(): lax.ppermute(x, 'dev', [(i, i ^ far) for i in range(group)])  10.8 us
    pallas_call x1, Pallas kernels, score_step(): pl.pallas_call(functools.partial(score_kernel, neg_count, plan, share), o...  10.5 us
    ppermute x3, waiting for transfers between devices, shift_layers(): lax.ppermute(block, 'grp', [(i, (i + far) % layers) for i in range(layers)])  7.37 us
    pallas_call x1, Pallas kernels, spread(): pl.pallas_call(functools.partial(spread_kernel, span, share), grid_spec=p...  6.48 us
  transfers between devices with their start and end apart: 17, of which 11 were waited for; matrix products, arithmetic and copies ran while one was open for 4% of the time, Pallas kernels for 20%

profile of v6, /device:TPU:0, one launch (start us, length us, event | category | flops | bytes accessed | tf_op | source)
XLA Modules:
  0.0 163.0 jit_solution(1021911248825833196)
XLA Ops:
  0.6 3.6 %pick_negs.1 = bf16[8,400,128]{2,1,0:T(8,128)(2,1)} custom-call(s32[1,128]{1,0:T(1,128)} %neg_ref.1, bf16[400,4096]{1,0:T(8,128)(2,1)} %bitcast.39), custom_call_target="tpu_custom_call" | custom-call | flops 419430400 | bytes 3276800 | tf_op jit(solution)/shard_map/pick_negs/pallas_call | solution.py:84
  4.2 5.2 %all-to-all-start = ((bf16[8,400,128]{2,1,0:T(8,128)(2,1)}), bf16[8,400,128]{2,1,0:T(8,128)(2,1)S(1)}, u32[]{:S(2)}, u32[]{:S(2)}) async-start(bf16[8,400,128]{2,1,0:T(8,128)(2,1)} %pick_negs.1), calls=%async_computation | async-start | bytes 1638400 | tf_op jit(solution)/shard_map/all_to_all | solution.py:579
  9.4 11.4 %pick_coef.1.picked_ref = f32[100,1024]{1,0:T(8,128)} custom-call(s32[1,1024]{1,0:T(1,128)} %bitcast.45, f32[100,14824]{1,0:T(8,128)} %bitcast.47), custom_call_target="tpu_custom_call" | custom-call | flops 6314786816 | bytes 5929600 | tf_op jit(solution)/shard_map/pick_coef/pallas_call | solution.py:158
  20.8 1.5 all-to-all-done.negs_ref
  22.4 0.9 copy-done.1
  23.3 10.5 %score_step.1 = (bf16[32,56,128]{2,1,0:T(8,128)(2,1)}, bf16[402,2048]{1,0:T(8,128)(2,1)}, f32[100,1024]{1,0:T(8,128)}, f32[100,400]{1,0:T(8,128)}, bf16[1024,102...) custom-call(s32[1,1024]{1,0:T(1,128)S(1)} %bitcast.46, f32[100,1024]{1,0:T(8,128)} %pick_coef.1.picked_ref, ...), custom_call_target="tpu_custom_call" | custom-call | flops 1677721600 | bytes 16777216 | tf_op jit(solution)/shard_map/score_step/pallas_call | solution.py:292
  33.7 4.8 %all-to-all-start.1 = ((bf16[32,56,128]{2,1,0:T(8,128)(2,1)}), bf16[32,56,128]{2,1,0:T(8,128)(2,1)S(1)}, u32[]{:S(2)}, u32[]{:S(2)}) async-start(bf16[32,56,128]{2,1,0:T(8,128)(2,1)} %get-tuple-element.78), calls=%async_computation.1 | async-start | bytes 917504 | tf_op jit(solution)/shard_map/all_to_all | solution.py:583
  38.5 11.3 %order_slots.1 = bf16[32,402,128]{2,1,0:T(8,128)(2,1)} custom-call(bf16[402,2048]{1,0:T(8,128)(2,1)} %get-tuple-element.77.grads_ref, s32[2,1024]{1,0:T(2,128)} %bitcast.52), custom_call_target="tpu_custom_call" | custom-call | flops 6744440832 | bytes 4194304 | tf_op jit(solution)/shard_map/order_slots/pallas_call | solution.py:337
  49.8 3.1 %all-to-all-done.1.recv_ref = bf16[32,56,128]{2,1,0:T(8,128)(2,1)S(1)} async-done(((bf16[32,56,128]{2,1,0:T(8,128)(2,1)}), bf16[32,56,128]{2,1,0:T(8,128)(2,1)S(1)}, u32[]{:S(2)}, u32[]{:S(2)}) %all-to-all-start.1) | async-done | bytes 458784 | tf_op jit(solution)/shard_map/all_to_all | solution.py:583
  52.9 0.9 coef_sum.1
  53.7 1.2 collective-permute-start.10
  55.5 2.2 %collective-permute-start.12 = (bf16[100,512]{1,0:T(8,128)(2,1)S(1)}, bf16[100,512]{1,0:T(8,128)(2,1)S(1)}, u32[]{:S(2)}, u32[]{:S(2)}) collective-permute-start(bf16[100,512]{1,0:T(8,128)(2,1)S(1)} %get-tuple-element.83), channel_id=1, source_target_pairs={{0,24},{8,0},{16,8},{24,16},{1,25},{9,1},{17,9},{25,17},{2,26},{10... | collective-permute-start | bytes 307208 | tf_op jit(solution)/shard_map/ppermute | solution.py:542
  57.6 3.9 %collective-permute-done.10 = bf16[100,512]{1,0:T(8,128)(2,1)S(1)} collective-permute-done((bf16[100,512]{1,0:T(8,128)(2,1)S(1)}, bf16[100,512]{1,0:T(8,128)(2,1)S(1)}, u32[]{:S(2)}, u32[]{:S(2)}) %collective-permute-start.10) | collective-permute-done | bytes 102432 | tf_op jit(solution)/shard_map/ppermute | solution.py:542
  61.5 3.5 %collective-permute-done.11 = bf16[100,512]{1,0:T(8,128)(2,1)S(1)} collective-permute-done((bf16[100,512]{1,0:T(8,128)(2,1)S(1)}, bf16[100,512]{1,0:T(8,128)(2,1)S(1)}, u32[]{:S(2)}, u32[]{:S(2)}) %collective-permute-start.11) | collective-permute-done | bytes 102432 | tf_op jit(solution)/shard_map/ppermute | solution.py:542
  65.7 3.8 %all-to-all-start.2 = ((bf16[32,402,128]{2,1,0:T(8,128)(2,1)}), bf16[32,402,128]{2,1,0:T(8,128)(2,1)S(1)}, u32[]{:S(2)}, u32[]{:S(2)}) async-start(bf16[32,402,128]{2,1,0:T(8,128)(2,1)} %order_slots.1), calls=%async_computation.2 | async-start | bytes 6684672 | tf_op jit(solution)/shard_map/all_to_all | solution.py:592
  69.5 3.9 %partial_step.1 = bf16[2,4,400,128]{3,2,1,0:T(8,128)(2,1)} custom-call(s32[1]{0:T(128)} %bitcast.16.me_ref, bf16[1024,1024]{1,0:T(8,128)(2,1)} %get-tuple-element.87.probs_ref, bf16[400,1024]{1,0:T(8,128)(2,1)} %get-tuple-element.88.hrel_ref), custom_call_target="tpu_custom_call" | custom-call | flops 1 | bytes 1 | tf_op jit(solution)/shard_map/partial_step/pallas_call | solution.py:364
  73.4 1.0 slice_bitcast_fusion
  74.6 1.7 %collective-permute-done.16 = bf16[4,400,128]{2,1,0:T(8,128)(2,1)S(1)} collective-permute-done((bf16[4,400,128]{2,1,0:T(8,128)(2,1)S(1)}, bf16[4,400,128]{2,1,0:T(8,128)(2,1)S(1)}, u32[]{:S(2)}, u32[]{:S(2)}) %collective-permute-start.16) | collective-permute-done | bytes 409632 | tf_op jit(solution)/shard_map/ppermute | solution.py:537
  76.2 1.1 fusion.3
  77.4 1.9 %maximum_bitcast_fusion = bf16[1,4,100,512]{3,2,1,0:T(8,128)(2,1)} fusion(bf16[1,100,512]{2,1,0:T(8,128)(2,1)} %bitcast.44, bf16[1,100,512]{2,1,0:T(8,128)(2,1)} %bitcast.43, bf16[1,100,512]{2,1,0:T(8,128)(2,1)} %bitcast.42, bf16[1,100,512]{2,1,0:T(8,128)(2,1)S(1)} %bitcast.35), kind=kLoop, calls=%fused_computation.9 | loop fusion | flops 614400 | bytes 819200 | tf_op jit(solution)/shard_map/broadcast_in_dim | solution.py:523
  79.2 1.6 collective-permute-start.13
  80.8 1.5 collective-permute-start.14
  83.4 1.6 collective-permute-start.17
  85.0 1.5 collective-permute-start.18
  86.4 39.2 %collective-permute-done.17 = bf16[1,400,128]{2,1,0:T(8,128)(2,1)} collective-permute-done((bf16[1,400,128]{2,1,0:T(8,128)(2,1)S(1)}, bf16[1,400,128]{2,1,0:T(8,128)(2,1)}, u32[]{:S(2)}, u32[]{:S(2)}) %collective-permute-start.17) | collective-permute-done | bytes 102432 | tf_op jit(solution)/shard_map/ppermute | solution.py:527
  125.6 3.2 %collective-permute-start.19 = (bf16[1,400,128]{2,1,0:T(8,128)(2,1)S(1)}, bf16[1,400,128]{2,1,0:T(8,128)(2,1)}, u32[]{:S(2)}, u32[]{:S(2)}) collective-permute-start(bf16[1,400,128]{2,1,0:T(8,128)(2,1)S(1)} %get-tuple-element.127), channel_id=1, source_target_pairs={{0,6},{1,7},{2,4},{3,5},{4,2},{5,3},{6,0},{7,1},{8,14},{9,15},{10,... | collective-permute-start | bytes 307208 | tf_op jit(solution)/shard_map/ppermute | solution.py:527
  128.8 2.9 %collective-permute-done.19 = bf16[1,400,128]{2,1,0:T(8,128)(2,1)} collective-permute-done((bf16[1,400,128]{2,1,0:T(8,128)(2,1)S(1)}, bf16[1,400,128]{2,1,0:T(8,128)(2,1)}, u32[]{:S(2)}, u32[]{:S(2)}) %collective-permute-start.19) | collective-permute-done | bytes 102432 | tf_op jit(solution)/shard_map/ppermute | solution.py:527
  132.8 1.1 add_bitcast_fusion.own_ref
  135.7 7.1 %conditional.1 = ((f32[100,14824]{1,0:T(8,128)}, f32[400,100]{1,0:T(8,128)})) conditional(s32[]{:T(128)} %bitcast.21, (s32[1024]{0:T(1024)S(1)}, f32[100,1024]{1,0:T(8,128)}, f32[100,400]{1,0:T(8,128)}) %tuple.41, (s32[]{:T(128)}, s32[1]{0:T(128)}, bf16[1,4,100,512]{3,2,1,0:T(8,128)(2,1)}, bf16[1,4,100,512]{3,2,1,0:T(8,128)(2,1)}, ...), branch_computations={%region_0.2_spmd, %region_2.0_spmd} | conditional | flops 7717472 | bytes 233237408 | solution.py:604
  136.3 6.5 %spread.1 = (f32[100,14824]{1,0:T(8,128)}, f32[400,100]{1,0:T(8,128)}) custom-call(s32[2]{0:T(128)} %pad_add_fusion.place_ref, bf16[1,4,100,512]{3,2,1,0:T(8,128)(2,1)} %get-tuple-element.32.refs_0_, bf16[1,4,100,512]{3,2,1,0:T(8,128)(2,1)} %get-tuple-element.33.refs_1_, bf16[1,4,100,512]{3,2,1,0:T(8,128)(2,1)} %get-tuple-element.34.refs_2_, ...), custom_call_target="tpu_custom_call" | custom-call | flops 1 | bytes 1 | tf_op jit(solution)/shard_map/cond/branch_1_fun/spread/pallas_call | solution.py:445
  142.8 2.7 %all-to-all-done.2.recv_ref = bf16[32,402,128]{2,1,0:T(8,128)(2,1)S(1)} async-done(((bf16[32,402,128]{2,1,0:T(8,128)(2,1)}), bf16[32,402,128]{2,1,0:T(8,128)(2,1)S(1)}, u32[]{:S(2)}, u32[]{:S(2)}) %all-to-all-start.2) | async-done | bytes 3293216 | tf_op jit(solution)/shard_map/all_to_all | solution.py:592
  145.4 17.4 %add_rows.1 = f32[400,4096]{1,0:T(8,128)} custom-call(bf16[32,402,128]{2,1,0:T(8,128)(2,1)S(1)} %all-to-all-done.2.recv_ref, s32[1,128]{1,0:T(1,128)S(1)} %copy-done, f32[400,128]{1,0:T(8,128)S(1)} %add_bitcast_fusion.own_ref), custom_call_target="tpu_custom_call" | custom-call | flops 1 | bytes 1 | tf_op jit(solution)/shard_map/add_rows/pallas_call | solution.py:507
  (29 shorter events, 5.9 us)
Async XLA Ops:
  4.2 18.1 %all-to-all-start = ((bf16[8,400,128]{2,1,0:T(8,128)(2,1)}), bf16[8,400,128]{2,1,0:T(8,128)(2,1)S(1)}, u32[]{:S(2)}, u32[]{:S(2)}) async-start(bf16[8,400,128]{2,1,0:T(8,128)(2,1)} %pick_negs.1), calls=%async_computation | async-start | bytes 1638400 | tf_op jit(solution)/shard_map/all_to_all | solution.py:579
  9.4 13.8 %copy-start.6 = (s32[1024]{0:T(1024)S(1)}, s32[1024]{0:T(1024)}, u32[]{:S(2)}) copy-start(s32[1024]{0:T(1024)} %param.13) | copy-start | bytes 12292
  22.4 0.9 copy-start.1
  33.7 19.1 %all-to-all-start.1 = ((bf16[32,56,128]{2,1,0:T(8,128)(2,1)}), bf16[32,56,128]{2,1,0:T(8,128)(2,1)S(1)}, u32[]{:S(2)}, u32[]{:S(2)}) async-start(bf16[32,56,128]{2,1,0:T(8,128)(2,1)} %get-tuple-element.78), calls=%async_computation.1 | async-start | bytes 917504 | tf_op jit(solution)/shard_map/all_to_all | solution.py:583
  53.7 7.8 %collective-permute-start.10 = (bf16[100,512]{1,0:T(8,128)(2,1)S(1)}, bf16[100,512]{1,0:T(8,128)(2,1)S(1)}, u32[]{:S(2)}, u32[]{:S(2)}) collective-permute-start(bf16[100,512]{1,0:T(8,128)(2,1)S(1)} %get-tuple-element.83), channel_id=1, source_target_pairs={{0,8},{8,16},{16,24},{24,0},{1,9},{9,17},{17,25},{25,1},{2,10},{10... | collective-permute-start | bytes 307208 | tf_op jit(solution)/shard_map/ppermute | solution.py:542
  55.0 10.0 %collective-permute-start.11 = (bf16[100,512]{1,0:T(8,128)(2,1)S(1)}, bf16[100,512]{1,0:T(8,128)(2,1)S(1)}, u32[]{:S(2)}, u32[]{:S(2)}) collective-permute-start(bf16[100,512]{1,0:T(8,128)(2,1)S(1)} %get-tuple-element.83), channel_id=1, source_target_pairs={{0,16},{8,24},{16,0},{24,8},{1,17},{9,25},{17,1},{25,9},{2,18},{10... | collective-permute-start | bytes 307208 | tf_op jit(solution)/shard_map/ppermute | solution.py:542
  55.5 9.5 %collective-permute-start.12 = (bf16[100,512]{1,0:T(8,128)(2,1)S(1)}, bf16[100,512]{1,0:T(8,128)(2,1)S(1)}, u32[]{:S(2)}, u32[]{:S(2)}) collective-permute-start(bf16[100,512]{1,0:T(8,128)(2,1)S(1)} %get-tuple-element.83), channel_id=1, source_target_pairs={{0,24},{8,0},{16,8},{24,16},{1,25},{9,1},{17,9},{25,17},{2,26},{10... | collective-permute-start | bytes 307208 | tf_op jit(solution)/shard_map/ppermute | solution.py:542
  61.5 3.5 %copy-start.3 = (bf16[100,512]{1,0:T(8,128)(2,1)}, bf16[100,512]{1,0:T(8,128)(2,1)S(1)}, u32[]{:S(2)}) copy-start(bf16[100,512]{1,0:T(8,128)(2,1)S(1)} %collective-permute-done.10) | copy-start | bytes 307204
  65.0 0.6 copy-start.4
  65.0 0.7 copy-start.5
  65.7 79.8 %all-to-all-start.2 = ((bf16[32,402,128]{2,1,0:T(8,128)(2,1)}), bf16[32,402,128]{2,1,0:T(8,128)(2,1)S(1)}, u32[]{:S(2)}, u32[]{:S(2)}) async-start(bf16[32,402,128]{2,1,0:T(8,128)(2,1)} %order_slots.1), calls=%async_computation.2 | async-start | bytes 6684672 | tf_op jit(solution)/shard_map/all_to_all | solution.py:592
  74.4 1.8 %collective-permute-start.16 = (bf16[4,400,128]{2,1,0:T(8,128)(2,1)S(1)}, bf16[4,400,128]{2,1,0:T(8,128)(2,1)S(1)}, u32[]{:S(2)}, u32[]{:S(2)}) collective-permute-start(bf16[4,400,128]{2,1,0:T(8,128)(2,1)S(1)} %slice_bitcast_fusion), channel_id=1, source_target_pairs={{0,1},{1,0},{2,3},{3,2},{4,5},{5,4},{6,7},{7,6},{8,9},{9,8},{10,11... | collective-permute-start | bytes 1228808 | tf_op jit(solution)/shard_map/ppermute | solution.py:537
  79.2 52.5 %collective-permute-start.13 = (bf16[1,4,100,512]{3,2,1,0:T(8,128)(2,1)}, bf16[1,4,100,512]{3,2,1,0:T(8,128)(2,1)}, u32[]{:S(2)}, u32[]{:S(2)}) collective-permute-start(bf16[1,4,100,512]{3,2,1,0:T(8,128)(2,1)} %maximum_bitcast_fusion), channel_id=1, source_target_pairs={{0,2},{1,3},{2,0},{3,1},{4,6},{5,7},{6,4},{7,5},{8,10},{9,11},{10,... | collective-permute-start | bytes 1228808 | tf_op jit(solution)/shard_map/ppermute | solution.py:527
  80.8 50.9 %collective-permute-start.14 = (bf16[1,4,100,512]{3,2,1,0:T(8,128)(2,1)}, bf16[1,4,100,512]{3,2,1,0:T(8,128)(2,1)}, u32[]{:S(2)}, u32[]{:S(2)}) collective-permute-start(bf16[1,4,100,512]{3,2,1,0:T(8,128)(2,1)} %maximum_bitcast_fusion), channel_id=1, source_target_pairs={{0,4},{1,5},{2,6},{3,7},{4,0},{5,1},{6,2},{7,3},{8,12},{9,13},{10,... | collective-permute-start | bytes 1228808 | tf_op jit(solution)/shard_map/ppermute | solution.py:527
  82.3 49.4 %collective-permute-start.15 = (bf16[1,4,100,512]{3,2,1,0:T(8,128)(2,1)}, bf16[1,4,100,512]{3,2,1,0:T(8,128)(2,1)}, u32[]{:S(2)}, u32[]{:S(2)}) collective-permute-start(bf16[1,4,100,512]{3,2,1,0:T(8,128)(2,1)} %maximum_bitcast_fusion), channel_id=1, source_target_pairs={{0,6},{1,7},{2,4},{3,5},{4,2},{5,3},{6,0},{7,1},{8,14},{9,15},{10,... | collective-permute-start | bytes 1228808 | tf_op jit(solution)/shard_map/ppermute | solution.py:527
  83.4 42.3 %collective-permute-start.17 = (bf16[1,400,128]{2,1,0:T(8,128)(2,1)S(1)}, bf16[1,400,128]{2,1,0:T(8,128)(2,1)}, u32[]{:S(2)}, u32[]{:S(2)}) collective-permute-start(bf16[1,400,128]{2,1,0:T(8,128)(2,1)S(1)} %get-tuple-element.129), channel_id=1, source_target_pairs={{0,2},{1,3},{2,0},{3,1},{4,6},{5,7},{6,4},{7,5},{8,10},{9,11},{10,... | collective-permute-start | bytes 307208 | tf_op jit(solution)/shard_map/ppermute | solution.py:527
  85.0 43.8 %collective-permute-start.18 = (bf16[1,400,128]{2,1,0:T(8,128)(2,1)S(1)}, bf16[1,400,128]{2,1,0:T(8,128)(2,1)}, u32[]{:S(2)}, u32[]{:S(2)}) collective-permute-start(bf16[1,400,128]{2,1,0:T(8,128)(2,1)S(1)} %get-tuple-element.128), channel_id=1, source_target_pairs={{0,4},{1,5},{2,6},{3,7},{4,0},{5,1},{6,2},{7,3},{8,12},{9,13},{10,... | collective-permute-start | bytes 307208 | tf_op jit(solution)/shard_map/ppermute | solution.py:527
  125.6 6.0 %collective-permute-start.19 = (bf16[1,400,128]{2,1,0:T(8,128)(2,1)S(1)}, bf16[1,400,128]{2,1,0:T(8,128)(2,1)}, u32[]{:S(2)}, u32[]{:S(2)}) collective-permute-start(bf16[1,400,128]{2,1,0:T(8,128)(2,1)S(1)} %get-tuple-element.127), channel_id=1, source_target_pairs={{0,6},{1,7},{2,4},{3,5},{4,2},{5,3},{6,0},{7,1},{8,14},{9,15},{10,... | collective-permute-start | bytes 307208 | tf_op jit(solution)/shard_map/ppermute | solution.py:527
  131.7 2.2 %collective-permute-start.20 = (bf16[1,4,100,512]{3,2,1,0:T(8,128)(2,1)}, bf16[1,4,100,512]{3,2,1,0:T(8,128)(2,1)}, u32[]{:S(2)}, u32[]{:S(2)}) collective-permute-start(bf16[1,4,100,512]{3,2,1,0:T(8,128)(2,1)} %maximum_bitcast_fusion), channel_id=1, source_target_pairs={{0,1},{1,0},{2,3},{3,2},{4,5},{5,4},{6,7},{7,6},{8,9},{9,8},{10,11... | collective-permute-start | bytes 1228808 | tf_op jit(solution)/shard_map/ppermute | solution.py:527
  131.8 2.7 %collective-permute-start.21 = (bf16[1,4,100,512]{3,2,1,0:T(8,128)(2,1)}, bf16[1,4,100,512]{3,2,1,0:T(8,128)(2,1)}, u32[]{:S(2)}, u32[]{:S(2)}) collective-permute-start(bf16[1,4,100,512]{3,2,1,0:T(8,128)(2,1)} %collective-permute-done.13), channel_id=1, source_target_pairs={{0,1},{1,0},{2,3},{3,2},{4,5},{5,4},{6,7},{7,6},{8,9},{9,8},{10,11... | collective-permute-start | bytes 1228808 | tf_op jit(solution)/shard_map/ppermute | solution.py:527
  132.2 2.8 %collective-permute-start.22 = (bf16[1,4,100,512]{3,2,1,0:T(8,128)(2,1)}, bf16[1,4,100,512]{3,2,1,0:T(8,128)(2,1)}, u32[]{:S(2)}, u32[]{:S(2)}) collective-permute-start(bf16[1,4,100,512]{3,2,1,0:T(8,128)(2,1)} %collective-permute-done.14), channel_id=1, source_target_pairs={{0,1},{1,0},{2,3},{3,2},{4,5},{5,4},{6,7},{7,6},{8,9},{9,8},{10,11... | collective-permute-start | bytes 1228808 | tf_op jit(solution)/shard_map/ppermute | solution.py:527
  132.3 3.3 %collective-permute-start.23 = (bf16[1,4,100,512]{3,2,1,0:T(8,128)(2,1)}, bf16[1,4,100,512]{3,2,1,0:T(8,128)(2,1)}, u32[]{:S(2)}, u32[]{:S(2)}) collective-permute-start(bf16[1,4,100,512]{3,2,1,0:T(8,128)(2,1)} %collective-permute-done.15), channel_id=1, source_target_pairs={{0,1},{1,0},{2,3},{3,2},{4,5},{5,4},{6,7},{7,6},{8,9},{9,8},{10,11... | collective-permute-start | bytes 1228808 | tf_op jit(solution)/shard_map/ppermute | solution.py:527
  135.7 9.8 %copy-start = (s32[1,128]{1,0:T(1,128)S(1)}, s32[1,128]{1,0:T(1,128)}, u32[]{:S(2)}) copy-start(s32[1,128]{1,0:T(1,128)} %neg_ref.1) | copy-start | bytes 1540

commit v7 on v5

--- a/solution.py
+++ b/solution.py
@@ -152,7 +152,7 @@
 def pick_coef(rel, coef_t):
     nb, nrel = coef_t.shape
     triples = rel.shape[1]
-    fold = 2
+    fold = 4
     width = fold * 1920
     tall = 2 * (pl.cdiv(nb, 8) * 8)
     return pl.pallas_call(

time: 163 us -> 163 us (level)
  no operation moved by 1% of the time
where the time goes in v7:
time: 163 us; the launch traced here: 162 us
  Pallas kernels  64.8 us (40%)
  waiting for transfers between devices  60.5 us (37%)
  starting transfers between devices  28.1 us (17%)
  other arithmetic  4.67 us (3%)
  local copies, waits for them, and re-layouts  3.26 us (2%)
    ppermute x10, waiting for transfers between devices, from_group(): lax.ppermute(x, 'dev', [(i, i ^ far) for i in range(group)])  43.9 us
    pallas_call x1, Pallas kernels, add_rows(): pl.pallas_call(functools.partial(add_rows_kernel, slots), grid=(ent // wi...  17.4 us
    pallas_call x1, Pallas kernels, order_slots(): pl.pallas_call(functools.partial(order_kernel, devices, slots), grid=(dev...  11.3 us
    pallas_call x1, Pallas kernels, pick_coef(): pl.pallas_call(functools.partial(pick_coef_kernel, nrel, fold), grid=(pl....  10.9 us
    ppermute x10, starting transfers between devices, from_group(): lax.ppermute(x, 'dev', [(i, i ^ far) for i in range(group)])  10.9 us
    pallas_call x1, Pallas kernels, score_step(): pl.pallas_call(functools.partial(score_kernel, neg_count, plan, share), o...  10.3 us
    ppermute x3, waiting for transfers between devices, shift_layers(): lax.ppermute(block, 'grp', [(i, (i + far) % layers) for i in range(layers)])  7.37 us
    pallas_call x1, Pallas kernels, spread(): pl.pallas_call(functools.partial(spread_kernel, span, share), grid_spec=p...  6.48 us
  transfers between devices with their start and end apart: 17, of which 11 were waited for; matrix products, arithmetic and copies ran while one was open for 4% of the time, Pallas kernels for 20%

profile of v7, /device:TPU:0, one launch (start us, length us, event | category | flops | bytes accessed | tf_op | source)
XLA Modules:
  0.0 162.3 jit_solution(2021785120833890670)
XLA Ops:
  0.6 3.6 %pick_negs.1 = bf16[8,400,128]{2,1,0:T(8,128)(2,1)} custom-call(s32[1,128]{1,0:T(1,128)} %neg_ref.1, bf16[400,4096]{1,0:T(8,128)(2,1)} %bitcast.39), custom_call_target="tpu_custom_call" | custom-call | flops 419430400 | bytes 3276800 | tf_op jit(solution)/shard_map/pick_negs/pallas_call | solution.py:84
  4.2 5.2 %all-to-all-start = ((bf16[8,400,128]{2,1,0:T(8,128)(2,1)}), bf16[8,400,128]{2,1,0:T(8,128)(2,1)S(1)}, u32[]{:S(2)}, u32[]{:S(2)}) async-start(bf16[8,400,128]{2,1,0:T(8,128)(2,1)} %pick_negs.1), calls=%async_computation | async-start | bytes 1638400 | tf_op jit(solution)/shard_map/all_to_all | solution.py:577
  9.4 10.9 %pick_coef.1.picked_ref = f32[100,1024]{1,0:T(8,128)} custom-call(s32[1,1024]{1,0:T(1,128)} %bitcast.45, f32[100,14824]{1,0:T(8,128)} %bitcast.47), custom_call_target="tpu_custom_call" | custom-call | flops 6314786816 | bytes 5929600 | tf_op jit(solution)/shard_map/pick_coef/pallas_call | solution.py:158
  20.4 2.0 %all-to-all-done.negs_ref = bf16[8,400,128]{2,1,0:T(8,128)(2,1)S(1)} async-done(((bf16[8,400,128]{2,1,0:T(8,128)(2,1)}), bf16[8,400,128]{2,1,0:T(8,128)(2,1)S(1)}, u32[]{:S(2)}, u32[]{:S(2)}) %all-to-all-start) | async-done | bytes 819232 | tf_op jit(solution)/shard_map/all_to_all | solution.py:577
  22.4 0.9 copy-done.1
  23.3 10.3 %score_step.1 = (bf16[32,56,128]{2,1,0:T(8,128)(2,1)}, bf16[402,2048]{1,0:T(8,128)(2,1)}, f32[100,1024]{1,0:T(8,128)}, f32[100,400]{1,0:T(8,128)}, bf16[1024,102...) custom-call(s32[1,1024]{1,0:T(1,128)S(1)} %bitcast.46, f32[100,1024]{1,0:T(8,128)} %pick_coef.1.picked_ref, ...), custom_call_target="tpu_custom_call" | custom-call | flops 1677721600 | bytes 16777216 | tf_op jit(solution)/shard_map/score_step/pallas_call | solution.py:290
  33.6 4.3 %all-to-all-start.1 = ((bf16[32,56,128]{2,1,0:T(8,128)(2,1)}), bf16[32,56,128]{2,1,0:T(8,128)(2,1)S(1)}, u32[]{:S(2)}, u32[]{:S(2)}) async-start(bf16[32,56,128]{2,1,0:T(8,128)(2,1)} %get-tuple-element.78), calls=%async_computation.1 | async-start | bytes 917504 | tf_op jit(solution)/shard_map/all_to_all | solution.py:581
  37.9 11.3 %order_slots.1 = bf16[32,402,128]{2,1,0:T(8,128)(2,1)} custom-call(bf16[402,2048]{1,0:T(8,128)(2,1)} %get-tuple-element.77.grads_ref, s32[2,1024]{1,0:T(2,128)} %bitcast.52), custom_call_target="tpu_custom_call" | custom-call | flops 6744440832 | bytes 4194304 | tf_op jit(solution)/shard_map/order_slots/pallas_call | solution.py:335
  49.2 3.1 %all-to-all-done.1.recv_ref = bf16[32,56,128]{2,1,0:T(8,128)(2,1)S(1)} async-done(((bf16[32,56,128]{2,1,0:T(8,128)(2,1)}), bf16[32,56,128]{2,1,0:T(8,128)(2,1)S(1)}, u32[]{:S(2)}, u32[]{:S(2)}) %all-to-all-start.1) | async-done | bytes 458784 | tf_op jit(solution)/shard_map/all_to_all | solution.py:581
  52.3 0.9 coef_sum.1
  53.2 1.2 collective-permute-start.10
  54.9 2.2 %collective-permute-start.12 = (bf16[100,512]{1,0:T(8,128)(2,1)S(1)}, bf16[100,512]{1,0:T(8,128)(2,1)S(1)}, u32[]{:S(2)}, u32[]{:S(2)}) collective-permute-start(bf16[100,512]{1,0:T(8,128)(2,1)S(1)} %get-tuple-element.83), channel_id=1, source_target_pairs={{0,24},{8,0},{16,8},{24,16},{1,25},{9,1},{17,9},{25,17},{2,26},{10... | collective-permute-start | bytes 307208 | tf_op jit(solution)/shard_map/ppermute | solution.py:540
  57.0 3.9 %collective-permute-done.10 = bf16[100,512]{1,0:T(8,128)(2,1)S(1)} collective-permute-done((bf16[100,512]{1,0:T(8,128)(2,1)S(1)}, bf16[100,512]{1,0:T(8,128)(2,1)S(1)}, u32[]{:S(2)}, u32[]{:S(2)}) %collective-permute-start.10) | collective-permute-done | bytes 102432 | tf_op jit(solution)/shard_map/ppermute | solution.py:540
  60.9 3.5 %collective-permute-done.11 = bf16[100,512]{1,0:T(8,128)(2,1)S(1)} collective-permute-done((bf16[100,512]{1,0:T(8,128)(2,1)S(1)}, bf16[100,512]{1,0:T(8,128)(2,1)S(1)}, u32[]{:S(2)}, u32[]{:S(2)}) %collective-permute-start.11) | collective-permute-done | bytes 102432 | tf_op jit(solution)/shard_map/ppermute | solution.py:540
  65.1 3.6 %all-to-all-start.2 = ((bf16[32,402,128]{2,1,0:T(8,128)(2,1)}), bf16[32,402,128]{2,1,0:T(8,128)(2,1)S(1)}, u32[]{:S(2)}, u32[]{:S(2)}) async-start(bf16[32,402,128]{2,1,0:T(8,128)(2,1)} %order_slots.1), calls=%async_computation.2 | async-start | bytes 6684672 | tf_op jit(solution)/shard_map/all_to_all | solution.py:590
  68.7 3.9 %partial_step.1 = bf16[2,4,400,128]{3,2,1,0:T(8,128)(2,1)} custom-call(s32[1]{0:T(128)} %bitcast.16.me_ref, bf16[1024,1024]{1,0:T(8,128)(2,1)} %get-tuple-element.87.probs_ref, bf16[400,1024]{1,0:T(8,128)(2,1)} %get-tuple-element.88.hrel_ref), custom_call_target="tpu_custom_call" | custom-call | flops 1 | bytes 1 | tf_op jit(solution)/shard_map/partial_step/pallas_call | solution.py:362
  72.6 1.0 slice_bitcast_fusion
  74.0 1.5 collective-permute-done.16
  75.5 1.1 fusion.3
  76.6 1.9 %maximum_bitcast_fusion = bf16[1,4,100,512]{3,2,1,0:T(8,128)(2,1)} fusion(bf16[1,100,512]{2,1,0:T(8,128)(2,1)} %bitcast.44, bf16[1,100,512]{2,1,0:T(8,128)(2,1)} %bitcast.43, bf16[1,100,512]{2,1,0:T(8,128)(2,1)} %bitcast.42, bf16[1,100,512]{2,1,0:T(8,128)(2,1)S(1)} %bitcast.35), kind=kLoop, calls=%fused_computation.9 | loop fusion | flops 614400 | bytes 819200 | tf_op jit(solution)/shard_map/broadcast_in_dim | solution.py:521
  78.4 1.8 %collective-permute-start.13 = (bf16[1,4,100,512]{3,2,1,0:T(8,128)(2,1)}, bf16[1,4,100,512]{3,2,1,0:T(8,128)(2,1)}, u32[]{:S(2)}, u32[]{:S(2)}) collective-permute-start(bf16[1,4,100,512]{3,2,1,0:T(8,128)(2,1)} %maximum_bitcast_fusion), channel_id=1, source_target_pairs={{0,2},{1,3},{2,0},{3,1},{4,6},{5,7},{6,4},{7,5},{8,10},{9,11},{10,... | collective-permute-start | bytes 1228808 | tf_op jit(solution)/shard_map/ppermute | solution.py:525
  80.2 1.5 collective-permute-start.14
  82.6 1.8 %collective-permute-start.17 = (bf16[1,400,128]{2,1,0:T(8,128)(2,1)S(1)}, bf16[1,400,128]{2,1,0:T(8,128)(2,1)}, u32[]{:S(2)}, u32[]{:S(2)}) collective-permute-start(bf16[1,400,128]{2,1,0:T(8,128)(2,1)S(1)} %get-tuple-element.129), channel_id=1, source_target_pairs={{0,2},{1,3},{2,0},{3,1},{4,6},{5,7},{6,4},{7,5},{8,10},{9,11},{10,... | collective-permute-start | bytes 307208 | tf_op jit(solution)/shard_map/ppermute | solution.py:525
  84.4 1.5 collective-permute-start.18
  85.8 39.3 %collective-permute-done.17 = bf16[1,400,128]{2,1,0:T(8,128)(2,1)} collective-permute-done((bf16[1,400,128]{2,1,0:T(8,128)(2,1)S(1)}, bf16[1,400,128]{2,1,0:T(8,128)(2,1)}, u32[]{:S(2)}, u32[]{:S(2)}) %collective-permute-start.17) | collective-permute-done | bytes 102432 | tf_op jit(solution)/shard_map/ppermute | solution.py:525
  125.1 3.1 %collective-permute-start.19 = (bf16[1,400,128]{2,1,0:T(8,128)(2,1)S(1)}, bf16[1,400,128]{2,1,0:T(8,128)(2,1)}, u32[]{:S(2)}, u32[]{:S(2)}) collective-permute-start(bf16[1,400,128]{2,1,0:T(8,128)(2,1)S(1)} %get-tuple-element.127), channel_id=1, source_target_pairs={{0,6},{1,7},{2,4},{3,5},{4,2},{5,3},{6,0},{7,1},{8,14},{9,15},{10,... | collective-permute-start | bytes 307208 | tf_op jit(solution)/shard_map/ppermute | solution.py:525
  128.2 2.9 %collective-permute-done.19 = bf16[1,400,128]{2,1,0:T(8,128)(2,1)} collective-permute-done((bf16[1,400,128]{2,1,0:T(8,128)(2,1)S(1)}, bf16[1,400,128]{2,1,0:T(8,128)(2,1)}, u32[]{:S(2)}, u32[]{:S(2)}) %collective-permute-start.19) | collective-permute-done | bytes 102432 | tf_op jit(solution)/shard_map/ppermute | solution.py:525
  132.2 1.1 add_bitcast_fusion.own_ref
  135.1 7.1 %conditional.1 = ((f32[100,14824]{1,0:T(8,128)}, f32[400,100]{1,0:T(8,128)})) conditional(s32[]{:T(128)} %bitcast.21, (s32[1024]{0:T(1024)S(1)}, f32[100,1024]{1,0:T(8,128)}, f32[100,400]{1,0:T(8,128)}) %tuple.41, (s32[]{:T(128)}, s32[1]{0:T(128)}, bf16[1,4,100,512]{3,2,1,0:T(8,128)(2,1)}, bf16[1,4,100,512]{3,2,1,0:T(8,128)(2,1)}, ...), branch_computations={%region_0.2_spmd, %region_2.0_spmd} | conditional | flops 7717472 | bytes 233237408 | solution.py:602
  135.7 6.5 %spread.1 = (f32[100,14824]{1,0:T(8,128)}, f32[400,100]{1,0:T(8,128)}) custom-call(s32[2]{0:T(128)} %pad_add_fusion.place_ref, bf16[1,4,100,512]{3,2,1,0:T(8,128)(2,1)} %get-tuple-element.32.refs_0_, bf16[1,4,100,512]{3,2,1,0:T(8,128)(2,1)} %get-tuple-element.33.refs_1_, bf16[1,4,100,512]{3,2,1,0:T(8,128)(2,1)} %get-tuple-element.34.refs_2_, ...), custom_call_target="tpu_custom_call" | custom-call | flops 1 | bytes 1 | tf_op jit(solution)/shard_map/cond/branch_1_fun/spread/pallas_call | solution.py:443
  142.2 2.5 %all-to-all-done.2.recv_ref = bf16[32,402,128]{2,1,0:T(8,128)(2,1)S(1)} async-done(((bf16[32,402,128]{2,1,0:T(8,128)(2,1)}), bf16[32,402,128]{2,1,0:T(8,128)(2,1)S(1)}, u32[]{:S(2)}, u32[]{:S(2)}) %all-to-all-start.2) | async-done | bytes 3293216 | tf_op jit(solution)/shard_map/all_to_all | solution.py:590
  144.7 17.4 %add_rows.1 = f32[400,4096]{1,0:T(8,128)} custom-call(bf16[32,402,128]{2,1,0:T(8,128)(2,1)S(1)} %all-to-all-done.2.recv_ref, s32[1,128]{1,0:T(1,128)S(1)} %copy-done, f32[400,128]{1,0:T(8,128)S(1)} %add_bitcast_fusion.own_ref), custom_call_target="tpu_custom_call" | custom-call | flops 1 | bytes 1 | tf_op jit(solution)/shard_map/add_rows/pallas_call | solution.py:505
  (29 shorter events, 5.9 us)
Async XLA Ops:
  4.2 18.1 %all-to-all-start = ((bf16[8,400,128]{2,1,0:T(8,128)(2,1)}), bf16[8,400,128]{2,1,0:T(8,128)(2,1)S(1)}, u32[]{:S(2)}, u32[]{:S(2)}) async-start(bf16[8,400,128]{2,1,0:T(8,128)(2,1)} %pick_negs.1), calls=%async_computation | async-start | bytes 1638400 | tf_op jit(solution)/shard_map/all_to_all | solution.py:577
  9.4 13.8 %copy-start.6 = (s32[1024]{0:T(1024)S(1)}, s32[1024]{0:T(1024)}, u32[]{:S(2)}) copy-start(s32[1024]{0:T(1024)} %param.13) | copy-start | bytes 12292
  22.4 0.9 copy-start.1
  33.6 18.7 %all-to-all-start.1 = ((bf16[32,56,128]{2,1,0:T(8,128)(2,1)}), bf16[32,56,128]{2,1,0:T(8,128)(2,1)S(1)}, u32[]{:S(2)}, u32[]{:S(2)}) async-start(bf16[32,56,128]{2,1,0:T(8,128)(2,1)} %get-tuple-element.78), calls=%async_computation.1 | async-start | bytes 917504 | tf_op jit(solution)/shard_map/all_to_all | solution.py:581
  53.2 7.8 %collective-permute-start.10 = (bf16[100,512]{1,0:T(8,128)(2,1)S(1)}, bf16[100,512]{1,0:T(8,128)(2,1)S(1)}, u32[]{:S(2)}, u32[]{:S(2)}) collective-permute-start(bf16[100,512]{1,0:T(8,128)(2,1)S(1)} %get-tuple-element.83), channel_id=1, source_target_pairs={{0,8},{8,16},{16,24},{24,0},{1,9},{9,17},{17,25},{25,1},{2,10},{10... | collective-permute-start | bytes 307208 | tf_op jit(solution)/shard_map/ppermute | solution.py:540
  54.4 10.0 %collective-permute-start.11 = (bf16[100,512]{1,0:T(8,128)(2,1)S(1)}, bf16[100,512]{1,0:T(8,128)(2,1)S(1)}, u32[]{:S(2)}, u32[]{:S(2)}) collective-permute-start(bf16[100,512]{1,0:T(8,128)(2,1)S(1)} %get-tuple-element.83), channel_id=1, source_target_pairs={{0,16},{8,24},{16,0},{24,8},{1,17},{9,25},{17,1},{25,9},{2,18},{10... | collective-permute-start | bytes 307208 | tf_op jit(solution)/shard_map/ppermute | solution.py:540
  54.9 9.5 %collective-permute-start.12 = (bf16[100,512]{1,0:T(8,128)(2,1)S(1)}, bf16[100,512]{1,0:T(8,128)(2,1)S(1)}, u32[]{:S(2)}, u32[]{:S(2)}) collective-permute-start(bf16[100,512]{1,0:T(8,128)(2,1)S(1)} %get-tuple-element.83), channel_id=1, source_target_pairs={{0,24},{8,0},{16,8},{24,16},{1,25},{9,1},{17,9},{25,17},{2,26},{10... | collective-permute-start | bytes 307208 | tf_op jit(solution)/shard_map/ppermute | solution.py:540
  60.9 3.5 %copy-start.3 = (bf16[100,512]{1,0:T(8,128)(2,1)}, bf16[100,512]{1,0:T(8,128)(2,1)S(1)}, u32[]{:S(2)}) copy-start(bf16[100,512]{1,0:T(8,128)(2,1)S(1)} %collective-permute-done.10) | copy-start | bytes 307204
  64.4 0.6 copy-start.4
  64.4 0.7 copy-start.5
  65.1 79.6 %all-to-all-start.2 = ((bf16[32,402,128]{2,1,0:T(8,128)(2,1)}), bf16[32,402,128]{2,1,0:T(8,128)(2,1)S(1)}, u32[]{:S(2)}, u32[]{:S(2)}) async-start(bf16[32,402,128]{2,1,0:T(8,128)(2,1)} %order_slots.1), calls=%async_computation.2 | async-start | bytes 6684672 | tf_op jit(solution)/shard_map/all_to_all | solution.py:590
  73.7 1.8 %collective-permute-start.16 = (bf16[4,400,128]{2,1,0:T(8,128)(2,1)S(1)}, bf16[4,400,128]{2,1,0:T(8,128)(2,1)S(1)}, u32[]{:S(2)}, u32[]{:S(2)}) collective-permute-start(bf16[4,400,128]{2,1,0:T(8,128)(2,1)S(1)} %slice_bitcast_fusion), channel_id=1, source_target_pairs={{0,1},{1,0},{2,3},{3,2},{4,5},{5,4},{6,7},{7,6},{8,9},{9,8},{10,11... | collective-permute-start | bytes 1228808 | tf_op jit(solution)/shard_map/ppermute | solution.py:535
  78.4 52.6 %collective-permute-start.13 = (bf16[1,4,100,512]{3,2,1,0:T(8,128)(2,1)}, bf16[1,4,100,512]{3,2,1,0:T(8,128)(2,1)}, u32[]{:S(2)}, u32[]{:S(2)}) collective-permute-start(bf16[1,4,100,512]{3,2,1,0:T(8,128)(2,1)} %maximum_bitcast_fusion), channel_id=1, source_target_pairs={{0,2},{1,3},{2,0},{3,1},{4,6},{5,7},{6,4},{7,5},{8,10},{9,11},{10,... | collective-permute-start | bytes 1228808 | tf_op jit(solution)/shard_map/ppermute | solution.py:525
  80.2 50.9 %collective-permute-start.14 = (bf16[1,4,100,512]{3,2,1,0:T(8,128)(2,1)}, bf16[1,4,100,512]{3,2,1,0:T(8,128)(2,1)}, u32[]{:S(2)}, u32[]{:S(2)}) collective-permute-start(bf16[1,4,100,512]{3,2,1,0:T(8,128)(2,1)} %maximum_bitcast_fusion), channel_id=1, source_target_pairs={{0,4},{1,5},{2,6},{3,7},{4,0},{5,1},{6,2},{7,3},{8,12},{9,13},{10,... | collective-permute-start | bytes 1228808 | tf_op jit(solution)/shard_map/ppermute | solution.py:525
  81.7 49.4 %collective-permute-start.15 = (bf16[1,4,100,512]{3,2,1,0:T(8,128)(2,1)}, bf16[1,4,100,512]{3,2,1,0:T(8,128)(2,1)}, u32[]{:S(2)}, u32[]{:S(2)}) collective-permute-start(bf16[1,4,100,512]{3,2,1,0:T(8,128)(2,1)} %maximum_bitcast_fusion), channel_id=1, source_target_pairs={{0,6},{1,7},{2,4},{3,5},{4,2},{5,3},{6,0},{7,1},{8,14},{9,15},{10,... | collective-permute-start | bytes 1228808 | tf_op jit(solution)/shard_map/ppermute | solution.py:525
  82.6 42.5 %collective-permute-start.17 = (bf16[1,400,128]{2,1,0:T(8,128)(2,1)S(1)}, bf16[1,400,128]{2,1,0:T(8,128)(2,1)}, u32[]{:S(2)}, u32[]{:S(2)}) collective-permute-start(bf16[1,400,128]{2,1,0:T(8,128)(2,1)S(1)} %get-tuple-element.129), channel_id=1, source_target_pairs={{0,2},{1,3},{2,0},{3,1},{4,6},{5,7},{6,4},{7,5},{8,10},{9,11},{10,... | collective-permute-start | bytes 307208 | tf_op jit(solution)/shard_map/ppermute | solution.py:525
  84.4 43.8 %collective-permute-start.18 = (bf16[1,400,128]{2,1,0:T(8,128)(2,1)S(1)}, bf16[1,400,128]{2,1,0:T(8,128)(2,1)}, u32[]{:S(2)}, u32[]{:S(2)}) collective-permute-start(bf16[1,400,128]{2,1,0:T(8,128)(2,1)S(1)} %get-tuple-element.128), channel_id=1, source_target_pairs={{0,4},{1,5},{2,6},{3,7},{4,0},{5,1},{6,2},{7,3},{8,12},{9,13},{10,... | collective-permute-start | bytes 307208 | tf_op jit(solution)/shard_map/ppermute | solution.py:525
  125.1 5.9 %collective-permute-start.19 = (bf16[1,400,128]{2,1,0:T(8,128)(2,1)S(1)}, bf16[1,400,128]{2,1,0:T(8,128)(2,1)}, u32[]{:S(2)}, u32[]{:S(2)}) collective-permute-start(bf16[1,400,128]{2,1,0:T(8,128)(2,1)S(1)} %get-tuple-element.127), channel_id=1, source_target_pairs={{0,6},{1,7},{2,4},{3,5},{4,2},{5,3},{6,0},{7,1},{8,14},{9,15},{10,... | collective-permute-start | bytes 307208 | tf_op jit(solution)/shard_map/ppermute | solution.py:525
  131.1 2.2 %collective-permute-start.20 = (bf16[1,4,100,512]{3,2,1,0:T(8,128)(2,1)}, bf16[1,4,100,512]{3,2,1,0:T(8,128)(2,1)}, u32[]{:S(2)}, u32[]{:S(2)}) collective-permute-start(bf16[1,4,100,512]{3,2,1,0:T(8,128)(2,1)} %maximum_bitcast_fusion), channel_id=1, source_target_pairs={{0,1},{1,0},{2,3},{3,2},{4,5},{5,4},{6,7},{7,6},{8,9},{9,8},{10,11... | collective-permute-start | bytes 1228808 | tf_op jit(solution)/shard_map/ppermute | solution.py:525
  131.2 2.7 %collective-permute-start.21 = (bf16[1,4,100,512]{3,2,1,0:T(8,128)(2,1)}, bf16[1,4,100,512]{3,2,1,0:T(8,128)(2,1)}, u32[]{:S(2)}, u32[]{:S(2)}) collective-permute-start(bf16[1,4,100,512]{3,2,1,0:T(8,128)(2,1)} %collective-permute-done.13), channel_id=1, source_target_pairs={{0,1},{1,0},{2,3},{3,2},{4,5},{5,4},{6,7},{7,6},{8,9},{9,8},{10,11... | collective-permute-start | bytes 1228808 | tf_op jit(solution)/shard_map/ppermute | solution.py:525
  131.7 2.8 %collective-permute-start.22 = (bf16[1,4,100,512]{3,2,1,0:T(8,128)(2,1)}, bf16[1,4,100,512]{3,2,1,0:T(8,128)(2,1)}, u32[]{:S(2)}, u32[]{:S(2)}) collective-permute-start(bf16[1,4,100,512]{3,2,1,0:T(8,128)(2,1)} %collective-permute-done.14), channel_id=1, source_target_pairs={{0,1},{1,0},{2,3},{3,2},{4,5},{5,4},{6,7},{7,6},{8,9},{9,8},{10,11... | collective-permute-start | bytes 1228808 | tf_op jit(solution)/shard_map/ppermute | solution.py:525
  131.7 3.3 %collective-permute-start.23 = (bf16[1,4,100,512]{3,2,1,0:T(8,128)(2,1)}, bf16[1,4,100,512]{3,2,1,0:T(8,128)(2,1)}, u32[]{:S(2)}, u32[]{:S(2)}) collective-permute-start(bf16[1,4,100,512]{3,2,1,0:T(8,128)(2,1)} %collective-permute-done.15), channel_id=1, source_target_pairs={{0,1},{1,0},{2,3},{3,2},{4,5},{5,4},{6,7},{7,6},{8,9},{9,8},{10,11... | collective-permute-start | bytes 1228808 | tf_op jit(solution)/shard_map/ppermute | solution.py:525
  135.1 9.6 %copy-start = (s32[1,128]{1,0:T(1,128)S(1)}, s32[1,128]{1,0:T(1,128)}, u32[]{:S(2)}) copy-start(s32[1,128]{1,0:T(1,128)} %neg_ref.1) | copy-start | bytes 1540
